TPU v7x, 128 devices: a whole 4x4x4 slice. The times are simulated.
128 devices in a mesh: tm: 16 (over y, x), sta: 8 (over z, core).
Axes of the slice: x: 4, y: 4, z: 4, core: 2. Of those that a mesh axis runs over, the one named last changes fastest.
Arguments:
- waveforms: bfloat16 [64, 8192], P('sta', 'tm'), may hold values from -220 to 220
- templates: bfloat16 [2048, 64, 512], P(None, 'sta'), may hold values from -6 to 6
- detection_flags: int32 [2048, 16], P('sta', 'tm'), may hold values from 0 to 1, as said below
- pair_events: int32 [2048, 2], P(('tm', 'sta')), may hold values from 0 to 2559, as said below
- pair_lags: int32 [2048], P(('tm', 'sta')), may hold values from -256 to 128
Outputs:
- network_stack: float32 [2048, 8192], P('sta', 'tm')
- pair_cc: float32 [2048, 128], P(('tm', 'sta'))
Inputs may be any that keep to these rules, and one draw needn't show every extreme that they name: `detection_flags`: among the 256 templates of one station group, in every time block at least one and at most 32 flags are 1, and exactly 32 in some such block. There are exactly 16 * 8 * (32 + max(1, 8)) // 2 flags equal to 1 in all. `pair_events`: every entry is the number of a detection, below the count of flags that are 1; the first and the last detection are named. Among the 32 entries of the pairs of one owner device, at most 1 are detections of one time block and station group, and exactly 1 for some.
All inputs are finite; a program needn't handle non-finite values.
Results may differ from a plain program's by a relative error of at most 0.0003.
Values may be sent and summed in bfloat16 or wider, within the bound.
No kernel may reach another device: no remote copies, remote signals or barrier semaphores. Data moves between devices by JAX's collectives and lax.ppermute only.
A program may use at most 384 MiB of HBM per device.

v0:
```python
import jax
import jax.numpy as jnp
from jax import lax
from jax.experimental import pallas as pl
from jax.experimental.pallas import tpu as pltpu
from jax.sharding import PartitionSpec as P

BLK = 512
TLEN = 512
NLAG = 128
LANES = 128
EXTRA = 8
epsilon = 1e-06
BOTH = ("tm", "sta")
VMEM = pl.BlockSpec(memory_space=pltpu.VMEM)
SMEM = pl.BlockSpec(memory_space=pltpu.SMEM)
f32 = jnp.float32
bf16 = jnp.bfloat16


def params(**extra):
    return pltpu.CompilerParams(vmem_limit_bytes=56 << 20, **extra)


def whole(kernel, outs, flops, *operands, smem=0):
    return pl.pallas_call(
        kernel,
        out_shape=outs,
        in_specs=[SMEM] * smem + [VMEM] * (len(operands) - smem),
        out_specs=jax.tree.map(lambda _: VMEM, outs),
        compiler_params=params(),
        cost_estimate=pl.CostEstimate(flops=flops, bytes_accessed=1 << 20, transcendentals=0),
    )(*operands)


def left(values, distance):
    return pltpu.roll(values, values.shape[-1] - distance, values.ndim - 1)


def build(wave_ref, next_ref, sliding_ref, energy_ref):
    segment = jnp.concatenate([wave_ref[...], next_ref[...]], axis=1).astype(f32)
    stations, length = segment.shape
    down = lax.broadcasted_iota(jnp.int32, (LANES, LANES), 0)
    along = lax.broadcasted_iota(jnp.int32, (LANES, LANES), 1)
    flip = (down + along == LANES - 1).astype(f32).astype(bf16)
    for s in range(stations):
        row = jnp.broadcast_to(segment[s : s + 1], (LANES, length))
        moved = pltpu.roll(row, length - LANES + 1, 1, stride=1, stride_axis=0).astype(bf16)
        shifted = jnp.dot(flip, moved, preferred_element_type=f32).astype(bf16)
        for k in range(0, TLEN, LANES):
            sliding_ref[pl.ds(s * TLEN + k, LANES), :] = shifted[:, k : k + BLK]
    window = jnp.sum(segment * segment, axis=0, keepdims=True)
    window = jnp.broadcast_to(window, (EXTRA, length))
    width = 1
    while width < TLEN:
        window = window + left(window, width)
        width *= 2
    energy_ref[...] = window[:, :BLK]


def correlate(place_ref, templates_ref, sliding_ref, energy_ref, keep_ref, send_ref):
    group = keep_ref.shape[0] - EXTRA
    core = place_ref[1]
    base = place_ref[0] * 2 * group
    other = templates_ref[pl.ds(base + (1 - core) * group, group)]
    own = templates_ref[pl.ds(base + core * group, group)]
    filters = jnp.concatenate([other, own], axis=0).reshape(2 * group, -1)
    product = jnp.dot(filters, sliding_ref[...], preferred_element_type=f32)
    send_ref[:group] = product[:group]
    send_ref[group:] = energy_ref[...]
    keep_ref[:group] = product[group:]
    keep_ref[group:] = energy_ref[...]


def three(values):
    high = values.astype(bf16)
    rest = values - high.astype(f32)
    middle = rest.astype(bf16)
    low = (rest - middle.astype(f32)).astype(bf16)
    return high, middle, low


def pick(selector, parts):
    high, middle, low = [jnp.dot(selector, part, preferred_element_type=f32) for part in parts]
    return high + (middle + low)


def finish(place_ref, a_ref, b_ref, c_ref, d_ref, e_ref, flags_ref, info_ref, stack_ref, windows_ref):
    group = stack_ref.shape[0]
    total = (a_ref[...] + b_ref[...]) + (c_ref[...] + d_ref[...]) + e_ref[...]
    stack = total[:group] / jnp.sqrt(total[group : group + 1] + epsilon)
    stack_ref[...] = stack
    info = info_ref[:, 0, :]
    devices = info.shape[0]
    rows = lax.broadcasted_iota(jnp.int32, info.shape, 0)
    lanes = lax.broadcasted_iota(jnp.int32, info.shape, 1)
    counted = lanes == LANES - 1
    here = place_ref[2]
    start = jnp.sum(jnp.where(counted & (rows < here), info, 0))
    found = jnp.sum(jnp.where(counted & (rows == here), info, 0))
    mine = (info >= start) & (info < start + found) & (lanes < 32)
    rank = jnp.sum(jnp.where(mine, info - start + 1, 0), axis=1, keepdims=True) - 1
    flags = jnp.broadcast_to(flags_ref[...], (8, group)).astype(f32)
    earlier = lax.broadcasted_iota(jnp.int32, (group, group), 0) < lax.broadcasted_iota(
        jnp.int32, (group, group), 1
    )
    before = jnp.dot(flags.astype(bf16), earlier.astype(f32).astype(bf16), preferred_element_type=f32)
    before = jnp.where(flags > 0.5, before, -2.0)
    selector = jnp.broadcast_to(before[:1], (devices, group)) == rank.astype(f32)
    windows = pick(selector.astype(f32).astype(bf16), three(stack))
    windows_ref[:, 0, :] = windows


def cross(lags_ref, events_ref, info_ref, received_ref, out_ref):
    info = info_ref[:, 0, :]
    devices = info.shape[0]
    pairs = out_ref.shape[0]
    rows = lax.broadcasted_iota(jnp.int32, (devices, devices), 0)
    columns = lax.broadcasted_iota(jnp.int32, (devices, devices), 1)
    counts = jnp.broadcast_to(info[:, LANES - 1 :], (devices, devices))
    starts = jnp.sum(jnp.where(rows < columns, counts, 0), axis=0, keepdims=True)
    ends = jnp.sum(jnp.where(rows <= columns, counts, 0), axis=0, keepdims=True)
    events = events_ref[...]
    both = jnp.concatenate([events[:, 0:1], events[:, 1:2]], axis=0)
    selector = (starts <= both) & (both < ends)
    picked = pick(selector.astype(f32).astype(bf16), three(received_ref[:, 0, :]))
    first, second = picked[:pairs], picked[pairs:]
    lane = lax.broadcasted_iota(jnp.int32, (NLAG, LANES), 1)
    raw = jnp.zeros((NLAG, LANES), f32)
    length = 2 * BLK
    for p in range(pairs):
        row = jnp.concatenate([first[p : p + 1], jnp.zeros((1, BLK), f32)], axis=1)
        shift = lax.rem(lags_ref[p] + length, length)
        row = pltpu.roll(jnp.broadcast_to(row, (8, length)), shift, 1)
        row = jnp.broadcast_to(row[:1], (NLAG, length))
        moved = pltpu.roll(row, 0, 1, stride=1, stride_axis=0)
        sums = jnp.sum(moved[:, :BLK] * second[p : p + 1], axis=1, keepdims=True)
        raw = jnp.where(lane == p, sums, raw)
    raw = jnp.transpose(raw)[:pairs]
    power_one = jnp.mean(first * first, axis=1, keepdims=True)
    power_two = jnp.mean(second * second, axis=1, keepdims=True)
    out_ref[...] = raw / jnp.sqrt(BLK * (power_one + epsilon) * (power_two + epsilon))


def shards(waveforms, templates, detection_flags, pair_events, pair_lags):
    across = lax.axis_size("sta")
    ahead = lax.axis_size("tm")
    devices = across * ahead
    group = detection_flags.shape[0]
    station_group = lax.axis_index("sta")
    place = lax.axis_index("tm") * across + station_group
    plane, core = station_group // 2, station_group % 2
    planes = across // 2

    following = lax.ppermute(waveforms, "tm", [(i, i - 1) for i in range(1, ahead)])
    sliding, energy = whole(
        build,
        (
            jax.ShapeDtypeStruct((waveforms.shape[0] * TLEN, BLK), bf16),
            jax.ShapeDtypeStruct((EXTRA, BLK), f32),
        ),
        1 << 24,
        waveforms,
        following,
    )

    def partial(distance):
        where = jnp.stack([(plane + distance) % planes, core]).astype(jnp.int32)
        shape = jax.ShapeDtypeStruct((group + EXTRA, BLK), f32)
        keep, send = whole(
            correlate,
            (shape, shape),
            2 * 2 * group * templates.shape[1] * TLEN * BLK,
            where,
            templates,
            sliding,
            energy,
            smem=1,
        )
        return keep, lax.ppermute(send, "sta", [(i, i ^ 1) for i in range(across)])

    arrived = []
    for distance in (2, 1, 3):
        keep, came = partial(distance)
        route = [(i, (i + 2 * distance) % across) for i in range(across)]
        arrived.append(lax.ppermute(keep + came, "sta", route))
    keep, came = partial(0)

    count = jnp.sum(detection_flags)
    note = jnp.concatenate(
        [
            pair_events.reshape(-1),
            jnp.zeros((LANES - 1 - pair_events.size,), jnp.int32),
            count[None],
        ]
    )
    note = jnp.broadcast_to(note[None, None], (devices, 1, LANES))
    note, keep = lax.optimization_barrier((note, keep))
    info = lax.all_to_all(note, BOTH, 0, 0, tiled=True)

    here = jnp.stack([plane, core, place]).astype(jnp.int32)
    network_stack, windows = whole(
        finish,
        (
            jax.ShapeDtypeStruct((group, BLK), f32),
            jax.ShapeDtypeStruct((devices, 1, BLK), f32),
        ),
        1 << 24,
        here,
        keep,
        came,
        *arrived,
        detection_flags.reshape(1, group),
        info,
        smem=1,
    )
    received = lax.all_to_all(windows, BOTH, 0, 0, tiled=True)
    pair_cc = whole(
        cross,
        jax.ShapeDtypeStruct((pair_events.shape[0], NLAG), f32),
        1 << 24,
        pair_lags,
        pair_events,
        info,
        received,
        smem=1,
    )
    return (network_stack, pair_cc)


def solution(mesh):
    return jax.shard_map(
        shards,
        mesh=mesh,
        in_specs=(
            P("sta", "tm"),
            P(None, "sta", None),
            P("sta", "tm"),
            P(("tm", "sta"), None),
            P(("tm", "sta")),
        ),
        out_specs=(P("sta", "tm"), P(("tm", "sta"), None)),
        check_vma=False,
    )
```

profile of v0, /device:TPU:1, one launch (start us, length us, event | category | flops | bytes accessed | tf_op | source)
XLA Modules:
  0.0 119.1 jit_solution(2132835560160974135)
XLA Ops:
  0.6 1.3 %collective-permute-start = (bf16[8,512]{1,0:T(8,128)(2,1)}, bf16[8,512]{1,0:T(8,128)(2,1)S(1)}, u32[]{:S(2)}, u32[]{:S(2)}) collective-permute-start(bf16[8,512]{1,0:T(8,128)(2,1)} %wave_ref.1), channel_id=1, source_target_pairs={{8,0},{16,8},{24,16},{32,24},{40,32},{48,40},{56,48},{64,56},{72,6... | collective-permute-start | bytes 24584 | tf_op jit(solution)/shard_map/ppermute | solution.py:155
  2.0 0.7 pad_add_fusion.4
  2.7 0.6 pad_add_fusion.2
  3.3 2.5 %collective-permute-done.next_ref = bf16[8,512]{1,0:T(8,128)(2,1)S(1)} collective-permute-done((bf16[8,512]{1,0:T(8,128)(2,1)}, bf16[8,512]{1,0:T(8,128)(2,1)S(1)}, u32[]{:S(2)}, u32[]{:S(2)}) %collective-permute-start) | collective-permute-done | bytes 8224 | tf_op jit(solution)/shard_map/ppermute | solution.py:155
  5.8 0.6 copy-done.10
  6.4 3.7 %shard_map.68 = (bf16[4096,512]{1,0:T(8,128)(2,1)}, f32[8,512]{1,0:T(8,128)}) custom-call(bf16[8,512]{1,0:T(8,128)(2,1)} %wave_ref.1, bf16[8,512]{1,0:T(8,128)(2,1)} %copy-done.10), custom_call_target="tpu_custom_call" | custom-call | flops 16777216 | bytes 1048576 | tf_op jit(solution)/shard_map/pallas_call | solution.py:26
  10.1 10.6 %shard_map.72 = (f32[264,512]{1,0:T(8,128)}, f32[264,512]{1,0:T(8,128)}) custom-call(s32[2]{0:T(128)} %get-tuple-element.33.place_ref, bf16[2048,8,512]{2,1,0:T(8,128)(2,1)} %templates_ref.7, bf16[4096,512]{1,0:T(8,128)(2,1)} %get-tuple-element.16.sliding_ref, f32[8,512]{1,0:T(8,128)} %get-tuple-element.17.energy_ref), custom_call_target="tpu_custom_call" | custom-call | flops 2147483648 | bytes 1048576 | tf_op jit(solution)/shard_map/pallas_call | solution.py:26
  20.8 2.0 %collective-permute-start.6 = (f32[264,512]{1,0:T(8,128)}, f32[264,512]{1,0:T(8,128)S(1)}, u32[]{:S(2)}, u32[]{:S(2)}) collective-permute-start(f32[264,512]{1,0:T(8,128)} %get-tuple-element.26), channel_id=1, source_target_pairs={{0,1},{1,0},{2,3},{3,2},{4,5},{5,4},{6,7},{7,6},{8,9},{9,8},{10,11... | collective-permute-start | bytes 1622024 | tf_op jit(solution)/shard_map/ppermute | solution.py:180
  22.7 10.6 %shard_map.71 = (f32[264,512]{1,0:T(8,128)}, f32[264,512]{1,0:T(8,128)}) custom-call(s32[2]{0:T(128)} %get-tuple-element.32.place_ref, bf16[2048,8,512]{2,1,0:T(8,128)(2,1)} %templates_ref.7, bf16[4096,512]{1,0:T(8,128)(2,1)} %get-tuple-element.16.sliding_ref, f32[8,512]{1,0:T(8,128)} %get-tuple-element.17.energy_ref), custom_call_target="tpu_custom_call" | custom-call | flops 2147483648 | bytes 1048576 | tf_op jit(solution)/shard_map/pallas_call | solution.py:26
  33.4 0.0 collective-permute-start.4
  33.4 0.0 copy-start.2
  33.4 10.8 %shard_map.70 = (f32[264,512]{1,0:T(8,128)}, f32[264,512]{1,0:T(8,128)}) custom-call(s32[2]{0:T(128)} %get-tuple-element.31.place_ref, bf16[2048,8,512]{2,1,0:T(8,128)(2,1)} %templates_ref.7, bf16[4096,512]{1,0:T(8,128)(2,1)} %get-tuple-element.16.sliding_ref, f32[8,512]{1,0:T(8,128)} %get-tuple-element.17.energy_ref), custom_call_target="tpu_custom_call" | custom-call | flops 2147483648 | bytes 1048576 | tf_op jit(solution)/shard_map/pallas_call | solution.py:26
  44.2 0.6 collective-permute-start.2
  44.7 10.6 %shard_map.69 = (f32[264,512]{1,0:T(8,128)}, f32[264,512]{1,0:T(8,128)}) custom-call(s32[2]{0:T(128)} %get-tuple-element.30.place_ref, bf16[2048,8,512]{2,1,0:T(8,128)(2,1)} %templates_ref.7, bf16[4096,512]{1,0:T(8,128)(2,1)} %get-tuple-element.16.sliding_ref, f32[8,512]{1,0:T(8,128)} %get-tuple-element.17.energy_ref), custom_call_target="tpu_custom_call" | custom-call | flops 2147483648 | bytes 1048576 | tf_op jit(solution)/shard_map/pallas_call | solution.py:26
  55.4 0.1 collective-permute-start.1
  55.4 0.0 collective-permute-done.6
  55.4 0.0 copy-done.3
  55.4 0.1 add.49
  55.5 4.1 %collective-permute-start.7 = (f32[264,512]{1,0:T(8,128)S(1)}, f32[264,512]{1,0:T(8,128)S(1)}, u32[]{:S(2)}, u32[]{:S(2)}) collective-permute-start(f32[264,512]{1,0:T(8,128)S(1)} %add.49), channel_id=1, source_target_pairs={{0,6},{1,7},{2,0},{3,1},{4,2},{5,3},{6,4},{7,5},{8,14},{9,15},{10,... | collective-permute-start | bytes 1622024 | tf_op jit(solution)/shard_map/ppermute | solution.py:186
  59.6 0.0 collective-permute-done.4
  59.6 0.0 copy-done.2
  59.6 0.1 add.46
  59.7 0.1 collective-permute-start.5
  59.8 0.0 collective-permute-done.2
  59.8 0.0 copy-done.1
  59.8 0.1 add.43
  59.9 1.4 %collective-permute-start.3 = (f32[264,512]{1,0:T(8,128)S(1)}, f32[264,512]{1,0:T(8,128)}, u32[]{:S(2)}, u32[]{:S(2)}) collective-permute-start(f32[264,512]{1,0:T(8,128)S(1)} %add.43), channel_id=1, source_target_pairs={{0,4},{1,5},{2,6},{3,7},{4,0},{5,1},{6,2},{7,3},{8,12},{9,13},{10,... | collective-permute-start | bytes 1622024 | tf_op jit(solution)/shard_map/ppermute | solution.py:186
  61.3 0.0 copy-done.9
  61.3 0.1 copy.9.events_ref
  61.4 0.1 reshape.13
  61.5 0.0 copy-done.8
  61.5 0.6 reduce_sum.9
  62.1 0.7 pad_add_fusion.1
  62.8 0.7 broadcast_in_dim.14
  63.5 11.3 %all-to-all-start = ((s32[128,1,128]{2,1,0:T(1,128)}), s32[128,1,128]{2,1,0:T(1,128)S(1)}, u32[]{:S(2)}, u32[]{:S(2)}) async-start(s32[128,1,128]{2,1,0:T(1,128)} %broadcast_in_dim.14), calls=%async_computation | async-start | bytes 131072 | tf_op jit(solution)/shard_map/all_to_all | solution.py:199
  74.8 0.6 pad_add_fusion.place_ref
  75.4 12.2 %all-to-all-done.info_ref = s32[128,1,128]{2,1,0:T(1,128)S(1)} async-done(((s32[128,1,128]{2,1,0:T(1,128)}), s32[128,1,128]{2,1,0:T(1,128)S(1)}, u32[]{:S(2)}, u32[]{:S(2)}) %all-to-all-start) | async-done | bytes 65568 | tf_op jit(solution)/shard_map/all_to_all | solution.py:199
  87.5 0.0 collective-permute-done.1.b_ref
  87.5 0.0 collective-permute-done.7.e_ref
  87.6 0.0 collective-permute-done.5.d_ref
  87.6 0.0 collective-permute-done.3.c_ref
  87.6 0.6 copy-done
  88.2 0.2 copy-done.4
  88.4 0.2 copy-done.5
  88.6 0.2 copy-done.6
  88.8 3.3 %shard_map.73 = (f32[256,512]{1,0:T(8,128)}, f32[128,1,512]{2,1,0:T(1,128)}) custom-call(s32[3]{0:T(128)} %pad_add_fusion.place_ref, f32[264,512]{1,0:T(8,128)} %get-tuple-element.19.a_ref, f32[264,512]{1,0:T(8,128)} %copy-done.4, f32[264,512]{1,0:T(8,128)} %collective-permute-done.3.c_ref, f32[264,512]{1,0:T(8,128)} %copy-done.6, f32[264,512]{1,0:T(8,128)} %copy-done.5, ...), custom_call_target="tpu_custom_call" | custom-call | flops 16777216 | bytes 1048576 | tf_op jit(solution)/shard_map/pallas_call | solution.py:26
  92.0 20.0 %all_to_all.10.received_ref = f32[128,1,512]{2,1,0:T(1,128)} all-to-all(f32[128,1,512]{2,1,0:T(1,128)} %get-tuple-element.29), channel_id=1, replica_groups=mesh['tm'=16,'sta'=8] {'tm','sta'}, dimensions={0} | all-to-all | bytes 524288 | tf_op jit(solution)/shard_map/all_to_all | solution.py:217
  112.1 7.0 %shard_map.74 = f32[16,128]{1,0:T(8,128)} custom-call(s32[16]{0:T(128)} %lags_ref.1, s32[16,2]{1,0:T(8,128)} %copy-done.7, s32[128,1,128]{2,1,0:T(1,128)} %copy-done, f32[128,1,512]{2,1,0:T(1,128)} %all_to_all.10.received_ref), custom_call_target="tpu_custom_call" | custom-call | flops 16777216 | bytes 1048576 | tf_op jit(solution)/shard_map/pallas_call | solution.py:26
  (12 shorter events, 0.0 us)
Async XLA Ops:
  0.6 5.2 %collective-permute-start = (bf16[8,512]{1,0:T(8,128)(2,1)}, bf16[8,512]{1,0:T(8,128)(2,1)S(1)}, u32[]{:S(2)}, u32[]{:S(2)}) collective-permute-start(bf16[8,512]{1,0:T(8,128)(2,1)} %wave_ref.1), channel_id=1, source_target_pairs={{8,0},{16,8},{24,16},{32,24},{40,32},{48,40},{56,48},{64,56},{72,6... | collective-permute-start | bytes 24584 | tf_op jit(solution)/shard_map/ppermute | solution.py:155
  5.8 0.6 copy-start.10
  20.8 34.7 %collective-permute-start.6 = (f32[264,512]{1,0:T(8,128)}, f32[264,512]{1,0:T(8,128)S(1)}, u32[]{:S(2)}, u32[]{:S(2)}) collective-permute-start(f32[264,512]{1,0:T(8,128)} %get-tuple-element.26), channel_id=1, source_target_pairs={{0,1},{1,0},{2,3},{3,2},{4,5},{5,4},{6,7},{7,6},{8,9},{9,8},{10,11... | collective-permute-start | bytes 1622024 | tf_op jit(solution)/shard_map/ppermute | solution.py:180
  33.4 26.2 %collective-permute-start.4 = (f32[264,512]{1,0:T(8,128)}, f32[264,512]{1,0:T(8,128)S(1)}, u32[]{:S(2)}, u32[]{:S(2)}) collective-permute-start(f32[264,512]{1,0:T(8,128)} %get-tuple-element.24), channel_id=1, source_target_pairs={{0,1},{1,0},{2,3},{3,2},{4,5},{5,4},{6,7},{7,6},{8,9},{9,8},{10,11... | collective-permute-start | bytes 1622024 | tf_op jit(solution)/shard_map/ppermute | solution.py:180
  33.4 22.1 %copy-start.3 = (f32[264,512]{1,0:T(8,128)S(1)}, f32[264,512]{1,0:T(8,128)}, u32[]{:S(2)}) copy-start(f32[264,512]{1,0:T(8,128)} %get-tuple-element.25) | copy-start | bytes 1622020
  33.4 26.2 %copy-start.2 = (f32[264,512]{1,0:T(8,128)S(1)}, f32[264,512]{1,0:T(8,128)}, u32[]{:S(2)}) copy-start(f32[264,512]{1,0:T(8,128)} %get-tuple-element.23) | copy-start | bytes 1622020
  44.2 15.7 %copy-start.1 = (f32[264,512]{1,0:T(8,128)S(1)}, f32[264,512]{1,0:T(8,128)}, u32[]{:S(2)}) copy-start(f32[264,512]{1,0:T(8,128)} %get-tuple-element.21) | copy-start | bytes 1622020
  44.2 17.1 %copy-start.9 = (s32[16,2]{0,1:T(2,128)S(1)}, s32[16,2]{0,1:T(2,128)}, u32[]{:S(2)}) copy-start(s32[16,2]{0,1:T(2,128)} %param.8) | copy-start | bytes 388
  44.2 17.3 %copy-start.8 = (s32[256,1]{0,1:T(1,128)S(1)}, s32[256,1]{0,1:T(1,128)}, u32[]{:S(2)}) copy-start(s32[256,1]{0,1:T(1,128)} %param.7) | copy-start | bytes 3076
  44.2 15.6 %collective-permute-start.2 = (f32[264,512]{1,0:T(8,128)}, f32[264,512]{1,0:T(8,128)S(1)}, u32[]{:S(2)}, u32[]{:S(2)}) collective-permute-start(f32[264,512]{1,0:T(8,128)} %get-tuple-element.22), channel_id=1, source_target_pairs={{0,1},{1,0},{2,3},{3,2},{4,5},{5,4},{6,7},{7,6},{8,9},{9,8},{10,11... | collective-permute-start | bytes 1622024 | tf_op jit(solution)/shard_map/ppermute | solution.py:180
  55.4 32.2 %collective-permute-start.1 = (f32[264,512]{1,0:T(8,128)}, f32[264,512]{1,0:T(8,128)S(1)}, u32[]{:S(2)}, u32[]{:S(2)}) collective-permute-start(f32[264,512]{1,0:T(8,128)} %get-tuple-element.20), channel_id=1, source_target_pairs={{0,1},{1,0},{2,3},{3,2},{4,5},{5,4},{6,7},{7,6},{8,9},{9,8},{10,11... | collective-permute-start | bytes 1622024 | tf_op jit(solution)/shard_map/ppermute | solution.py:180
  55.5 32.0 %collective-permute-start.7 = (f32[264,512]{1,0:T(8,128)S(1)}, f32[264,512]{1,0:T(8,128)S(1)}, u32[]{:S(2)}, u32[]{:S(2)}) collective-permute-start(f32[264,512]{1,0:T(8,128)S(1)} %add.49), channel_id=1, source_target_pairs={{0,6},{1,7},{2,0},{3,1},{4,2},{5,3},{6,4},{7,5},{8,14},{9,15},{10,... | collective-permute-start | bytes 1622024 | tf_op jit(solution)/shard_map/ppermute | solution.py:186
  59.7 27.9 %collective-permute-start.5 = (f32[264,512]{1,0:T(8,128)S(1)}, f32[264,512]{1,0:T(8,128)S(1)}, u32[]{:S(2)}, u32[]{:S(2)}) collective-permute-start(f32[264,512]{1,0:T(8,128)S(1)} %add.46), channel_id=1, source_target_pairs={{0,2},{1,3},{2,4},{3,5},{4,6},{5,7},{6,0},{7,1},{8,10},{9,11},{10,... | collective-permute-start | bytes 1622024 | tf_op jit(solution)/shard_map/ppermute | solution.py:186
  59.9 27.7 %collective-permute-start.3 = (f32[264,512]{1,0:T(8,128)S(1)}, f32[264,512]{1,0:T(8,128)}, u32[]{:S(2)}, u32[]{:S(2)}) collective-permute-start(f32[264,512]{1,0:T(8,128)S(1)} %add.43), channel_id=1, source_target_pairs={{0,4},{1,5},{2,6},{3,7},{4,0},{5,1},{6,2},{7,3},{8,12},{9,13},{10,... | collective-permute-start | bytes 1622024 | tf_op jit(solution)/shard_map/ppermute | solution.py:186
  61.4 50.7 %copy-start.7 = (s32[16,2]{1,0:T(8,128)}, s32[16,2]{1,0:T(8,128)S(1)}, u32[]{:S(2)}) copy-start(s32[16,2]{1,0:T(8,128)S(1)} %copy.9.events_ref) | copy-start | bytes 388
  63.5 24.1 %all-to-all-start = ((s32[128,1,128]{2,1,0:T(1,128)}), s32[128,1,128]{2,1,0:T(1,128)S(1)}, u32[]{:S(2)}, u32[]{:S(2)}) async-start(s32[128,1,128]{2,1,0:T(1,128)} %broadcast_in_dim.14), calls=%async_computation | async-start | bytes 131072 | tf_op jit(solution)/shard_map/all_to_all | solution.py:199
  87.5 0.6 copy-start
  87.5 0.8 copy-start.4
  87.6 1.0 copy-start.5
  87.6 1.2 %copy-start.6 = (f32[264,512]{1,0:T(8,128)}, f32[264,512]{1,0:T(8,128)S(1)}, u32[]{:S(2)}) copy-start(f32[264,512]{1,0:T(8,128)S(1)} %collective-permute-done.5.d_ref) | copy-start | bytes 1622020
where the time goes:
time: 119 us
  Pallas kernels  56.6 us (48%)
  starting transfers between devices  20.7 us (17%)
  blocking collectives  20 us (17%)
  waiting for transfers between devices  14.7 us (12%)
  other arithmetic  3.48 us (3%)
  local copies, waits for them, and re-layouts  2.64 us (2%)
    pallas_call x7, Pallas kernels, whole(): pl.pallas_call(kernel, out_shape=outs, in_specs=[SMEM] * smem + [VMEM] *...  56.6 us
    all_to_all x1, blocking collectives, shards(): received = lax.all_to_all(windows, BOTH, 0, 0, tiled=True)  20 us
    all_to_all x1, waiting for transfers between devices, shards(): info = lax.all_to_all(note, BOTH, 0, 0, tiled=True)  12.2 us
    all_to_all x1, starting transfers between devices, shards(): info = lax.all_to_all(note, BOTH, 0, 0, tiled=True)  11.3 us
    ppermute x3, starting transfers between devices, shards(): arrived.append(lax.ppermute(keep + came, 'sta', route))  5.53 us
    ppermute x4, starting transfers between devices, partial(): lax.ppermute(send, 'sta', [(i, i ^ 1) for i in range(across)])  2.62 us
    ppermute x1, waiting for transfers between devices, shards(): lax.ppermute(waveforms, 'tm', [(i, i - 1) for i in range(1, ahead)])  2.51 us
  transfers between devices with their start and end apart: 9, of which 2 were waited for; matrix products, arithmetic and copies ran while one was open for 4% of the time, Pallas kernels for 27%

commit v1 on v0

--- a/solution.py
+++ b/solution.py
@@ -18,19 +18,21 @@
 bf16 = jnp.bfloat16
 
 
-def params(**extra):
-    return pltpu.CompilerParams(vmem_limit_bytes=56 << 20, **extra)
-
-
 def whole(kernel, outs, flops, *operands, smem=0):
     return pl.pallas_call(
         kernel,
         out_shape=outs,
         in_specs=[SMEM] * smem + [VMEM] * (len(operands) - smem),
         out_specs=jax.tree.map(lambda _: VMEM, outs),
-        compiler_params=params(),
+        compiler_params=pltpu.CompilerParams(vmem_limit_bytes=20 << 20),
         cost_estimate=pl.CostEstimate(flops=flops, bytes_accessed=1 << 20, transcendentals=0),
     )(*operands)
+
+
+def fetch(templates_ref, held_ref, arrival):
+    copy = pltpu.make_async_copy(templates_ref, held_ref, arrival)
+    copy.start()
+    copy.wait()
 
 
 def left(values, distance):
@@ -152,27 +154,37 @@
     plane, core = station_group // 2, station_group % 2
     planes = across // 2
 
+    held = pl.pallas_call(
+        fetch,
+        out_shape=pltpu.VMEM(templates.shape, templates.dtype),
+        in_specs=[pl.BlockSpec(memory_space=pltpu.HBM)],
+        out_specs=VMEM,
+        scratch_shapes=[pltpu.SemaphoreType.DMA],
+        compiler_params=pltpu.CompilerParams(vmem_limit_bytes=20 << 20),
+        cost_estimate=pl.CostEstimate(flops=0, bytes_accessed=2 * templates.size * 2, transcendentals=0),
+    )(templates)
     following = lax.ppermute(waveforms, "tm", [(i, i - 1) for i in range(1, ahead)])
     sliding, energy = whole(
         build,
         (
-            jax.ShapeDtypeStruct((waveforms.shape[0] * TLEN, BLK), bf16),
-            jax.ShapeDtypeStruct((EXTRA, BLK), f32),
+            pltpu.VMEM((waveforms.shape[0] * TLEN, BLK), bf16),
+            pltpu.VMEM((EXTRA, BLK), f32),
         ),
         1 << 24,
         waveforms,
         following,
     )
 
-    def partial(distance):
+    def partial(distance, after):
         where = jnp.stack([(plane + distance) % planes, core]).astype(jnp.int32)
-        shape = jax.ShapeDtypeStruct((group + EXTRA, BLK), f32)
+        where, after = lax.optimization_barrier((where, after))
+        shape = pltpu.VMEM((group + EXTRA, BLK), f32)
         keep, send = whole(
             correlate,
             (shape, shape),
             2 * 2 * group * templates.shape[1] * TLEN * BLK,
             where,
-            templates,
+            held,
             sliding,
             energy,
             smem=1,
@@ -180,11 +192,15 @@
         return keep, lax.ppermute(send, "sta", [(i, i ^ 1) for i in range(across)])
 
     arrived = []
-    for distance in (2, 1, 3):
-        keep, came = partial(distance)
+    order = (2, 1, 3, 0)
+    keep, came = partial(order[0], ())
+    for distance, following in zip(order, order[1:]):
+        after = () if distance == order[0] else (total,)
+        new = partial(following, after)
+        total = keep + came
         route = [(i, (i + 2 * distance) % across) for i in range(across)]
-        arrived.append(lax.ppermute(keep + came, "sta", route))
-    keep, came = partial(0)
+        arrived.append(lax.ppermute(total, "sta", route))
+        keep, came = new
 
     count = jnp.sum(detection_flags)
     note = jnp.concatenate(
@@ -195,7 +211,7 @@
         ]
     )
     note = jnp.broadcast_to(note[None, None], (devices, 1, LANES))
-    note, keep = lax.optimization_barrier((note, keep))
+    note, _ = lax.optimization_barrier((note, total))
     info = lax.all_to_all(note, BOTH, 0, 0, tiled=True)
 
     here = jnp.stack([plane, core, place]).astype(jnp.int32)

time: 119 us -> 102 us (0.86)
  Pallas kernels: 56.6 us -> 24.1 us
  local copies, waits for them, and re-layouts: 2.64 us -> 28.3 us
  waiting for transfers between devices: 14.7 us -> 9.26 us
  blocking collectives: 20 us -> 15.3 us
  starting transfers between devices: 20.7 us -> 18.4 us
  other arithmetic: 3.48 us -> 5.63 us
    pallas_call x7, Pallas kernels: 56.6 us -> 22.9 us  [whole(): pl.pallas_call(kernel, out_shape=outs, in_specs=[SMEM] * smem + [VMEM] *...]
    unnamed x23, local copies, waits for them, and re-layouts: 1.89 us -> 27.5 us
    all_to_all x1, blocking collectives: 20 us -> 15.3 us  [shards(): received = lax.all_to_all(windows, BOTH, 0, 0, tiled=True)]
    add x3, other arithmetic: 0.25 us -> 3.96 us  [shards(): total = keep + came]
    all_to_all x1, starting transfers between devices: 11.3 us -> 7.98 us  [shards(): info = lax.all_to_all(note, BOTH, 0, 0, tiled=True)]
    all_to_all x1, waiting for transfers between devices: 12.2 us -> 9.24 us  [shards(): info = lax.all_to_all(note, BOTH, 0, 0, tiled=True)]
    ppermute x1, waiting for transfers between devices: 2.51 us -> 0.01 us  [shards(): lax.ppermute(waveforms, 'tm', [(i, i - 1) for i in range(1, ahead)])]
  transfers between devices with their start and end apart: 9 -> 9, of which waited for: 2 -> 1; matrix products, arithmetic and copies ran while one was open for 4% -> 6% of each run, Pallas kernels for 27% -> 11%
where the time goes in v1:
time: 102 us
  local copies, waits for them, and re-layouts  28.3 us (28%)
  Pallas kernels  24.1 us (24%)
  starting transfers between devices  18.4 us (18%)
  blocking collectives  15.3 us (15%)
  waiting for transfers between devices  9.26 us (9%)
  other arithmetic  5.63 us (6%)
    unnamed x23, local copies, waits for them, and re-layouts  27.5 us
    pallas_call x7, Pallas kernels, whole(): pl.pallas_call(kernel, out_shape=outs, in_specs=[SMEM] * smem + [VMEM] *...  22.9 us
    all_to_all x1, blocking collectives, shards(): received = lax.all_to_all(windows, BOTH, 0, 0, tiled=True)  15.3 us
    all_to_all x1, waiting for transfers between devices, shards(): info = lax.all_to_all(note, BOTH, 0, 0, tiled=True)  9.24 us
    all_to_all x1, starting transfers between devices, shards(): info = lax.all_to_all(note, BOTH, 0, 0, tiled=True)  7.98 us
    ppermute x3, starting transfers between devices, shards(): arrived.append(lax.ppermute(total, 'sta', route))  6.43 us
    add x3, other arithmetic, shards(): total = keep + came  3.96 us
    ppermute x4, starting transfers between devices, partial(): lax.ppermute(send, 'sta', [(i, i ^ 1) for i in range(across)])  2.69 us
  transfers between devices with their start and end apart: 9, of which 1 were waited for; matrix products, arithmetic and copies ran while one was open for 6% of the time, Pallas kernels for 11%

profile of v1, /device:TPU:1, one launch (start us, length us, event | category | flops | bytes accessed | tf_op | source)
XLA Modules:
  0.0 101.8 jit_solution(4360969998010179843)
XLA Ops:
  0.6 1.3 %collective-permute-start = (bf16[8,512]{1,0:T(8,128)(2,1)}, bf16[8,512]{1,0:T(8,128)(2,1)S(1)}, u32[]{:S(2)}, u32[]{:S(2)}) collective-permute-start(bf16[8,512]{1,0:T(8,128)(2,1)} %wave_ref.1), channel_id=1, source_target_pairs={{8,0},{16,8},{24,16},{32,24},{40,32},{48,40},{56,48},{64,56},{72,6... | collective-permute-start | bytes 24584 | tf_op jit(solution)/shard_map/ppermute | solution.py:166
  2.0 0.1 pad_add_fusion.2
  2.1 5.8 %copy-done.6 = bf16[2048,8,512]{2,1,0:T(8,128)(2,1)S(1)} copy-done((bf16[2048,8,512]{2,1,0:T(8,128)(2,1)S(1)}, bf16[2048,8,512]{2,1,0:T(8,128)(2,1)}, u32[]{:S(2)}) %copy-start.6) | copy-done | bytes 16777240
  7.8 1.2 %shard_map.68.templates_ref = bf16[2048,8,512]{2,1,0:T(8,128)(2,1)S(1)} custom-call(bf16[2048,8,512]{2,1,0:T(8,128)(2,1)S(1)} %copy-done.6), custom_call_target="tpu_custom_call" | custom-call | bytes 33554432 | tf_op jit(solution)/shard_map/pallas_call | solution.py:157
  9.0 0.0 collective-permute-done.next_ref
  9.0 1.1 %shard_map.69 = (bf16[4096,512]{1,0:T(8,128)(2,1)S(1)}, f32[8,512]{1,0:T(8,128)S(1)}) custom-call(bf16[8,512]{1,0:T(8,128)(2,1)S(1)} %copy-done.9, bf16[8,512]{1,0:T(8,128)(2,1)S(1)} %collective-permute-done.next_ref), custom_call_target="tpu_custom_call" | custom-call | flops 16777216 | bytes 1048576 | tf_op jit(solution)/shard_map/pallas_call | solution.py:22
  10.1 3.2 %shard_map.72 = (f32[264,512]{1,0:T(8,128)S(1)}, f32[264,512]{1,0:T(8,128)S(1)}) custom-call(s32[2]{0:T(128)S(1)} %get-tuple-element.33.place_ref, bf16[2048,8,512]{2,1,0:T(8,128)(2,1)S(1)} %shard_map.68.templates_ref, bf16[4096,512]{1,0:T(8,128)(2,1)S(1)} %get-tuple-element.17.sliding_ref, f32[8,512]{1,0:T(8,128)S(1)} %get-tuple-element.18.energy_ref), custom_call_target="tpu_custom_call" | custom-call | flops 2147483648 | bytes 1048576 | tf_op jit(solution)/shard_map/pallas_call | solution.py:22
  13.3 5.7 %copy-done = bf16[2048,8,512]{2,1,0:T(8,128)(2,1)} copy-done((bf16[2048,8,512]{2,1,0:T(8,128)(2,1)}, bf16[2048,8,512]{2,1,0:T(8,128)(2,1)S(1)}, u32[]{:S(2)}) %copy-start) | copy-done | bytes 16777240
  19.0 1.4 %collective-permute-start.3 = (f32[264,512]{1,0:T(8,128)S(1)}, f32[264,512]{1,0:T(8,128)S(1)}, u32[]{:S(2)}, u32[]{:S(2)}) collective-permute-start(f32[264,512]{1,0:T(8,128)S(1)} %get-tuple-element.25), channel_id=1, source_target_pairs={{0,1},{1,0},{2,3},{3,2},{4,5},{5,4},{6,7},{7,6},{8,9},{9,8},{10,11... | collective-permute-start | bytes 1622024 | tf_op jit(solution)/shard_map/ppermute | solution.py:192
  20.5 5.8 %copy-done.1 = bf16[2048,8,512]{2,1,0:T(8,128)(2,1)S(1)} copy-done((bf16[2048,8,512]{2,1,0:T(8,128)(2,1)S(1)}, bf16[2048,8,512]{2,1,0:T(8,128)(2,1)}, u32[]{:S(2)}) %copy-start.1) | copy-done | bytes 16777240
  26.2 2.2 %copy-done.4 = bf16[4096,512]{1,0:T(8,128)(2,1)S(1)} copy-done((bf16[4096,512]{1,0:T(8,128)(2,1)S(1)}, bf16[4096,512]{1,0:T(8,128)(2,1)}, u32[]{:S(2)}) %copy-start.4) | copy-done | bytes 4194328
  28.4 3.2 %shard_map.70 = (f32[264,512]{1,0:T(8,128)S(1)}, f32[264,512]{1,0:T(8,128)S(1)}) custom-call(s32[2]{0:T(128)S(1)} %get-tuple-element.32.place_ref, bf16[2048,8,512]{2,1,0:T(8,128)(2,1)S(1)} %copy-done.1, bf16[4096,512]{1,0:T(8,128)(2,1)S(1)} %copy-done.4, f32[8,512]{1,0:T(8,128)S(1)} %get-tuple-element.18.energy_ref), custom_call_target="tpu_custom_call" | custom-call | flops 2147483648 | bytes 1048576 | tf_op jit(solution)/shard_map/pallas_call | solution.py:22
  31.6 0.1 collective-permute-start.1
  31.7 0.1 pad_add_fusion.4.place_ref
  31.8 0.0 collective-permute-done.3
  31.8 0.9 add.46
  32.7 3.2 %shard_map.73 = (f32[264,512]{1,0:T(8,128)S(1)}, f32[264,512]{1,0:T(8,128)S(1)}) custom-call(s32[2]{0:T(128)S(1)} %pad_add_fusion.4.place_ref, bf16[2048,8,512]{2,1,0:T(8,128)(2,1)S(1)} %copy-done.1, bf16[4096,512]{1,0:T(8,128)(2,1)S(1)} %copy-done.4, f32[8,512]{1,0:T(8,128)S(1)} %get-tuple-element.18.energy_ref), custom_call_target="tpu_custom_call" | custom-call | flops 2147483648 | bytes 1048576 | tf_op jit(solution)/shard_map/pallas_call | solution.py:22
  35.8 0.0 copy-start.7
  35.8 0.0 copy-start.10
  35.9 0.0 copy-start.8
  35.9 0.6 collective-permute-start.6
  36.4 0.1 pad_add_fusion.1.place_ref
  36.5 3.7 %collective-permute-start.4 = (f32[264,512]{1,0:T(8,128)}, f32[264,512]{1,0:T(8,128)S(1)}, u32[]{:S(2)}, u32[]{:S(2)}) collective-permute-start(f32[264,512]{1,0:T(8,128)} %add.46), channel_id=1, source_target_pairs={{0,4},{1,5},{2,6},{3,7},{4,0},{5,1},{6,2},{7,3},{8,12},{9,13},{10,... | collective-permute-start | bytes 1622024 | tf_op jit(solution)/shard_map/ppermute | solution.py:202
  40.2 0.0 collective-permute-done.1
  40.2 1.9 %add.43 = f32[264,512]{1,0:T(8,128)} add(f32[264,512]{1,0:T(8,128)S(1)} %get-tuple-element.19, f32[264,512]{1,0:T(8,128)} %collective-permute-done.1) | non-fusion elementwise | flops 135168 | bytes 1622016 | tf_op jit(solution)/shard_map/add | solution.py:200
  42.1 0.7 collective-permute-start.5
  42.9 5.8 %copy-done.2 = bf16[2048,8,512]{2,1,0:T(8,128)(2,1)S(1)} copy-done((bf16[2048,8,512]{2,1,0:T(8,128)(2,1)S(1)}, bf16[2048,8,512]{2,1,0:T(8,128)(2,1)}, u32[]{:S(2)}) %copy-start.2) | copy-done | bytes 16777240
  48.6 2.2 %copy-done.5 = bf16[4096,512]{1,0:T(8,128)(2,1)S(1)} copy-done((bf16[4096,512]{1,0:T(8,128)(2,1)S(1)}, bf16[4096,512]{1,0:T(8,128)(2,1)}, u32[]{:S(2)}) %copy-start.5) | copy-done | bytes 4194328
  50.8 3.9 %shard_map.71 = (f32[264,512]{1,0:T(8,128)S(1)}, f32[264,512]{1,0:T(8,128)}) custom-call(s32[2]{0:T(128)S(1)} %pad_add_fusion.1.place_ref, bf16[2048,8,512]{2,1,0:T(8,128)(2,1)S(1)} %copy-done.2, bf16[4096,512]{1,0:T(8,128)(2,1)S(1)} %copy-done.5, f32[8,512]{1,0:T(8,128)S(1)} %get-tuple-element.18.energy_ref), custom_call_target="tpu_custom_call" | custom-call | flops 2147483648 | bytes 1048576 | tf_op jit(solution)/shard_map/pallas_call | solution.py:22
  54.7 0.6 collective-permute-start.2
  55.3 0.0 collective-permute-done.6
  55.4 1.1 %add.49 = f32[264,512]{1,0:T(8,128)S(1)} add(f32[264,512]{1,0:T(8,128)S(1)} %get-tuple-element.27, f32[264,512]{1,0:T(8,128)} %collective-permute-done.6) | non-fusion elementwise | flops 135168 | bytes 1622016 | tf_op jit(solution)/shard_map/add | solution.py:200
  56.5 2.0 %collective-permute-start.7 = (f32[264,512]{1,0:T(8,128)S(1)}, f32[264,512]{1,0:T(8,128)S(1)}, u32[]{:S(2)}, u32[]{:S(2)}) collective-permute-start(f32[264,512]{1,0:T(8,128)S(1)} %add.49), channel_id=1, source_target_pairs={{0,6},{1,7},{2,0},{3,1},{4,2},{5,3},{6,4},{7,5},{8,14},{9,15},{10,... | collective-permute-start | bytes 1622024 | tf_op jit(solution)/shard_map/ppermute | solution.py:202
  58.5 0.6 reduce_sum.9
  59.1 0.1 copy.9.events_ref
  59.2 0.1 reshape.14
  59.3 0.7 pad_add_fusion.5
  60.0 0.7 broadcast_in_dim.14
  60.7 8.0 %all-to-all-start = ((s32[128,1,128]{2,1,0:T(1,128)}), s32[128,1,128]{2,1,0:T(1,128)S(1)}, u32[]{:S(2)}, u32[]{:S(2)}) async-start(s32[128,1,128]{2,1,0:T(1,128)} %broadcast_in_dim.14), calls=%async_computation | async-start | bytes 131072 | tf_op jit(solution)/shard_map/all_to_all | solution.py:215
  68.7 0.1 pad_add_fusion.place_ref
  68.8 0.0 collective-permute-done.4.c_ref
  68.8 0.0 collective-permute-done.2.b_ref
  68.8 0.0 collective-permute-done.5.d_ref
  68.8 9.2 %all-to-all-done.info_ref = s32[128,1,128]{2,1,0:T(1,128)S(1)} async-done(((s32[128,1,128]{2,1,0:T(1,128)}), s32[128,1,128]{2,1,0:T(1,128)S(1)}, u32[]{:S(2)}, u32[]{:S(2)}) %all-to-all-start) | async-done | bytes 65568 | tf_op jit(solution)/shard_map/all_to_all | solution.py:215
  78.0 0.0 collective-permute-done.7.e_ref
  78.0 1.9 %shard_map.74 = (f32[256,512]{1,0:T(8,128)}, f32[128,1,512]{2,1,0:T(1,128)S(1)}) custom-call(s32[3]{0:T(128)S(1)} %pad_add_fusion.place_ref, f32[264,512]{1,0:T(8,128)S(1)} %get-tuple-element.22.a_ref, f32[264,512]{1,0:T(8,128)S(1)} %collective-permute-done.2.b_ref, f32[264,512]{1,0:T(8,128)S(1)} %collective-permute-done.4.c_ref, ...), custom_call_target="tpu_custom_call" | custom-call | flops 16777216 | bytes 1048576 | tf_op jit(solution)/shard_map/pallas_call | solution.py:22
  79.9 15.3 %all_to_all.10.received_ref = f32[128,1,512]{2,1,0:T(1,128)S(1)} all-to-all(f32[128,1,512]{2,1,0:T(1,128)S(1)} %get-tuple-element.31), channel_id=1, replica_groups=mesh['tm'=16,'sta'=8] {'tm','sta'}, dimensions={0} | all-to-all | bytes 524288 | tf_op jit(solution)/shard_map/all_to_all | solution.py:233
  95.3 6.5 %shard_map.75 = f32[16,128]{1,0:T(8,128)} custom-call(s32[16]{0:T(128)S(1)} %copy-done.8, s32[16,2]{1,0:T(8,128)S(1)} %copy.9.events_ref, s32[128,1,128]{2,1,0:T(1,128)S(1)} %all-to-all-done.info_ref, f32[128,1,512]{2,1,0:T(1,128)S(1)} %all_to_all.10.received_ref), custom_call_target="tpu_custom_call" | custom-call | flops 16777216 | bytes 1048576 | tf_op jit(solution)/shard_map/pallas_call | solution.py:22
  (14 shorter events, 0.0 us)
Async XLA Ops:
  0.6 8.4 %collective-permute-start = (bf16[8,512]{1,0:T(8,128)(2,1)}, bf16[8,512]{1,0:T(8,128)(2,1)S(1)}, u32[]{:S(2)}, u32[]{:S(2)}) collective-permute-start(bf16[8,512]{1,0:T(8,128)(2,1)} %wave_ref.1), channel_id=1, source_target_pairs={{8,0},{16,8},{24,16},{32,24},{40,32},{48,40},{56,48},{64,56},{72,6... | collective-permute-start | bytes 24584 | tf_op jit(solution)/shard_map/ppermute | solution.py:166
  2.1 5.8 %copy-start.6 = (bf16[2048,8,512]{2,1,0:T(8,128)(2,1)S(1)}, bf16[2048,8,512]{2,1,0:T(8,128)(2,1)}, u32[]{:S(2)}) copy-start(bf16[2048,8,512]{2,1,0:T(8,128)(2,1)} %templates_ref.1) | copy-start | bytes 50331652
  7.8 1.2 %copy-start.9 = (bf16[8,512]{1,0:T(8,128)(2,1)S(1)}, bf16[8,512]{1,0:T(8,128)(2,1)}, u32[]{:S(2)}) copy-start(bf16[8,512]{1,0:T(8,128)(2,1)} %wave_ref.1) | copy-start | bytes 24580
  10.1 3.2 %copy-start.3 = (bf16[4096,512]{1,0:T(8,128)(2,1)}, bf16[4096,512]{1,0:T(8,128)(2,1)S(1)}, u32[]{:S(2)}) copy-start(bf16[4096,512]{1,0:T(8,128)(2,1)S(1)} %get-tuple-element.17.sliding_ref) | copy-start | bytes 12582916
  13.3 5.7 %copy-start = (bf16[2048,8,512]{2,1,0:T(8,128)(2,1)}, bf16[2048,8,512]{2,1,0:T(8,128)(2,1)S(1)}, u32[]{:S(2)}) copy-start(bf16[2048,8,512]{2,1,0:T(8,128)(2,1)S(1)} %shard_map.68.templates_ref) | copy-start | bytes 50331652
  19.0 12.7 %collective-permute-start.3 = (f32[264,512]{1,0:T(8,128)S(1)}, f32[264,512]{1,0:T(8,128)S(1)}, u32[]{:S(2)}, u32[]{:S(2)}) collective-permute-start(f32[264,512]{1,0:T(8,128)S(1)} %get-tuple-element.25), channel_id=1, source_target_pairs={{0,1},{1,0},{2,3},{3,2},{4,5},{5,4},{6,7},{7,6},{8,9},{9,8},{10,11... | collective-permute-start | bytes 1622024 | tf_op jit(solution)/shard_map/ppermute | solution.py:192
  20.5 5.8 %copy-start.1 = (bf16[2048,8,512]{2,1,0:T(8,128)(2,1)S(1)}, bf16[2048,8,512]{2,1,0:T(8,128)(2,1)}, u32[]{:S(2)}) copy-start(bf16[2048,8,512]{2,1,0:T(8,128)(2,1)} %copy-done) | copy-start | bytes 50331652
  26.2 2.2 %copy-start.4 = (bf16[4096,512]{1,0:T(8,128)(2,1)S(1)}, bf16[4096,512]{1,0:T(8,128)(2,1)}, u32[]{:S(2)}) copy-start(bf16[4096,512]{1,0:T(8,128)(2,1)} %copy-done.3) | copy-start | bytes 12582916
  31.6 8.6 %collective-permute-start.1 = (f32[264,512]{1,0:T(8,128)S(1)}, f32[264,512]{1,0:T(8,128)}, u32[]{:S(2)}, u32[]{:S(2)}) collective-permute-start(f32[264,512]{1,0:T(8,128)S(1)} %get-tuple-element.20), channel_id=1, source_target_pairs={{0,1},{1,0},{2,3},{3,2},{4,5},{5,4},{6,7},{7,6},{8,9},{9,8},{10,11... | collective-permute-start | bytes 1622024 | tf_op jit(solution)/shard_map/ppermute | solution.py:192
  35.8 22.7 %copy-start.7 = (s32[256,1]{0,1:T(1,128)S(1)}, s32[256,1]{0,1:T(1,128)}, u32[]{:S(2)}) copy-start(s32[256,1]{0,1:T(1,128)} %param.7) | copy-start | bytes 3076
  35.8 23.3 %copy-start.10 = (s32[16,2]{0,1:T(2,128)S(1)}, s32[16,2]{0,1:T(2,128)}, u32[]{:S(2)}) copy-start(s32[16,2]{0,1:T(2,128)} %param.8) | copy-start | bytes 388
  35.9 59.4 %copy-start.8 = (s32[16]{0:T(128)S(1)}, s32[16]{0:T(128)}, u32[]{:S(2)}) copy-start(s32[16]{0:T(128)} %lags_ref.1) | copy-start | bytes 196
  35.9 19.5 %collective-permute-start.6 = (f32[264,512]{1,0:T(8,128)S(1)}, f32[264,512]{1,0:T(8,128)}, u32[]{:S(2)}, u32[]{:S(2)}) collective-permute-start(f32[264,512]{1,0:T(8,128)S(1)} %get-tuple-element.28), channel_id=1, source_target_pairs={{0,1},{1,0},{2,3},{3,2},{4,5},{5,4},{6,7},{7,6},{8,9},{9,8},{10,11... | collective-permute-start | bytes 1622024 | tf_op jit(solution)/shard_map/ppermute | solution.py:192
  36.5 32.3 %collective-permute-start.4 = (f32[264,512]{1,0:T(8,128)}, f32[264,512]{1,0:T(8,128)S(1)}, u32[]{:S(2)}, u32[]{:S(2)}) collective-permute-start(f32[264,512]{1,0:T(8,128)} %add.46), channel_id=1, source_target_pairs={{0,4},{1,5},{2,6},{3,7},{4,0},{5,1},{6,2},{7,3},{8,12},{9,13},{10,... | collective-permute-start | bytes 1622024 | tf_op jit(solution)/shard_map/ppermute | solution.py:202
  42.1 26.7 %collective-permute-start.5 = (f32[264,512]{1,0:T(8,128)}, f32[264,512]{1,0:T(8,128)S(1)}, u32[]{:S(2)}, u32[]{:S(2)}) collective-permute-start(f32[264,512]{1,0:T(8,128)} %add.43), channel_id=1, source_target_pairs={{0,2},{1,3},{2,4},{3,5},{4,6},{5,7},{6,0},{7,1},{8,10},{9,11},{10,... | collective-permute-start | bytes 1622024 | tf_op jit(solution)/shard_map/ppermute | solution.py:202
  42.9 5.8 %copy-start.2 = (bf16[2048,8,512]{2,1,0:T(8,128)(2,1)S(1)}, bf16[2048,8,512]{2,1,0:T(8,128)(2,1)}, u32[]{:S(2)}) copy-start(bf16[2048,8,512]{2,1,0:T(8,128)(2,1)} %copy-done) | copy-start | bytes 50331652
  48.6 2.2 %copy-start.5 = (bf16[4096,512]{1,0:T(8,128)(2,1)S(1)}, bf16[4096,512]{1,0:T(8,128)(2,1)}, u32[]{:S(2)}) copy-start(bf16[4096,512]{1,0:T(8,128)(2,1)} %copy-done.3) | copy-start | bytes 12582916
  54.7 14.0 %collective-permute-start.2 = (f32[264,512]{1,0:T(8,128)}, f32[264,512]{1,0:T(8,128)S(1)}, u32[]{:S(2)}, u32[]{:S(2)}) collective-permute-start(f32[264,512]{1,0:T(8,128)} %get-tuple-element.23), channel_id=1, source_target_pairs={{0,1},{1,0},{2,3},{3,2},{4,5},{5,4},{6,7},{7,6},{8,9},{9,8},{10,11... | collective-permute-start | bytes 1622024 | tf_op jit(solution)/shard_map/ppermute | solution.py:192
  56.5 21.5 %collective-permute-start.7 = (f32[264,512]{1,0:T(8,128)S(1)}, f32[264,512]{1,0:T(8,128)S(1)}, u32[]{:S(2)}, u32[]{:S(2)}) collective-permute-start(f32[264,512]{1,0:T(8,128)S(1)} %add.49), channel_id=1, source_target_pairs={{0,6},{1,7},{2,0},{3,1},{4,2},{5,3},{6,4},{7,5},{8,14},{9,15},{10,... | collective-permute-start | bytes 1622024 | tf_op jit(solution)/shard_map/ppermute | solution.py:202
  60.7 17.3 %all-to-all-start = ((s32[128,1,128]{2,1,0:T(1,128)}), s32[128,1,128]{2,1,0:T(1,128)S(1)}, u32[]{:S(2)}, u32[]{:S(2)}) async-start(s32[128,1,128]{2,1,0:T(1,128)} %broadcast_in_dim.14), calls=%async_computation | async-start | bytes 131072 | tf_op jit(solution)/shard_map/all_to_all | solution.py:215

commit v2 on v0

v2 whole, which is shorter than its diff:
```python
import functools

import jax
import jax.numpy as jnp
from jax import lax
from jax.experimental import pallas as pl
from jax.experimental.pallas import tpu as pltpu
from jax.sharding import PartitionSpec as P

BLK = 512
TLEN = 512
NLAG = 128
LANES = 128
EXTRA = 8
epsilon = 1e-06
BOTH = ("tm", "sta")
VMEM = pl.BlockSpec(memory_space=pltpu.VMEM)
SMEM = pl.BlockSpec(memory_space=pltpu.SMEM)
f32 = jnp.float32
bf16 = jnp.bfloat16


def whole(kernel, outs, flops, *operands, smem=0, scratch=()):
    return pl.pallas_call(
        kernel,
        out_shape=outs,
        in_specs=[SMEM] * smem + [VMEM] * (len(operands) - smem),
        out_specs=jax.tree.map(lambda _: VMEM, outs),
        scratch_shapes=scratch,
        compiler_params=pltpu.CompilerParams(vmem_limit_bytes=20 << 20),
        cost_estimate=pl.CostEstimate(flops=flops, bytes_accessed=1 << 20, transcendentals=0),
    )(*operands)


def left(values, distance):
    return pltpu.roll(values, values.shape[-1] - distance, values.ndim - 1)


def build(segment, sliding_ref):
    stations, length = segment.shape
    down = lax.broadcasted_iota(jnp.int32, (LANES, LANES), 0)
    along = lax.broadcasted_iota(jnp.int32, (LANES, LANES), 1)
    flip = (down + along == LANES - 1).astype(f32).astype(bf16)
    for s in range(stations):
        row = jnp.broadcast_to(segment[s : s + 1], (LANES, length))
        moved = pltpu.roll(row, length - LANES + 1, 1, stride=1, stride_axis=0).astype(bf16)
        shifted = jnp.dot(flip, moved, preferred_element_type=f32).astype(bf16)
        for k in range(0, TLEN, LANES):
            sliding_ref[pl.ds(s * TLEN + k, LANES), :] = shifted[:, k : k + BLK]


def energy_of(segment):
    window = jnp.sum(segment * segment, axis=0, keepdims=True)
    window = jnp.broadcast_to(window, (EXTRA, window.shape[1]))
    width = 1
    while width < TLEN:
        window = window + left(window, width)
        width *= 2
    return window[:, :BLK]


def correlate(distances, here_ref, wave_ref, next_ref, templates_ref, *rest):
    planes = len(distances)
    if len(rest) > 5:
        flags_ref, events_ref, keep_ref, send_ref, note_ref, held, sliding, arrival = rest
    else:
        keep_ref, send_ref, held, sliding, arrival = rest
    group = keep_ref.shape[1] - EXTRA
    plane, core, around = here_ref[0], here_ref[1], here_ref[3]

    def copy(i, half):
        chip = lax.rem(plane + distances[i], around)
        first = (chip * 2 + (1 - core if half == 0 else core)) * group
        return pltpu.make_async_copy(
            templates_ref.at[pl.ds(first, group)], held.at[i, half], arrival.at[i, half]
        )

    for i in range(planes):
        for half in range(2):
            copy(i, half).start()
    segment = jnp.concatenate([wave_ref[...], next_ref[...]], axis=1).astype(f32)
    build(segment, sliding)
    energy = energy_of(segment)
    if len(rest) > 5:
        fill = jnp.zeros((2, LANES - events_ref.shape[1]), jnp.int32)
        events = jnp.concatenate([events_ref[...], fill], axis=1)
        count = jnp.sum(flags_ref[...], axis=1, keepdims=True)
        lane = lax.broadcasted_iota(jnp.int32, (1, LANES), 1)
        note = events[0:1] + pltpu.roll(events, events_ref.shape[1], 1)[1:2]
        note = jnp.where(lane == LANES - 1, count, note)
        note_ref[...] = jnp.broadcast_to(note[None], note_ref.shape)
    for i in range(planes):
        for half, out_ref in enumerate((send_ref, keep_ref)):
            copy(i, half).wait()
            filters = held[i, half].reshape(group, -1)
            out_ref[i, :group] = jnp.dot(filters, sliding[...], preferred_element_type=f32)
            out_ref[i, group:] = energy


def merge(keep_ref, came_ref, *sum_refs):
    for i, sum_ref in enumerate(sum_refs):
        sum_ref[...] = keep_ref[i] + came_ref[i]


def three(values):
    high = values.astype(bf16)
    rest = values - high.astype(f32)
    middle = rest.astype(bf16)
    low = (rest - middle.astype(f32)).astype(bf16)
    return high, middle, low


def pick(selector, parts):
    high, middle, low = [jnp.dot(selector, part, preferred_element_type=f32) for part in parts]
    return high + (middle + low)


def finish(place_ref, a_ref, b_ref, c_ref, d_ref, e_ref, flags_ref, info_ref, stack_ref, windows_ref):
    group = stack_ref.shape[0]
    total = (a_ref[...] + b_ref[...]) + (c_ref[...] + d_ref[...]) + e_ref[...]
    stack = total[:group] / jnp.sqrt(total[group : group + 1] + epsilon)
    stack_ref[...] = stack
    info = info_ref[:, 0, :]
    devices = info.shape[0]
    rows = lax.broadcasted_iota(jnp.int32, info.shape, 0)
    lanes = lax.broadcasted_iota(jnp.int32, info.shape, 1)
    counted = lanes == LANES - 1
    here = place_ref[2]
    start = jnp.sum(jnp.where(counted & (rows < here), info, 0))
    found = jnp.sum(jnp.where(counted & (rows == here), info, 0))
    mine = (info >= start) & (info < start + found) & (lanes < 32)
    rank = jnp.sum(jnp.where(mine, info - start + 1, 0), axis=1, keepdims=True) - 1
    flags = jnp.broadcast_to(flags_ref[...], (8, group)).astype(f32)
    earlier = lax.broadcasted_iota(jnp.int32, (group, group), 0) < lax.broadcasted_iota(
        jnp.int32, (group, group), 1
    )
    before = jnp.dot(flags.astype(bf16), earlier.astype(f32).astype(bf16), preferred_element_type=f32)
    before = jnp.where(flags > 0.5, before, -2.0)
    selector = jnp.broadcast_to(before[:1], (devices, group)) == rank.astype(f32)
    windows = pick(selector.astype(f32).astype(bf16), three(stack))
    windows_ref[:, 0, :] = windows


def cross(lags_ref, events_ref, info_ref, received_ref, out_ref, turned, products):
    info = info_ref[:, 0, :]
    devices = info.shape[0]
    pairs = out_ref.shape[0]
    rows = lax.broadcasted_iota(jnp.int32, (devices, devices), 0)
    columns = lax.broadcasted_iota(jnp.int32, (devices, devices), 1)
    counts = jnp.broadcast_to(info[:, LANES - 1 :], (devices, devices))
    starts = jnp.sum(jnp.where(rows < columns, counts, 0), axis=0, keepdims=True)
    ends = jnp.sum(jnp.where(rows <= columns, counts, 0), axis=0, keepdims=True)
    square = lax.broadcasted_iota(jnp.int32, (pairs, pairs), 0) == lax.broadcasted_iota(
        jnp.int32, (pairs, pairs), 1
    )
    both = jnp.concatenate(
        [
            jnp.sum(jnp.where(square, events_ref[i : i + 1], 0), axis=1, keepdims=True)
            for i in range(2)
        ],
        axis=0,
    )
    selector = (starts <= both) & (both < ends)
    picked = pick(selector.astype(f32).astype(bf16), three(received_ref[:, 0, :]))
    first, second = picked[:pairs], picked[pairs:]
    length = 2 * BLK
    nothing = jnp.zeros((pairs, BLK), f32)
    ahead = jnp.concatenate([first, nothing], axis=1)
    behind = jnp.concatenate([second, nothing], axis=1)

    def near(values):
        return jnp.concatenate([values[:, length - NLAG :], values[:, :BLK]], axis=1)

    for u in range(NLAG // 8):
        turned[u] = near(behind if u == 0 else left(behind, 8 * u))
    for p in range(pairs):
        shift = lax.rem(lags_ref[p] + length, length)
        moved = pltpu.roll(jnp.broadcast_to(ahead[p : p + 1], (8, length)), shift, 1)
        moved = near(pltpu.roll(moved, 0, 1, stride=1, stride_axis=0))
        for u in range(NLAG // 8):
            product = moved * turned[u, pl.ds(p, 1), :]
            part = product[:, :LANES]
            for k in range(LANES, NLAG + BLK, LANES):
                part = part + product[:, k : k + LANES]
            products[pl.ds(p * NLAG + 8 * u, 8), :] = part
    ones = jnp.ones((8, LANES), bf16)
    high, middle, low = [
        lax.dot_general(ones, part, (((1,), (1,)), ((), ())), preferred_element_type=f32)
        for part in three(products[...])
    ]
    raw = high + (middle + low)
    raw = jnp.concatenate([raw[:1, p * NLAG : (p + 1) * NLAG] for p in range(pairs)], axis=0)
    power_one = jnp.mean(first * first, axis=1, keepdims=True)
    power_two = jnp.mean(second * second, axis=1, keepdims=True)
    out_ref[...] = raw / jnp.sqrt(BLK * (power_one + epsilon) * (power_two + epsilon))


def shards(waveforms, templates, detection_flags, pair_events, pair_lags):
    across = lax.axis_size("sta")
    ahead = lax.axis_size("tm")
    devices = across * ahead
    group = detection_flags.shape[0]
    station_group = lax.axis_index("sta")
    place = lax.axis_index("tm") * across + station_group
    plane, core = station_group // 2, station_group % 2
    planes = across // 2

    following = lax.ppermute(waveforms, "tm", [(i, i - 1) for i in range(1, ahead)])

    here = jnp.stack([plane, core, place, planes]).astype(jnp.int32)
    flags = detection_flags.reshape(1, group)
    events = pair_events.T

    def partial(distances, here, *others):
        count = len(distances)
        shape = jax.ShapeDtypeStruct((count, group + EXTRA, BLK), f32)
        stations = templates.shape[1]
        note = (jax.ShapeDtypeStruct((devices, 1, LANES), jnp.int32),) if others else ()
        return pl.pallas_call(
            functools.partial(correlate, distances),
            out_shape=(shape, shape) + note,
            in_specs=[SMEM, VMEM, VMEM, pl.BlockSpec(memory_space=pltpu.HBM)] + [VMEM] * len(others),
            out_specs=(VMEM, VMEM) + (VMEM,) * len(note),
            scratch_shapes=[
                pltpu.VMEM((count, 2, group, stations, TLEN), bf16),
                pltpu.VMEM((stations * TLEN, BLK), bf16),
                pltpu.SemaphoreType.DMA((count, 2)),
            ],
            compiler_params=pltpu.CompilerParams(vmem_limit_bytes=52 << 20),
            cost_estimate=pl.CostEstimate(
                flops=count * 4 * group * stations * TLEN * BLK,
                bytes_accessed=count * 4 * group * stations * TLEN,
                transcendentals=0,
            ),
        )(here, waveforms, following, templates, *others)

    def over(distance, values):
        return lax.ppermute(values, "sta", [(i, (i + 2 * distance) % across) for i in range(across)])

    def swap(values):
        return lax.ppermute(values, "sta", [(i, i ^ 1) for i in range(across)])

    away = (2, 1, 3)
    keeps, sends, note = partial(away, here, flags, events)
    cames = swap(sends)
    later, _ = lax.optimization_barrier((here, keeps))
    keep, send = partial((0,), later)
    came = swap(send)
    shape = jax.ShapeDtypeStruct(keep.shape[1:], f32)
    cames, _ = lax.optimization_barrier((cames, keep))
    sums = whole(merge, (shape,) * len(away), 1 << 20, keeps, cames)
    arrived = [over(distance, values) for distance, values in zip(away, sums)]

    note, _ = lax.optimization_barrier((note, sums))
    info = lax.all_to_all(note, BOTH, 0, 0, tiled=True)

    network_stack, windows = whole(
        finish,
        (
            jax.ShapeDtypeStruct((group, BLK), f32),
            jax.ShapeDtypeStruct((devices, 1, BLK), f32),
        ),
        1 << 24,
        here,
        keep[0],
        came[0],
        *arrived,
        flags,
        info,
        smem=1,
    )
    received = lax.all_to_all(windows, BOTH, 0, 0, tiled=True)
    pairs = pair_events.shape[0]
    pair_cc = whole(
        cross,
        jax.ShapeDtypeStruct((pairs, NLAG), f32),
        1 << 24,
        pair_lags,
        events,
        info,
        received,
        smem=1,
        scratch=[
            pltpu.VMEM((NLAG // 8, pairs, NLAG + BLK), f32),
            pltpu.VMEM((pairs * NLAG, LANES), f32),
        ],
    )
    return (network_stack, pair_cc)


def solution(mesh):
    return jax.shard_map(
        shards,
        mesh=mesh,
        in_specs=(
            P("sta", "tm"),
            P(None, "sta", None),
            P("sta", "tm"),
            P(("tm", "sta"), None),
            P(("tm", "sta")),
        ),
        out_specs=(P("sta", "tm"), P(("tm", "sta"), None)),
        check_vma=False,
    )
```

time: 119 us -> 86.4 us (0.73)
  Pallas kernels: 56.6 us -> 24.5 us
  other arithmetic: 3.48 us -> 0.08 us
  waiting for transfers between devices: 14.7 us -> 17.5 us
  blocking collectives: 20 us -> 21.6 us
    pallas_call x7 -> x3, Pallas kernels: 56.6 us -> 7.3 us  [whole(): pl.pallas_call(kernel, out_shape=outs, in_specs=[SMEM] * smem + [VMEM] *...]
    pallas_call x0 -> x2, Pallas kernels: none -> 17.2 us  [partial(): pl.pallas_call(functools.partial(correlate, distances), out_shape=(shape,...]
    another operation x3 -> x1, other arithmetic: 1.88 us -> 0.08 us  [shards(): here = jnp.stack([plane, core, place, planes]).astype(jnp.int32)]
    all_to_all x1, starting transfers between devices: 11.3 us -> 9.67 us  [shards(): info = lax.all_to_all(note, BOTH, 0, 0, tiled=True)]
    all_to_all x1, blocking collectives: 20 us -> 21.6 us  [shards(): received = lax.all_to_all(windows, BOTH, 0, 0, tiled=True)]
    all_to_all x1, waiting for transfers between devices: 12.2 us -> 13.7 us  [shards(): info = lax.all_to_all(note, BOTH, 0, 0, tiled=True)]
    ppermute x1, waiting for transfers between devices: 2.51 us -> 3.8 us  [shards(): lax.ppermute(waveforms, 'tm', [(i, i - 1) for i in range(1, ahead)])]
    ppermute x7 -> x5, starting transfers between devices: 8.16 us -> 8.71 us  [the longest x3 6.37 us: over(): lax.ppermute(values, 'sta', [(i, (i + 2 * distance) % across) for i in ra...]
  transfers between devices with their start and end apart: 9 -> 7, of which waited for: 2 -> 2; matrix products, arithmetic and copies ran while one was open for 4% -> 0% of each run, Pallas kernels for 27% -> 8%
where the time goes in v2:
time: 86.4 us; the launch traced here: 86.2 us
  Pallas kernels  24.5 us (28%)
  blocking collectives  21.6 us (25%)
  starting transfers between devices  19.7 us (23%)
  waiting for transfers between devices  17.5 us (20%)
  local copies, waits for them, and re-layouts  2.07 us (2%)
    all_to_all x1, blocking collectives, shards(): received = lax.all_to_all(windows, BOTH, 0, 0, tiled=True)  21.6 us
    pallas_call x2, Pallas kernels, partial(): pl.pallas_call(functools.partial(correlate, distances), out_shape=(shape,...  17.2 us
    all_to_all x1, waiting for transfers between devices, shards(): info = lax.all_to_all(note, BOTH, 0, 0, tiled=True)  13.7 us
    all_to_all x1, starting transfers between devices, shards(): info = lax.all_to_all(note, BOTH, 0, 0, tiled=True)  9.67 us
    pallas_call x3, Pallas kernels, whole(): pl.pallas_call(kernel, out_shape=outs, in_specs=[SMEM] * smem + [VMEM] *...  7.3 us
    ppermute x3, starting transfers between devices, over(): lax.ppermute(values, 'sta', [(i, (i + 2 * distance) % across) for i in ra...  6.37 us
    ppermute x1, waiting for transfers between devices, shards(): lax.ppermute(waveforms, 'tm', [(i, i - 1) for i in range(1, ahead)])  3.8 us
    ppermute x2, starting transfers between devices, swap(): return lax.ppermute(values, 'sta', [(i, i ^ 1) for i in range(across)])  2.34 us
  transfers between devices with their start and end apart: 7, of which 2 were waited for; matrix products, arithmetic and copies ran while one was open for 0% of the time, Pallas kernels for 8%

profile of v2, /device:TPU:1, one launch (start us, length us, event | category | flops | bytes accessed | tf_op | source)
XLA Modules:
  0.0 86.2 jit_solution(10826449636158683185)
XLA Ops:
  0.6 1.3 %collective-permute-start = (bf16[8,512]{1,0:T(8,128)(2,1)}, bf16[8,512]{1,0:T(8,128)(2,1)S(1)}, u32[]{:S(2)}, u32[]{:S(2)}) collective-permute-start(bf16[8,512]{1,0:T(8,128)(2,1)} %wave_ref.3), channel_id=1, source_target_pairs={{8,0},{16,8},{24,16},{32,24},{40,32},{48,40},{56,48},{64,56},{72,6... | collective-permute-start | bytes 24584 | tf_op jit(solution)/shard_map/ppermute | solution.py:208
  1.9 0.1 pad_add_fusion.here_ref.place_ref
  2.0 3.8 %collective-permute-done.next_ref = bf16[8,512]{1,0:T(8,128)(2,1)S(1)} collective-permute-done((bf16[8,512]{1,0:T(8,128)(2,1)}, bf16[8,512]{1,0:T(8,128)(2,1)S(1)}, u32[]{:S(2)}, u32[]{:S(2)}) %collective-permute-start) | collective-permute-done | bytes 8224 | tf_op jit(solution)/shard_map/ppermute | solution.py:208
  5.8 0.0 copy-start
  5.8 0.7 copy-done
  6.5 0.0 copy-start.1
  6.5 0.7 copy-done.1
  7.2 0.0 copy-start.3
  7.2 0.7 copy-done.3
  7.9 11.6 %shard_map.68 = (f32[3,264,512]{2,1,0:T(8,128)S(1)}, f32[3,264,512]{2,1,0:T(8,128)}, s32[128,1,128]{2,1,0:T(1,128)}) custom-call(s32[4]{0:T(128)S(1)} %pad_add_fusion.here_ref.place_ref, bf16[8,512]{1,0:T(8,128)(2,1)S(1)} %copy-done, bf16[8,512]{1,0:T(8,128)(2,1)S(1)} %collective-permute-done.next_ref, bf16[2048,8,512]{2,1,0:T(8,128)(2,1)} %templates_ref.3, ...), custom_call_target="tpu_custom_call" | custom-call | flops 6442450944 | bytes 12582912 | tf_op jit(solution)/shard_map/pallas_call | solution.py:219
  19.5 2.2 %collective-permute-start.2 = (f32[3,264,512]{2,1,0:T(8,128)}, f32[3,264,512]{2,1,0:T(8,128)S(1)}, u32[]{:S(2)}, u32[]{:S(2)}) collective-permute-start(f32[3,264,512]{2,1,0:T(8,128)} %get-tuple-element.19), channel_id=1, source_target_pairs={{0,1},{1,0},{2,3},{3,2},{4,5},{5,4},{6,7},{7,6},{8,9},{9,8},{10,11... | collective-permute-start | bytes 4866056 | tf_op jit(solution)/shard_map/ppermute | solution.py:241
  21.7 5.6 %shard_map.69 = (f32[1,264,512]{2,1,0:T(8,128)S(1)}, f32[1,264,512]{2,1,0:T(8,128)}) custom-call(s32[4]{0:T(128)S(1)} %pad_add_fusion.here_ref.place_ref, bf16[8,512]{1,0:T(8,128)(2,1)S(1)} %copy-done, bf16[8,512]{1,0:T(8,128)(2,1)S(1)} %collective-permute-done.next_ref, bf16[2048,8,512]{2,1,0:T(8,128)(2,1)} %templates_ref.3), custom_call_target="tpu_custom_call" | custom-call | flops 2147483648 | bytes 4194304 | tf_op jit(solution)/shard_map/pallas_call | solution.py:219
  27.3 0.1 collective-permute-start.1
  27.4 0.0 collective-permute-done.2.came_ref
  27.4 0.0 copy-start.2
  27.4 1.2 %shard_map.70 = (f32[264,512]{1,0:T(8,128)}, f32[264,512]{1,0:T(8,128)}, f32[264,512]{1,0:T(8,128)S(1)}) custom-call(f32[3,264,512]{2,1,0:T(8,128)S(1)} %get-tuple-element.15.keep_ref, f32[3,264,512]{2,1,0:T(8,128)S(1)} %collective-permute-done.2.came_ref), custom_call_target="tpu_custom_call" | custom-call | flops 1048576 | bytes 1048576 | tf_op jit(solution)/shard_map/pallas_call | solution.py:24
  28.6 3.7 %collective-permute-start.3 = (f32[264,512]{1,0:T(8,128)}, f32[264,512]{1,0:T(8,128)S(1)}, u32[]{:S(2)}, u32[]{:S(2)}) collective-permute-start(f32[264,512]{1,0:T(8,128)} %get-tuple-element.21), channel_id=1, source_target_pairs={{0,4},{1,5},{2,6},{3,7},{4,0},{5,1},{6,2},{7,3},{8,12},{9,13},{10,... | collective-permute-start | bytes 1622024 | tf_op jit(solution)/shard_map/ppermute | solution.py:238
  32.3 0.7 collective-permute-start.4
  33.0 1.9 %collective-permute-start.5 = (f32[264,512]{1,0:T(8,128)S(1)}, f32[264,512]{1,0:T(8,128)S(1)}, u32[]{:S(2)}, u32[]{:S(2)}) collective-permute-start(f32[264,512]{1,0:T(8,128)S(1)} %get-tuple-element.23), channel_id=1, source_target_pairs={{0,6},{1,7},{2,0},{3,1},{4,2},{5,3},{6,4},{7,5},{8,14},{9,15},{10,... | collective-permute-start | bytes 1622024 | tf_op jit(solution)/shard_map/ppermute | solution.py:238
  35.0 9.7 %all-to-all-start = ((s32[128,1,128]{2,1,0:T(1,128)}), s32[128,1,128]{2,1,0:T(1,128)S(1)}, u32[]{:S(2)}, u32[]{:S(2)}) async-start(s32[128,1,128]{2,1,0:T(1,128)} %get-tuple-element.25), calls=%async_computation | async-start | bytes 131072 | tf_op jit(solution)/shard_map/all_to_all | solution.py:255
  44.6 0.0 collective-permute-done.1
  44.6 13.7 %all-to-all-done.info_ref = s32[128,1,128]{2,1,0:T(1,128)S(1)} async-done(((s32[128,1,128]{2,1,0:T(1,128)}), s32[128,1,128]{2,1,0:T(1,128)S(1)}, u32[]{:S(2)}, u32[]{:S(2)}) %all-to-all-start) | async-done | bytes 65568 | tf_op jit(solution)/shard_map/all_to_all | solution.py:255
  58.4 0.0 collective-permute-done.3.c_ref
  58.4 0.0 collective-permute-done.4.d_ref
  58.4 0.0 collective-permute-done.5.e_ref
  58.4 0.0 copy-done.2
  58.4 0.0 copy-start.4
  58.4 0.0 copy-start.5
  58.4 1.9 %shard_map.71 = (f32[256,512]{1,0:T(8,128)}, f32[128,1,512]{2,1,0:T(1,128)S(1)}) custom-call(s32[4]{0:T(128)S(1)} %pad_add_fusion.here_ref.place_ref, f32[264,512]{1,0:T(8,128)S(1)} %bitcast.7, f32[264,512]{1,0:T(8,128)S(1)} %bitcast.8, f32[264,512]{1,0:T(8,128)S(1)} %collective-permute-done.3.c_ref, f32[264,512]{1,0:T(8,128)S(1)} %collective-permute-done.4.d_ref, ...), custom_call_target="tpu_custom_call" | custom-call | flops 16777216 | bytes 1048576 | tf_op jit(solution)/shard_map/pallas_call | solution.py:24
  60.3 21.6 %all_to_all.10.received_ref = f32[128,1,512]{2,1,0:T(1,128)S(1)} all-to-all(f32[128,1,512]{2,1,0:T(1,128)S(1)} %get-tuple-element.27), channel_id=1, replica_groups=mesh['tm'=16,'sta'=8] {'tm','sta'}, dimensions={0} | all-to-all | bytes 524288 | tf_op jit(solution)/shard_map/all_to_all | solution.py:272
  81.9 0.0 copy-done.4
  81.9 0.0 copy-done.5
  81.9 4.2 %shard_map.72 = f32[16,128]{1,0:T(8,128)} custom-call(s32[16]{0:T(128)S(1)} %copy-done.5, s32[2,16]{1,0:T(2,128)S(1)} %bitcast.12, s32[128,1,128]{2,1,0:T(1,128)S(1)} %all-to-all-done.info_ref, f32[128,1,512]{2,1,0:T(1,128)S(1)} %all_to_all.10.received_ref), custom_call_target="tpu_custom_call" | custom-call | flops 16777216 | bytes 1048576 | tf_op jit(solution)/shard_map/pallas_call | solution.py:24
Async XLA Ops:
  0.6 5.2 %collective-permute-start = (bf16[8,512]{1,0:T(8,128)(2,1)}, bf16[8,512]{1,0:T(8,128)(2,1)S(1)}, u32[]{:S(2)}, u32[]{:S(2)}) collective-permute-start(bf16[8,512]{1,0:T(8,128)(2,1)} %wave_ref.3), channel_id=1, source_target_pairs={{8,0},{16,8},{24,16},{32,24},{40,32},{48,40},{56,48},{64,56},{72,6... | collective-permute-start | bytes 24584 | tf_op jit(solution)/shard_map/ppermute | solution.py:208
  5.8 0.7 copy-start
  6.5 0.7 copy-start.1
  7.2 0.7 copy-start.3
  19.5 8.0 %collective-permute-start.2 = (f32[3,264,512]{2,1,0:T(8,128)}, f32[3,264,512]{2,1,0:T(8,128)S(1)}, u32[]{:S(2)}, u32[]{:S(2)}) collective-permute-start(f32[3,264,512]{2,1,0:T(8,128)} %get-tuple-element.19), channel_id=1, source_target_pairs={{0,1},{1,0},{2,3},{3,2},{4,5},{5,4},{6,7},{7,6},{8,9},{9,8},{10,11... | collective-permute-start | bytes 4866056 | tf_op jit(solution)/shard_map/ppermute | solution.py:241
  27.3 17.3 %collective-permute-start.1 = (f32[1,264,512]{2,1,0:T(8,128)}, f32[1,264,512]{2,1,0:T(8,128)S(1)}, u32[]{:S(2)}, u32[]{:S(2)}) collective-permute-start(f32[1,264,512]{2,1,0:T(8,128)} %get-tuple-element.18), channel_id=1, source_target_pairs={{0,1},{1,0},{2,3},{3,2},{4,5},{5,4},{6,7},{7,6},{8,9},{9,8},{10,11... | collective-permute-start | bytes 1622024 | tf_op jit(solution)/shard_map/ppermute | solution.py:241
  27.4 30.9 %copy-start.2 = (s32[256,1]{0,1:T(1,128)S(1)}, s32[256,1]{0,1:T(1,128)}, u32[]{:S(2)}) copy-start(s32[256,1]{0,1:T(1,128)} %param.7) | copy-start | bytes 3076
  28.6 29.8 %collective-permute-start.3 = (f32[264,512]{1,0:T(8,128)}, f32[264,512]{1,0:T(8,128)S(1)}, u32[]{:S(2)}, u32[]{:S(2)}) collective-permute-start(f32[264,512]{1,0:T(8,128)} %get-tuple-element.21), channel_id=1, source_target_pairs={{0,4},{1,5},{2,6},{3,7},{4,0},{5,1},{6,2},{7,3},{8,12},{9,13},{10,... | collective-permute-start | bytes 1622024 | tf_op jit(solution)/shard_map/ppermute | solution.py:238
  32.3 26.1 %collective-permute-start.4 = (f32[264,512]{1,0:T(8,128)}, f32[264,512]{1,0:T(8,128)S(1)}, u32[]{:S(2)}, u32[]{:S(2)}) collective-permute-start(f32[264,512]{1,0:T(8,128)} %get-tuple-element.22), channel_id=1, source_target_pairs={{0,2},{1,3},{2,4},{3,5},{4,6},{5,7},{6,0},{7,1},{8,10},{9,11},{10,... | collective-permute-start | bytes 1622024 | tf_op jit(solution)/shard_map/ppermute | solution.py:238
  33.0 25.3 %collective-permute-start.5 = (f32[264,512]{1,0:T(8,128)S(1)}, f32[264,512]{1,0:T(8,128)S(1)}, u32[]{:S(2)}, u32[]{:S(2)}) collective-permute-start(f32[264,512]{1,0:T(8,128)S(1)} %get-tuple-element.23), channel_id=1, source_target_pairs={{0,6},{1,7},{2,0},{3,1},{4,2},{5,3},{6,4},{7,5},{8,14},{9,15},{10,... | collective-permute-start | bytes 1622024 | tf_op jit(solution)/shard_map/ppermute | solution.py:238
  35.0 23.4 %all-to-all-start = ((s32[128,1,128]{2,1,0:T(1,128)}), s32[128,1,128]{2,1,0:T(1,128)S(1)}, u32[]{:S(2)}, u32[]{:S(2)}) async-start(s32[128,1,128]{2,1,0:T(1,128)} %get-tuple-element.25), calls=%async_computation | async-start | bytes 131072 | tf_op jit(solution)/shard_map/all_to_all | solution.py:255
  58.4 23.5 %copy-start.4 = (s32[16,2]{0,1:T(2,128)S(1)}, s32[16,2]{0,1:T(2,128)}, u32[]{:S(2)}) copy-start(s32[16,2]{0,1:T(2,128)} %param.8) | copy-start | bytes 388
  58.4 23.5 %copy-start.5 = (s32[16]{0:T(128)S(1)}, s32[16]{0:T(128)}, u32[]{:S(2)}) copy-start(s32[16]{0:T(128)} %lags_ref.1) | copy-start | bytes 196

commit v3 on v2

--- a/solution.py
+++ b/solution.py
@@ -11,7 +11,7 @@
 TLEN = 512
 NLAG = 128
 LANES = 128
-EXTRA = 8
+STEPS = 32767.0
 epsilon = 1e-06
 BOTH = ("tm", "sta")
 VMEM = pl.BlockSpec(memory_space=pltpu.VMEM)
@@ -49,9 +49,18 @@
             sliding_ref[pl.ds(s * TLEN + k, LANES), :] = shifted[:, k : k + BLK]
 
 
-def energy_of(segment):
-    window = jnp.sum(segment * segment, axis=0, keepdims=True)
-    window = jnp.broadcast_to(window, (EXTRA, window.shape[1]))
+def announce(flags_ref, events_ref, note_ref):
+    fill = jnp.zeros((2, LANES - events_ref.shape[1]), jnp.int32)
+    events = jnp.concatenate([events_ref[...], fill], axis=1)
+    count = jnp.sum(flags_ref[...], axis=1, keepdims=True)
+    lane = lax.broadcasted_iota(jnp.int32, (1, LANES), 1)
+    words = events[0:1] + pltpu.roll(events, events_ref.shape[1], 1)[1:2]
+    words = jnp.where(lane == LANES - 1, count, words)
+    note_ref[...] = jnp.broadcast_to(words[None], note_ref.shape)
+
+
+def sums_of_window(squares):
+    window = jnp.broadcast_to(squares, (8, squares.shape[1]))
     width = 1
     while width < TLEN:
         window = window + left(window, width)
@@ -59,13 +68,9 @@
     return window[:, :BLK]
 
 
-def correlate(distances, here_ref, wave_ref, next_ref, templates_ref, *rest):
+def correlate(distances, here_ref, wave_ref, next_ref, templates_ref, keep_ref, send_ref, waves, held, sliding, arrival):
     planes = len(distances)
-    if len(rest) > 5:
-        flags_ref, events_ref, keep_ref, send_ref, note_ref, held, sliding, arrival = rest
-    else:
-        keep_ref, send_ref, held, sliding, arrival = rest
-    group = keep_ref.shape[1] - EXTRA
+    group = held.shape[2]
     plane, core, around = here_ref[0], here_ref[1], here_ref[3]
 
     def copy(i, half):
@@ -75,31 +80,76 @@
             templates_ref.at[pl.ds(first, group)], held.at[i, half], arrival.at[i, half]
         )
 
+    pieces = [
+        pltpu.make_async_copy(wave_ref, waves.at[0], arrival.at[planes, 0]),
+        pltpu.make_async_copy(next_ref, waves.at[1], arrival.at[planes, 1]),
+    ]
+    for piece in pieces:
+        piece.start()
     for i in range(planes):
         for half in range(2):
             copy(i, half).start()
-    segment = jnp.concatenate([wave_ref[...], next_ref[...]], axis=1).astype(f32)
+    for piece in pieces:
+        piece.wait()
+    segment = jnp.concatenate([waves[0], waves[1]], axis=1).astype(f32)
     build(segment, sliding)
-    energy = energy_of(segment)
-    if len(rest) > 5:
-        fill = jnp.zeros((2, LANES - events_ref.shape[1]), jnp.int32)
-        events = jnp.concatenate([events_ref[...], fill], axis=1)
-        count = jnp.sum(flags_ref[...], axis=1, keepdims=True)
-        lane = lax.broadcasted_iota(jnp.int32, (1, LANES), 1)
-        note = events[0:1] + pltpu.roll(events, events_ref.shape[1], 1)[1:2]
-        note = jnp.where(lane == LANES - 1, count, note)
-        note_ref[...] = jnp.broadcast_to(note[None], note_ref.shape)
+    if keep_ref.shape[0] > planes * group:
+        energy = sums_of_window(jnp.sum(segment * segment, axis=0, keepdims=True))
+        keep_ref[planes * group :] = energy
+        send_ref[planes * group :] = energy
     for i in range(planes):
         for half, out_ref in enumerate((send_ref, keep_ref)):
             copy(i, half).wait()
             filters = held[i, half].reshape(group, -1)
-            out_ref[i, :group] = jnp.dot(filters, sliding[...], preferred_element_type=f32)
-            out_ref[i, group:] = energy
-
-
-def merge(keep_ref, came_ref, *sum_refs):
-    for i, sum_ref in enumerate(sum_refs):
-        sum_ref[...] = keep_ref[i] + came_ref[i]
+            out_ref[i * group : (i + 1) * group] = jnp.dot(
+                filters, sliding[...], preferred_element_type=f32
+            )
+
+
+def diagonal(size):
+    rows = lax.broadcasted_iota(jnp.int32, (size, size), 0)
+    return rows == lax.broadcasted_iota(jnp.int32, (size, size), 1)
+
+
+def merge(keep_ref, came_ref, energy_ref, *code_refs):
+    half = code_refs[0].shape[0] - 8
+    group = 2 * half
+    square = diagonal(group)
+    last = len(code_refs) * group
+    energy = keep_ref[last:] + came_ref[last:]
+    energy_ref[...] = energy
+    logarithm = jnp.log2(jnp.maximum(energy, 1e-30))
+    sample = jnp.round(4.0 * logarithm)
+    level = jnp.exp2(sample[:1] * -0.125)
+    power = jnp.floor(logarithm)
+    bits = jnp.round(energy * jnp.exp2(23.0 - power))
+    row = lax.broadcasted_iota(jnp.int32, (8, BLK), 0)
+    below = jnp.where(row == 1, sample, jnp.where(row == 2, power, bits)).astype(jnp.int32)
+    for i, code_ref in enumerate(code_refs):
+        here = slice(i * group, (i + 1) * group)
+        values = (keep_ref[here] + came_ref[here]) * level
+        largest = jnp.max(jnp.abs(values), axis=1, keepdims=True)
+        exponent = jnp.floor(8.0 * jnp.log2(jnp.maximum(largest, 1e-30)) + 0.01) + 1.0
+        codes = jnp.round(values * (STEPS * jnp.exp2(exponent * -0.125))).astype(jnp.int32)
+        code_ref[:half] = (codes[:half] & 0xFFFF) | lax.shift_left(codes[half:], 16)
+        exponents = jnp.sum(jnp.where(square, exponent, 0.0), axis=0, keepdims=True)
+        exponents = jnp.broadcast_to(exponents.astype(jnp.int32), (8, group))
+        exponents = jnp.concatenate([exponents] * (BLK // group), axis=1)
+        code_ref[half:] = jnp.where(row == 0, exponents, below)
+
+
+def decode(code_ref, square):
+    half = code_ref.shape[0] - 8
+    words = code_ref[:half]
+    codes = jnp.concatenate(
+        [lax.shift_right_arithmetic(lax.shift_left(words, 16), 16), lax.shift_right_arithmetic(words, 16)],
+        axis=0,
+    )
+    below = code_ref[half:].astype(f32)
+    exponent = jnp.sum(jnp.where(square, below[:1, : 2 * half], 0.0), axis=1, keepdims=True)
+    level = jnp.exp2(below[1:2] * 0.125)
+    energy = below[3:4] * jnp.exp2(below[2:3] - 23.0)
+    return codes.astype(f32) * (jnp.exp2(exponent * 0.125) * (1.0 / STEPS)) * level, energy
 
 
 def three(values):
@@ -115,17 +165,23 @@
     return high + (middle + low)
 
 
-def finish(place_ref, a_ref, b_ref, c_ref, d_ref, e_ref, flags_ref, info_ref, stack_ref, windows_ref):
+def finish(here_ref, keep_ref, came_ref, energy_ref, a_ref, b_ref, c_ref, flags_ref, info_ref, stack_ref, windows_ref):
     group = stack_ref.shape[0]
-    total = (a_ref[...] + b_ref[...]) + (c_ref[...] + d_ref[...]) + e_ref[...]
-    stack = total[:group] / jnp.sqrt(total[group : group + 1] + epsilon)
+    square = diagonal(group)
+    stack = keep_ref[...] + came_ref[...]
+    energy = energy_ref[:1]
+    for code_ref in (a_ref, b_ref, c_ref):
+        values, more = decode(code_ref, square)
+        stack = stack + values
+        energy = energy + more
+    stack = stack * (1.0 / jnp.sqrt(energy + epsilon))
     stack_ref[...] = stack
     info = info_ref[:, 0, :]
     devices = info.shape[0]
     rows = lax.broadcasted_iota(jnp.int32, info.shape, 0)
     lanes = lax.broadcasted_iota(jnp.int32, info.shape, 1)
     counted = lanes == LANES - 1
-    here = place_ref[2]
+    here = here_ref[2]
     start = jnp.sum(jnp.where(counted & (rows < here), info, 0))
     found = jnp.sum(jnp.where(counted & (rows == here), info, 0))
     mine = (info >= start) & (info < start + found) & (lanes < 32)
@@ -150,9 +206,7 @@
     counts = jnp.broadcast_to(info[:, LANES - 1 :], (devices, devices))
     starts = jnp.sum(jnp.where(rows < columns, counts, 0), axis=0, keepdims=True)
     ends = jnp.sum(jnp.where(rows <= columns, counts, 0), axis=0, keepdims=True)
-    square = lax.broadcasted_iota(jnp.int32, (pairs, pairs), 0) == lax.broadcasted_iota(
-        jnp.int32, (pairs, pairs), 1
-    )
+    square = diagonal(pairs)
     both = jnp.concatenate(
         [
             jnp.sum(jnp.where(square, events_ref[i : i + 1], 0), axis=1, keepdims=True)
@@ -211,28 +265,28 @@
     flags = detection_flags.reshape(1, group)
     events = pair_events.T
 
-    def partial(distances, here, *others):
+    def partial(distances, here, below):
         count = len(distances)
-        shape = jax.ShapeDtypeStruct((count, group + EXTRA, BLK), f32)
+        shape = pltpu.VMEM((count * group + below, BLK), f32)
         stations = templates.shape[1]
-        note = (jax.ShapeDtypeStruct((devices, 1, LANES), jnp.int32),) if others else ()
         return pl.pallas_call(
             functools.partial(correlate, distances),
-            out_shape=(shape, shape) + note,
-            in_specs=[SMEM, VMEM, VMEM, pl.BlockSpec(memory_space=pltpu.HBM)] + [VMEM] * len(others),
-            out_specs=(VMEM, VMEM) + (VMEM,) * len(note),
+            out_shape=(shape, shape),
+            in_specs=[SMEM] + [pl.BlockSpec(memory_space=pl.ANY)] * 2 + [pl.BlockSpec(memory_space=pltpu.HBM)],
+            out_specs=(VMEM, VMEM),
             scratch_shapes=[
+                pltpu.VMEM((2, stations, BLK), bf16),
                 pltpu.VMEM((count, 2, group, stations, TLEN), bf16),
                 pltpu.VMEM((stations * TLEN, BLK), bf16),
-                pltpu.SemaphoreType.DMA((count, 2)),
+                pltpu.SemaphoreType.DMA((count + 1, 2)),
             ],
-            compiler_params=pltpu.CompilerParams(vmem_limit_bytes=52 << 20),
+            compiler_params=pltpu.CompilerParams(vmem_limit_bytes=48 << 20),
             cost_estimate=pl.CostEstimate(
                 flops=count * 4 * group * stations * TLEN * BLK,
                 bytes_accessed=count * 4 * group * stations * TLEN,
                 transcendentals=0,
             ),
-        )(here, waveforms, following, templates, *others)
+        )(here, waveforms, following, templates)
 
     def over(distance, values):
         return lax.ppermute(values, "sta", [(i, (i + 2 * distance) % across) for i in range(across)])
@@ -241,17 +295,20 @@
         return lax.ppermute(values, "sta", [(i, i ^ 1) for i in range(across)])
 
     away = (2, 1, 3)
-    keeps, sends, note = partial(away, here, flags, events)
+    keeps, sends = partial(away, here, 8)
     cames = swap(sends)
     later, _ = lax.optimization_barrier((here, keeps))
-    keep, send = partial((0,), later)
+    keep, send = partial((0,), later, 0)
     came = swap(send)
-    shape = jax.ShapeDtypeStruct(keep.shape[1:], f32)
     cames, _ = lax.optimization_barrier((cames, keep))
-    sums = whole(merge, (shape,) * len(away), 1 << 20, keeps, cames)
-    arrived = [over(distance, values) for distance, values in zip(away, sums)]
-
-    note, _ = lax.optimization_barrier((note, sums))
+    shape = jax.ShapeDtypeStruct((group // 2 + 8, BLK), jnp.int32)
+    energy, *codes = whole(
+        merge, (jax.ShapeDtypeStruct((8, BLK), f32),) + (shape,) * len(away), 1 << 22, keeps, cames
+    )
+    arrived = [over(distance, values) for distance, values in zip(away, codes)]
+
+    note = whole(announce, jax.ShapeDtypeStruct((devices, 1, LANES), jnp.int32), 1 << 20, flags, events)
+    note, _ = lax.optimization_barrier((note, codes))
     info = lax.all_to_all(note, BOTH, 0, 0, tiled=True)
 
     network_stack, windows = whole(
@@ -262,8 +319,9 @@
         ),
         1 << 24,
         here,
-        keep[0],
-        came[0],
+        keep,
+        came,
+        energy,
         *arrived,
         flags,
         info,

time: 86.4 us -> 73.1 us (0.85)
  blocking collectives: 21.6 us -> 15.3 us
  waiting for transfers between devices: 17.5 us -> 13.1 us
  local copies, waits for them, and re-layouts: 2.07 us -> 0.72 us
  Pallas kernels: 24.5 us -> 23.2 us
    all_to_all x1, blocking collectives: 21.6 us -> 15.3 us  [shards(): received = lax.all_to_all(windows, BOTH, 0, 0, tiled=True)]
    all_to_all x1, waiting for transfers between devices: 13.7 us -> 9.32 us  [shards(): info = lax.all_to_all(note, BOTH, 0, 0, tiled=True)]
    pallas_call x2, Pallas kernels: 17.2 us -> 15.6 us  [partial(): pl.pallas_call(functools.partial(correlate, distances), out_shape=(shape,...]
    unnamed x12 -> x8, local copies, waits for them, and re-layouts: 2.07 us -> 0.72 us
    pallas_call x3 -> x4, Pallas kernels: 7.3 us -> 7.57 us  [whole(): pl.pallas_call(kernel, out_shape=outs, in_specs=[SMEM] * smem + [VMEM] *...]
  transfers between devices with their start and end apart: 7 -> 7, of which waited for: 2 -> 2; matrix products, arithmetic and copies ran while one was open for 0% -> 0% of each run, Pallas kernels for 8% -> 9%
where the time goes in v3:
time: 73.1 us; the launch traced here: 72.9 us
  Pallas kernels  23.2 us (32%)
  starting transfers between devices  19.7 us (27%)
  blocking collectives  15.3 us (21%)
  waiting for transfers between devices  13.1 us (18%)
  between operations  0.74 us (1%)
    pallas_call x2, Pallas kernels, partial(): pl.pallas_call(functools.partial(correlate, distances), out_shape=(shape,...  15.6 us
    all_to_all x1, blocking collectives, shards(): received = lax.all_to_all(windows, BOTH, 0, 0, tiled=True)  15.3 us
    all_to_all x1, starting transfers between devices, shards(): info = lax.all_to_all(note, BOTH, 0, 0, tiled=True)  9.68 us
    all_to_all x1, waiting for transfers between devices, shards(): info = lax.all_to_all(note, BOTH, 0, 0, tiled=True)  9.32 us
    pallas_call x4, Pallas kernels, whole(): pl.pallas_call(kernel, out_shape=outs, in_specs=[SMEM] * smem + [VMEM] *...  7.57 us
    ppermute x3, starting transfers between devices, over(): lax.ppermute(values, 'sta', [(i, (i + 2 * distance) % across) for i in ra...  6.44 us
    ppermute x1, waiting for transfers between devices, shards(): lax.ppermute(waveforms, 'tm', [(i, i - 1) for i in range(1, ahead)])  3.8 us
    ppermute x2, starting transfers between devices, swap(): return lax.ppermute(values, 'sta', [(i, i ^ 1) for i in range(across)])  2.33 us
  transfers between devices with their start and end apart: 7, of which 2 were waited for; matrix products, arithmetic and copies ran while one was open for 0% of the time, Pallas kernels for 9%

profile of v3, /device:TPU:1, one launch (start us, length us, event | category | flops | bytes accessed | tf_op | source)
XLA Modules:
  0.0 72.9 jit_solution(7192435088485178696)
XLA Ops:
  0.6 1.3 %collective-permute-start = (bf16[8,512]{1,0:T(8,128)(2,1)}, bf16[8,512]{1,0:T(8,128)(2,1)S(1)}, u32[]{:S(2)}, u32[]{:S(2)}) collective-permute-start(bf16[8,512]{1,0:T(8,128)(2,1)} %wave_ref.3), channel_id=1, source_target_pairs={{8,0},{16,8},{24,16},{32,24},{40,32},{48,40},{56,48},{64,56},{72,6... | collective-permute-start | bytes 24584 | tf_op jit(solution)/shard_map/ppermute | solution.py:262
  1.9 0.1 pad_add_fusion.here_ref
  2.0 3.8 %collective-permute-done.next_ref = bf16[8,512]{1,0:T(8,128)(2,1)S(1)} collective-permute-done((bf16[8,512]{1,0:T(8,128)(2,1)}, bf16[8,512]{1,0:T(8,128)(2,1)S(1)}, u32[]{:S(2)}, u32[]{:S(2)}) %collective-permute-start) | collective-permute-done | bytes 8224 | tf_op jit(solution)/shard_map/ppermute | solution.py:262
  5.8 0.0 copy-start
  5.8 0.7 copy-done
  6.5 10.6 %shard_map.68 = (f32[776,512]{1,0:T(8,128)S(1)}, f32[776,512]{1,0:T(8,128)S(1)}) custom-call(s32[4]{0:T(128)S(1)} %pad_add_fusion.here_ref, bf16[8,512]{1,0:T(8,128)(2,1)S(1)} %copy-done, bf16[8,512]{1,0:T(8,128)(2,1)S(1)} %collective-permute-done.next_ref, bf16[2048,8,512]{2,1,0:T(8,128)(2,1)} %templates_ref.3), custom_call_target="tpu_custom_call" | custom-call | flops 6442450944 | bytes 12582912 | tf_op jit(solution)/shard_map/pallas_call | solution.py:272
  17.1 2.1 %collective-permute-start.2 = (f32[776,512]{1,0:T(8,128)S(1)}, f32[776,512]{1,0:T(8,128)S(1)}, u32[]{:S(2)}, u32[]{:S(2)}) collective-permute-start(f32[776,512]{1,0:T(8,128)S(1)} %get-tuple-element.19), channel_id=1, source_target_pairs={{0,1},{1,0},{2,3},{3,2},{4,5},{5,4},{6,7},{7,6},{8,9},{9,8},{10,11... | collective-permute-start | bytes 4767752 | tf_op jit(solution)/shard_map/ppermute | solution.py:295
  19.2 5.0 %shard_map.69 = (f32[256,512]{1,0:T(8,128)S(1)}, f32[256,512]{1,0:T(8,128)S(1)}) custom-call(s32[4]{0:T(128)S(1)} %pad_add_fusion.here_ref, bf16[8,512]{1,0:T(8,128)(2,1)S(1)} %copy-done, bf16[8,512]{1,0:T(8,128)(2,1)S(1)} %collective-permute-done.next_ref, bf16[2048,8,512]{2,1,0:T(8,128)(2,1)} %templates_ref.3), custom_call_target="tpu_custom_call" | custom-call | flops 2147483648 | bytes 4194304 | tf_op jit(solution)/shard_map/pallas_call | solution.py:272
  24.2 0.3 collective-permute-start.1
  24.5 0.0 collective-permute-done.2.came_ref
  24.5 0.0 copy-start.1
  24.5 0.0 copy-start.2
  24.5 0.5 shard_map.70
  25.0 0.0 copy-start.3
  25.1 3.8 %collective-permute-start.3 = (s32[136,512]{1,0:T(8,128)S(1)}, s32[136,512]{1,0:T(8,128)S(1)}, u32[]{:S(2)}, u32[]{:S(2)}) collective-permute-start(s32[136,512]{1,0:T(8,128)S(1)} %get-tuple-element.22), channel_id=1, source_target_pairs={{0,4},{1,5},{2,6},{3,7},{4,0},{5,1},{6,2},{7,3},{8,12},{9,13},{10,... | collective-permute-start | bytes 835592 | tf_op jit(solution)/shard_map/ppermute | solution.py:292
  28.8 0.7 %collective-permute-start.4 = (s32[136,512]{1,0:T(8,128)S(1)}, s32[136,512]{1,0:T(8,128)S(1)}, u32[]{:S(2)}, u32[]{:S(2)}) collective-permute-start(s32[136,512]{1,0:T(8,128)S(1)} %get-tuple-element.23), channel_id=1, source_target_pairs={{0,2},{1,3},{2,4},{3,5},{4,6},{5,7},{6,0},{7,1},{8,10},{9,11},{10,... | collective-permute-start | bytes 835592 | tf_op jit(solution)/shard_map/ppermute | solution.py:292
  29.5 1.9 %collective-permute-start.5 = (s32[136,512]{1,0:T(8,128)S(1)}, s32[136,512]{1,0:T(8,128)S(1)}, u32[]{:S(2)}, u32[]{:S(2)}) collective-permute-start(s32[136,512]{1,0:T(8,128)S(1)} %get-tuple-element.24), channel_id=1, source_target_pairs={{0,6},{1,7},{2,0},{3,1},{4,2},{5,3},{6,4},{7,5},{8,14},{9,15},{10,... | collective-permute-start | bytes 835592 | tf_op jit(solution)/shard_map/ppermute | solution.py:292
  31.5 0.0 copy-done.1
  31.5 0.0 copy-done.2
  31.5 0.7 %shard_map.71 = s32[128,1,128]{2,1,0:T(1,128)} custom-call(s32[1,256]{1,0:T(1,128)S(1)} %bitcast.5, s32[2,16]{1,0:T(2,128)S(1)} %bitcast.7), custom_call_target="tpu_custom_call" | custom-call | flops 1048576 | bytes 1048576 | tf_op jit(solution)/shard_map/pallas_call | solution.py:24
  32.2 9.7 %all-to-all-start = ((s32[128,1,128]{2,1,0:T(1,128)}), s32[128,1,128]{2,1,0:T(1,128)S(1)}, u32[]{:S(2)}, u32[]{:S(2)}) async-start(s32[128,1,128]{2,1,0:T(1,128)} %shard_map.71), calls=%async_computation | async-start | bytes 131072 | tf_op jit(solution)/shard_map/all_to_all | solution.py:312
  41.9 0.0 collective-permute-done.1.came_ref
  41.9 9.3 %all-to-all-done.info_ref = s32[128,1,128]{2,1,0:T(1,128)S(1)} async-done(((s32[128,1,128]{2,1,0:T(1,128)}), s32[128,1,128]{2,1,0:T(1,128)S(1)}, u32[]{:S(2)}, u32[]{:S(2)}) %all-to-all-start) | async-done | bytes 65568 | tf_op jit(solution)/shard_map/all_to_all | solution.py:312
  51.3 0.0 collective-permute-done.3.a_ref
  51.3 0.0 collective-permute-done.4.b_ref
  51.3 0.0 collective-permute-done.5.c_ref
  51.3 2.1 %shard_map.72 = (f32[256,512]{1,0:T(8,128)}, f32[128,1,512]{2,1,0:T(1,128)S(1)}) custom-call(s32[4]{0:T(128)S(1)} %pad_add_fusion.here_ref, f32[256,512]{1,0:T(8,128)S(1)} %get-tuple-element.17.keep_ref, f32[256,512]{1,0:T(8,128)S(1)} %collective-permute-done.1.came_ref, f32[8,512]{1,0:T(8,128)S(1)} %get-tuple-element.21.energy_ref, ...), custom_call_target="tpu_custom_call" | custom-call | flops 16777216 | bytes 1048576 | tf_op jit(solution)/shard_map/pallas_call | solution.py:24
  53.3 15.3 %all_to_all.10.received_ref = f32[128,1,512]{2,1,0:T(1,128)S(1)} all-to-all(f32[128,1,512]{2,1,0:T(1,128)S(1)} %get-tuple-element.27), channel_id=1, replica_groups=mesh['tm'=16,'sta'=8] {'tm','sta'}, dimensions={0} | all-to-all | bytes 524288 | tf_op jit(solution)/shard_map/all_to_all | solution.py:330
  68.7 0.0 copy-done.3
  68.7 4.2 %shard_map.73 = f32[16,128]{1,0:T(8,128)} custom-call(s32[16]{0:T(128)S(1)} %copy-done.3, s32[2,16]{1,0:T(2,128)S(1)} %bitcast.8, s32[128,1,128]{2,1,0:T(1,128)S(1)} %all-to-all-done.info_ref, f32[128,1,512]{2,1,0:T(1,128)S(1)} %all_to_all.10.received_ref), custom_call_target="tpu_custom_call" | custom-call | flops 16777216 | bytes 1048576 | tf_op jit(solution)/shard_map/pallas_call | solution.py:24
Async XLA Ops:
  0.6 5.2 %collective-permute-start = (bf16[8,512]{1,0:T(8,128)(2,1)}, bf16[8,512]{1,0:T(8,128)(2,1)S(1)}, u32[]{:S(2)}, u32[]{:S(2)}) collective-permute-start(bf16[8,512]{1,0:T(8,128)(2,1)} %wave_ref.3), channel_id=1, source_target_pairs={{8,0},{16,8},{24,16},{32,24},{40,32},{48,40},{56,48},{64,56},{72,6... | collective-permute-start | bytes 24584 | tf_op jit(solution)/shard_map/ppermute | solution.py:262
  5.8 0.7 copy-start
  17.1 7.4 %collective-permute-start.2 = (f32[776,512]{1,0:T(8,128)S(1)}, f32[776,512]{1,0:T(8,128)S(1)}, u32[]{:S(2)}, u32[]{:S(2)}) collective-permute-start(f32[776,512]{1,0:T(8,128)S(1)} %get-tuple-element.19), channel_id=1, source_target_pairs={{0,1},{1,0},{2,3},{3,2},{4,5},{5,4},{6,7},{7,6},{8,9},{9,8},{10,11... | collective-permute-start | bytes 4767752 | tf_op jit(solution)/shard_map/ppermute | solution.py:295
  24.2 17.7 %collective-permute-start.1 = (f32[256,512]{1,0:T(8,128)S(1)}, f32[256,512]{1,0:T(8,128)S(1)}, u32[]{:S(2)}, u32[]{:S(2)}) collective-permute-start(f32[256,512]{1,0:T(8,128)S(1)} %get-tuple-element.18), channel_id=1, source_target_pairs={{0,1},{1,0},{2,3},{3,2},{4,5},{5,4},{6,7},{7,6},{8,9},{9,8},{10,11... | collective-permute-start | bytes 1572872 | tf_op jit(solution)/shard_map/ppermute | solution.py:295
  24.5 7.0 %copy-start.1 = (s32[256,1]{0,1:T(1,128)S(1)}, s32[256,1]{0,1:T(1,128)}, u32[]{:S(2)}) copy-start(s32[256,1]{0,1:T(1,128)} %param.7) | copy-start | bytes 3076
  24.5 7.0 %copy-start.2 = (s32[16,2]{0,1:T(2,128)S(1)}, s32[16,2]{0,1:T(2,128)}, u32[]{:S(2)}) copy-start(s32[16,2]{0,1:T(2,128)} %param.8) | copy-start | bytes 388
  25.0 43.6 %copy-start.3 = (s32[16]{0:T(128)S(1)}, s32[16]{0:T(128)}, u32[]{:S(2)}) copy-start(s32[16]{0:T(128)} %lags_ref.1) | copy-start | bytes 196
  25.1 26.2 %collective-permute-start.3 = (s32[136,512]{1,0:T(8,128)S(1)}, s32[136,512]{1,0:T(8,128)S(1)}, u32[]{:S(2)}, u32[]{:S(2)}) collective-permute-start(s32[136,512]{1,0:T(8,128)S(1)} %get-tuple-element.22), channel_id=1, source_target_pairs={{0,4},{1,5},{2,6},{3,7},{4,0},{5,1},{6,2},{7,3},{8,12},{9,13},{10,... | collective-permute-start | bytes 835592 | tf_op jit(solution)/shard_map/ppermute | solution.py:292
  28.8 22.5 %collective-permute-start.4 = (s32[136,512]{1,0:T(8,128)S(1)}, s32[136,512]{1,0:T(8,128)S(1)}, u32[]{:S(2)}, u32[]{:S(2)}) collective-permute-start(s32[136,512]{1,0:T(8,128)S(1)} %get-tuple-element.23), channel_id=1, source_target_pairs={{0,2},{1,3},{2,4},{3,5},{4,6},{5,7},{6,0},{7,1},{8,10},{9,11},{10,... | collective-permute-start | bytes 835592 | tf_op jit(solution)/shard_map/ppermute | solution.py:292
  29.5 21.7 %collective-permute-start.5 = (s32[136,512]{1,0:T(8,128)S(1)}, s32[136,512]{1,0:T(8,128)S(1)}, u32[]{:S(2)}, u32[]{:S(2)}) collective-permute-start(s32[136,512]{1,0:T(8,128)S(1)} %get-tuple-element.24), channel_id=1, source_target_pairs={{0,6},{1,7},{2,0},{3,1},{4,2},{5,3},{6,4},{7,5},{8,14},{9,15},{10,... | collective-permute-start | bytes 835592 | tf_op jit(solution)/shard_map/ppermute | solution.py:292
  32.2 19.0 %all-to-all-start = ((s32[128,1,128]{2,1,0:T(1,128)}), s32[128,1,128]{2,1,0:T(1,128)S(1)}, u32[]{:S(2)}, u32[]{:S(2)}) async-start(s32[128,1,128]{2,1,0:T(1,128)} %shard_map.71), calls=%async_computation | async-start | bytes 131072 | tf_op jit(solution)/shard_map/all_to_all | solution.py:312

commit v4 on v3

--- a/solution.py
+++ b/solution.py
@@ -11,9 +11,10 @@
 TLEN = 512
 NLAG = 128
 LANES = 128
+SLOT = 64
+WORDS = 4
 STEPS = 32767.0
 epsilon = 1e-06
-BOTH = ("tm", "sta")
 VMEM = pl.BlockSpec(memory_space=pltpu.VMEM)
 SMEM = pl.BlockSpec(memory_space=pltpu.SMEM)
 f32 = jnp.float32
@@ -49,14 +50,14 @@
             sliding_ref[pl.ds(s * TLEN + k, LANES), :] = shifted[:, k : k + BLK]
 
 
-def announce(flags_ref, events_ref, note_ref):
-    fill = jnp.zeros((2, LANES - events_ref.shape[1]), jnp.int32)
-    events = jnp.concatenate([events_ref[...], fill], axis=1)
-    count = jnp.sum(flags_ref[...], axis=1, keepdims=True)
-    lane = lax.broadcasted_iota(jnp.int32, (1, LANES), 1)
-    words = events[0:1] + pltpu.roll(events, events_ref.shape[1], 1)[1:2]
-    words = jnp.where(lane == LANES - 1, count, words)
-    note_ref[...] = jnp.broadcast_to(words[None], note_ref.shape)
+def announce(wave_ref, flags_ref, events_ref, words_ref, held_ref):
+    held_ref[...] = wave_ref[...]
+    fill = jnp.zeros((2, LANES - events_ref.shape[1]), f32)
+    words = jnp.concatenate([events_ref[...].astype(f32), fill], axis=1)
+    words = words[0:1] + pltpu.roll(words, events_ref.shape[1], 1)[1:2]
+    count = jnp.sum(flags_ref[...].astype(f32), axis=1, keepdims=True)
+    lane = lax.broadcasted_iota(jnp.int32, words.shape, 1)
+    words_ref[...] = jnp.broadcast_to(jnp.where(lane == SLOT - 1, count, words), words_ref.shape)
 
 
 def sums_of_window(squares):
@@ -68,7 +69,7 @@
     return window[:, :BLK]
 
 
-def correlate(distances, here_ref, wave_ref, next_ref, templates_ref, keep_ref, send_ref, waves, held, sliding, arrival):
+def correlate(distances, here_ref, wave_ref, next_ref, words_ref, templates_ref, keep_ref, send_ref, waves, held, sliding, arrival):
     planes = len(distances)
     group = held.shape[2]
     plane, core, around = here_ref[0], here_ref[1], here_ref[3]
@@ -95,8 +96,11 @@
     build(segment, sliding)
     if keep_ref.shape[0] > planes * group:
         energy = sums_of_window(jnp.sum(segment * segment, axis=0, keepdims=True))
-        keep_ref[planes * group :] = energy
-        send_ref[planes * group :] = energy
+        words = jnp.concatenate([words_ref[...]] * (BLK // LANES), axis=1)
+        row = lax.broadcasted_iota(jnp.int32, energy.shape, 0)
+        below = jnp.where(row == WORDS, words, energy)
+        keep_ref[planes * group :] = below
+        send_ref[planes * group :] = below
     for i in range(planes):
         for half, out_ref in enumerate((send_ref, keep_ref)):
             copy(i, half).wait()
@@ -111,13 +115,18 @@
     return rows == lax.broadcasted_iota(jnp.int32, (size, size), 1)
 
 
-def merge(keep_ref, came_ref, energy_ref, *code_refs):
+def merge(keep_ref, came_ref, energy_ref, note_ref, *code_refs):
     half = code_refs[0].shape[0] - 8
     group = 2 * half
     square = diagonal(group)
     last = len(code_refs) * group
     energy = keep_ref[last:] + came_ref[last:]
     energy_ref[...] = energy
+    words = [ref[last + WORDS : last + WORDS + 1, :LANES].astype(jnp.int32) for ref in (keep_ref, came_ref)]
+    lane = lax.broadcasted_iota(jnp.int32, (1, LANES), 1)
+    words = jnp.where(lane < SLOT, words[0], pltpu.roll(words[1], SLOT, 1))
+    words = jnp.concatenate([words] * (note_ref.shape[2] // LANES), axis=1)
+    note_ref[...] = jnp.broadcast_to(words[None], note_ref.shape)
     logarithm = jnp.log2(jnp.maximum(energy, 1e-30))
     sample = jnp.round(4.0 * logarithm)
     level = jnp.exp2(sample[:1] * -0.125)
@@ -176,36 +185,49 @@
         energy = energy + more
     stack = stack * (1.0 / jnp.sqrt(energy + epsilon))
     stack_ref[...] = stack
-    info = info_ref[:, 0, :]
-    devices = info.shape[0]
-    rows = lax.broadcasted_iota(jnp.int32, info.shape, 0)
+    info = info_ref[:, 0, :LANES]
+    chips = info.shape[0]
+    core, here = here_ref[1], here_ref[2]
     lanes = lax.broadcasted_iota(jnp.int32, info.shape, 1)
-    counted = lanes == LANES - 1
-    here = here_ref[2]
-    start = jnp.sum(jnp.where(counted & (rows < here), info, 0))
-    found = jnp.sum(jnp.where(counted & (rows == here), info, 0))
-    mine = (info >= start) & (info < start + found) & (lanes < 32)
-    rank = jnp.sum(jnp.where(mine, info - start + 1, 0), axis=1, keepdims=True) - 1
+    second = lanes >= SLOT
+    device = 2 * lax.broadcasted_iota(jnp.int32, info.shape, 0) + jnp.where(second, 1 - core, core)
+    word = jnp.where(second, lanes - SLOT, lanes)
+    start = jnp.sum(jnp.where((word == SLOT - 1) & (device < here), info, 0))
+    found = jnp.sum(flags_ref[...])
+    mine = (info >= start) & (info < start + found) & (word < 32)
+    rank = jnp.where(mine, info - start + 1, 0)
+    ranks = [jnp.sum(jnp.where(side, rank, 0), axis=1, keepdims=True) - 1 for side in (lanes < SLOT, second)]
+    ranks = [jnp.where(core == 0, ranks[k], ranks[1 - k]) for k in range(2)]
+    rank = jnp.concatenate(ranks, axis=0)
     flags = jnp.broadcast_to(flags_ref[...], (8, group)).astype(f32)
     earlier = lax.broadcasted_iota(jnp.int32, (group, group), 0) < lax.broadcasted_iota(
         jnp.int32, (group, group), 1
     )
     before = jnp.dot(flags.astype(bf16), earlier.astype(f32).astype(bf16), preferred_element_type=f32)
     before = jnp.where(flags > 0.5, before, -2.0)
-    selector = jnp.broadcast_to(before[:1], (devices, group)) == rank.astype(f32)
+    selector = jnp.broadcast_to(before[:1], (2 * chips, group)) == rank.astype(f32)
     windows = pick(selector.astype(f32).astype(bf16), three(stack))
-    windows_ref[:, 0, :] = windows
-
-
-def cross(lags_ref, events_ref, info_ref, received_ref, out_ref, turned, products):
-    info = info_ref[:, 0, :]
-    devices = info.shape[0]
+    across = BLK // LANES
+    for k in range(across):
+        rows = pl.ds(k, windows.shape[0], stride=across)
+        windows_ref[rows, :] = windows[:, k * LANES : (k + 1) * LANES]
+
+
+def cross(here_ref, lags_ref, events_ref, info_ref, received_ref, out_ref, turned, products):
+    info = info_ref[:, 0, :LANES]
+    chips = info.shape[0]
     pairs = out_ref.shape[0]
-    rows = lax.broadcasted_iota(jnp.int32, (devices, devices), 0)
-    columns = lax.broadcasted_iota(jnp.int32, (devices, devices), 1)
-    counts = jnp.broadcast_to(info[:, LANES - 1 :], (devices, devices))
-    starts = jnp.sum(jnp.where(rows < columns, counts, 0), axis=0, keepdims=True)
-    ends = jnp.sum(jnp.where(rows <= columns, counts, 0), axis=0, keepdims=True)
+    core = here_ref[1]
+    counts = [jnp.where(core == k, info[:, SLOT - 1 : SLOT], info[:, LANES - 1 :]) for k in range(2)]
+    rows = lax.broadcasted_iota(jnp.int32, (chips, 2 * chips), 0)
+    lanes = lax.broadcasted_iota(jnp.int32, (chips, 2 * chips), 1)
+    second = lanes >= chips
+    chip = jnp.where(second, lanes - chips, lanes)
+    earlier = jnp.where(rows < chip, counts[0] + counts[1], 0)
+    earlier = earlier + jnp.where((rows == chip) & second, counts[0], 0)
+    starts = jnp.sum(earlier, axis=0, keepdims=True)
+    own = jnp.where(rows == chip, jnp.where(second, counts[1], counts[0]), 0)
+    ends = starts + jnp.sum(own, axis=0, keepdims=True)
     square = diagonal(pairs)
     both = jnp.concatenate(
         [
@@ -215,7 +237,9 @@
         axis=0,
     )
     selector = (starts <= both) & (both < ends)
-    picked = pick(selector.astype(f32).astype(bf16), three(received_ref[:, 0, :]))
+    across = BLK // LANES
+    received = [received_ref[pl.ds(k, 2 * chips, stride=across), :] for k in range(across)]
+    picked = pick(selector.astype(f32).astype(bf16), three(jnp.concatenate(received, axis=1)))
     first, second = picked[:pairs], picked[pairs:]
     length = 2 * BLK
     nothing = jnp.zeros((pairs, BLK), f32)
@@ -238,11 +262,12 @@
                 part = part + product[:, k : k + LANES]
             products[pl.ds(p * NLAG + 8 * u, 8), :] = part
     ones = jnp.ones((8, LANES), bf16)
-    high, middle, low = [
+    high, middle, _ = three(products[...])
+    high, middle = [
         lax.dot_general(ones, part, (((1,), (1,)), ((), ())), preferred_element_type=f32)
-        for part in three(products[...])
+        for part in (high, middle)
     ]
-    raw = high + (middle + low)
+    raw = high + middle
     raw = jnp.concatenate([raw[:1, p * NLAG : (p + 1) * NLAG] for p in range(pairs)], axis=0)
     power_one = jnp.mean(first * first, axis=1, keepdims=True)
     power_two = jnp.mean(second * second, axis=1, keepdims=True)
@@ -250,29 +275,35 @@
 
 
 def shards(waveforms, templates, detection_flags, pair_events, pair_lags):
-    across = lax.axis_size("sta")
-    ahead = lax.axis_size("tm")
-    devices = across * ahead
+    ahead, planes = lax.axis_size("tm"), lax.axis_size("z")
+    chips = ahead * planes
     group = detection_flags.shape[0]
-    station_group = lax.axis_index("sta")
-    place = lax.axis_index("tm") * across + station_group
-    plane, core = station_group // 2, station_group % 2
-    planes = across // 2
+    plane, core = lax.axis_index("z"), lax.axis_index("core")
+    place = (lax.axis_index("tm") * planes + plane) * 2 + core
 
     following = lax.ppermute(waveforms, "tm", [(i, i - 1) for i in range(1, ahead)])
-
-    here = jnp.stack([plane, core, place, planes]).astype(jnp.int32)
+    here = jnp.stack([plane, core, place, jnp.int32(planes)]).astype(jnp.int32)
     flags = detection_flags.reshape(1, group)
     events = pair_events.T
+    words, waves = whole(
+        announce,
+        (pltpu.VMEM((8, LANES), f32), pltpu.VMEM(waveforms.shape, bf16)),
+        1 << 20,
+        waveforms,
+        flags,
+        events,
+    )
+
+    stations = templates.shape[1]
 
     def partial(distances, here, below):
         count = len(distances)
+        flops = 4 * count * group * stations * TLEN * BLK
         shape = pltpu.VMEM((count * group + below, BLK), f32)
-        stations = templates.shape[1]
         return pl.pallas_call(
             functools.partial(correlate, distances),
             out_shape=(shape, shape),
-            in_specs=[SMEM] + [pl.BlockSpec(memory_space=pl.ANY)] * 2 + [pl.BlockSpec(memory_space=pltpu.HBM)],
+            in_specs=[SMEM] + [pl.BlockSpec(memory_space=pl.ANY)] * 2 + [VMEM, pl.BlockSpec(memory_space=pltpu.HBM)],
             out_specs=(VMEM, VMEM),
             scratch_shapes=[
                 pltpu.VMEM((2, stations, BLK), bf16),
@@ -282,17 +313,15 @@
             ],
             compiler_params=pltpu.CompilerParams(vmem_limit_bytes=48 << 20),
             cost_estimate=pl.CostEstimate(
-                flops=count * 4 * group * stations * TLEN * BLK,
-                bytes_accessed=count * 4 * group * stations * TLEN,
-                transcendentals=0,
+                flops=flops, bytes_accessed=flops // BLK, transcendentals=0
             ),
-        )(here, waveforms, following, templates)
+        )(here, waves, following, words, templates)
 
     def over(distance, values):
-        return lax.ppermute(values, "sta", [(i, (i + 2 * distance) % across) for i in range(across)])
+        return lax.ppermute(values, "z", [(i, (i + distance) % planes) for i in range(planes)])
 
     def swap(values):
-        return lax.ppermute(values, "sta", [(i, i ^ 1) for i in range(across)])
+        return lax.ppermute(values, "core", [(0, 1), (1, 0)])
 
     away = (2, 1, 3)
     keeps, sends = partial(away, here, 8)
@@ -302,21 +331,20 @@
     came = swap(send)
     cames, _ = lax.optimization_barrier((cames, keep))
     shape = jax.ShapeDtypeStruct((group // 2 + 8, BLK), jnp.int32)
-    energy, *codes = whole(
-        merge, (jax.ShapeDtypeStruct((8, BLK), f32),) + (shape,) * len(away), 1 << 22, keeps, cames
+    note = jax.ShapeDtypeStruct((chips, 1, LANES), jnp.int32)
+    energy, note, *codes = whole(
+        merge,
+        (jax.ShapeDtypeStruct((8, BLK), f32), note) + (shape,) * len(away),
+        1 << 22,
+        keeps,
+        cames,
     )
     arrived = [over(distance, values) for distance, values in zip(away, codes)]
-
-    note = whole(announce, jax.ShapeDtypeStruct((devices, 1, LANES), jnp.int32), 1 << 20, flags, events)
-    note, _ = lax.optimization_barrier((note, codes))
-    info = lax.all_to_all(note, BOTH, 0, 0, tiled=True)
+    info = lax.all_to_all(note, ("tm", "z"), 0, 0, tiled=True)
 
     network_stack, windows = whole(
         finish,
-        (
-            jax.ShapeDtypeStruct((group, BLK), f32),
-            jax.ShapeDtypeStruct((devices, 1, BLK), f32),
-        ),
+        (jax.ShapeDtypeStruct((group, BLK), f32), jax.ShapeDtypeStruct((2 * chips * BLK // LANES, LANES), f32)),
         1 << 24,
         here,
         keep,
@@ -327,17 +355,20 @@
         info,
         smem=1,
     )
-    received = lax.all_to_all(windows, BOTH, 0, 0, tiled=True)
+    windows = windows.reshape(2 * chips, BLK // LANES, LANES)
+    received = lax.all_to_all(windows, ("core", "tm", "z"), 0, 0, tiled=True)
+    received = received.reshape(-1, LANES)
     pairs = pair_events.shape[0]
     pair_cc = whole(
         cross,
         jax.ShapeDtypeStruct((pairs, NLAG), f32),
         1 << 24,
+        here,
         pair_lags,
         events,
         info,
         received,
-        smem=1,
+        smem=2,
         scratch=[
             pltpu.VMEM((NLAG // 8, pairs, NLAG + BLK), f32),
             pltpu.VMEM((pairs * NLAG, LANES), f32),
@@ -347,16 +378,20 @@
 
 
 def solution(mesh):
+    ahead, across = mesh.devices.shape
+    split = jax.sharding.Mesh(mesh.devices.reshape(ahead, across // 2, 2), ("tm", "z", "core"))
+    stations = ("z", "core")
+    owners = ("tm", "z", "core")
     return jax.shard_map(
         shards,
-        mesh=mesh,
+        mesh=split,
         in_specs=(
-            P("sta", "tm"),
-            P(None, "sta", None),
-            P("sta", "tm"),
-            P(("tm", "sta"), None),
-            P(("tm", "sta")),
+            P(stations, "tm"),
+            P(None, stations, None),
+            P(stations, "tm"),
+            P(owners, None),
+            P(owners),
         ),
-        out_specs=(P("sta", "tm"), P(("tm", "sta"), None)),
+        out_specs=(P(stations, "tm"), P(owners, None)),
         check_vma=False,
     )

time: 73.1 us -> 70.6 us (0.966)
  waiting for transfers between devices: 13.1 us -> 10 us
  Pallas kernels: 23.2 us -> 21.3 us
  blocking collectives: 15.3 us -> 16.7 us
  local copies, waits for them, and re-layouts: 0.72 us -> 2.07 us
    ppermute x1, waiting for transfers between devices: 3.8 us -> 1.68 us  [shards(): lax.ppermute(waveforms, 'tm', [(i, i - 1) for i in range(1, ahead)])]
    pallas_call x4, Pallas kernels: 7.57 us -> 5.65 us  [whole(): pl.pallas_call(kernel, out_shape=outs, in_specs=[SMEM] * smem + [VMEM] *...]
    all_to_all x1, blocking collectives: 15.3 us -> 16.7 us  [shards(): received = lax.all_to_all(windows, ('core', 'tm', 'z'), 0, 0, tiled=True)]
    unnamed x8 -> x12, local copies, waits for them, and re-layouts: 0.72 us -> 2.07 us
    all_to_all x1, waiting for transfers between devices: 9.32 us -> 8.31 us  [shards(): info = lax.all_to_all(note, ('tm', 'z'), 0, 0, tiled=True)]
  transfers between devices with their start and end apart: 7 -> 7, of which waited for: 2 -> 2; matrix products, arithmetic and copies ran while one was open for 0% -> 0% of each run, Pallas kernels for 9% -> 8%
where the time goes in v4:
time: 70.6 us; the launch traced here: 70.3 us
  Pallas kernels  21.3 us (30%)
  starting transfers between devices  19.5 us (28%)
  blocking collectives  16.7 us (24%)
  waiting for transfers between devices  10 us (14%)
  local copies, waits for them, and re-layouts  2.07 us (3%)
  between operations  0.71 us (1%)
    all_to_all x1, blocking collectives, shards(): received = lax.all_to_all(windows, ('core', 'tm', 'z'), 0, 0, tiled=True)  16.7 us
    pallas_call x2, Pallas kernels, partial(): pl.pallas_call(functools.partial(correlate, distances), out_shape=(shape,...  15.6 us
    all_to_all x1, starting transfers between devices, shards(): info = lax.all_to_all(note, ('tm', 'z'), 0, 0, tiled=True)  9.49 us
    all_to_all x1, waiting for transfers between devices, shards(): info = lax.all_to_all(note, ('tm', 'z'), 0, 0, tiled=True)  8.31 us
    ppermute x3, starting transfers between devices, over(): lax.ppermute(values, 'z', [(i, (i + distance) % planes) for i in range(pl...  6.37 us
    pallas_call x4, Pallas kernels, whole(): pl.pallas_call(kernel, out_shape=outs, in_specs=[SMEM] * smem + [VMEM] *...  5.65 us
    ppermute x2, starting transfers between devices, swap(): return lax.ppermute(values, 'core', [(0, 1), (1, 0)])  2.33 us
    unnamed x12, local copies, waits for them, and re-layouts  2.07 us
  transfers between devices with their start and end apart: 7, of which 2 were waited for; matrix products, arithmetic and copies ran while one was open for 0% of the time, Pallas kernels for 8%

profile of v4, /device:TPU:1, one launch (start us, length us, event | category | flops | bytes accessed | tf_op | source)
XLA Modules:
  0.0 70.3 jit_solution(16744661566834126021)
XLA Ops:
  0.6 1.3 %collective-permute-start = (bf16[8,512]{1,0:T(8,128)(2,1)}, bf16[8,512]{1,0:T(8,128)(2,1)S(1)}, u32[]{:S(2)}, u32[]{:S(2)}) collective-permute-start(bf16[8,512]{1,0:T(8,128)(2,1)} %wave_ref.1), channel_id=1, source_target_pairs={{8,0},{16,8},{24,16},{32,24},{40,32},{48,40},{56,48},{64,56},{72,6... | collective-permute-start | bytes 24584 | tf_op jit(solution)/shard_map/ppermute | solution.py:284
  1.9 0.1 pad_add_fusion.here_ref
  2.0 0.0 copy-start
  2.0 0.7 copy-done
  2.7 0.0 copy-start.1
  2.7 0.7 copy-done.1
  3.4 0.0 copy-start.3
  3.4 0.7 copy-done.3
  4.1 0.1 shard_map.68
  4.1 1.7 %collective-permute-done.next_ref = bf16[8,512]{1,0:T(8,128)(2,1)S(1)} collective-permute-done((bf16[8,512]{1,0:T(8,128)(2,1)}, bf16[8,512]{1,0:T(8,128)(2,1)S(1)}, u32[]{:S(2)}, u32[]{:S(2)}) %collective-permute-start) | collective-permute-done | bytes 8224 | tf_op jit(solution)/shard_map/ppermute | solution.py:284
  5.8 10.6 %shard_map.69 = (f32[776,512]{1,0:T(8,128)S(1)}, f32[776,512]{1,0:T(8,128)S(1)}) custom-call(s32[4]{0:T(128)S(1)} %pad_add_fusion.here_ref, bf16[8,512]{1,0:T(8,128)(2,1)S(1)} %get-tuple-element.17.wave_ref, bf16[8,512]{1,0:T(8,128)(2,1)S(1)} %collective-permute-done.next_ref, f32[8,128]{1,0:T(8,128)S(1)} %get-tuple-element.18.words_ref, ...), custom_call_target="tpu_custom_call" | custom-call | flops 6442450944 | bytes 12582912 | tf_op jit(solution)/shard_map/pallas_call | solution.py:303
  16.5 2.1 %collective-permute-start.2 = (f32[776,512]{1,0:T(8,128)S(1)}, f32[776,512]{1,0:T(8,128)S(1)}, u32[]{:S(2)}, u32[]{:S(2)}) collective-permute-start(f32[776,512]{1,0:T(8,128)S(1)} %get-tuple-element.23), channel_id=1, source_target_pairs={{0,1},{1,0},{2,3},{3,2},{4,5},{5,4},{6,7},{7,6},{8,9},{9,8},{10,11... | collective-permute-start | bytes 4767752 | tf_op jit(solution)/shard_map/ppermute | solution.py:324
  18.5 5.0 %shard_map.70 = (f32[256,512]{1,0:T(8,128)S(1)}, f32[256,512]{1,0:T(8,128)S(1)}) custom-call(s32[4]{0:T(128)S(1)} %pad_add_fusion.here_ref, bf16[8,512]{1,0:T(8,128)(2,1)S(1)} %get-tuple-element.17.wave_ref, bf16[8,512]{1,0:T(8,128)(2,1)S(1)} %collective-permute-done.next_ref, f32[8,128]{1,0:T(8,128)S(1)} %get-tuple-element.18.words_ref, ...), custom_call_target="tpu_custom_call" | custom-call | flops 2147483648 | bytes 4194304 | tf_op jit(solution)/shard_map/pallas_call | solution.py:303
  23.5 0.3 collective-permute-start.1
  23.8 0.0 collective-permute-done.2.came_ref
  23.8 0.0 copy-start.2
  23.8 0.8 %shard_map.71 = (f32[8,512]{1,0:T(8,128)S(1)}, s32[64,1,128]{2,1,0:T(1,128)}, s32[136,512]{1,0:T(8,128)S(1)}, s32[136,512]{1,0:T(8,128)S(1)}, s32[136,512]{1,0:T(8,128)S(1)}) custom-call(f32[776,512]{1,0:T(8,128)S(1)} %get-tuple-element.19.keep_ref, f32[776,512]{1,0:T(8,128)S(1)} %collective-permute-done.2.came_ref), custom_call_target="tpu_custom_call" | custom-call | flops 4194304 | bytes 1048576 | tf_op jit(solution)/shard_map/pallas_call | solution.py:25
  24.6 0.0 copy-start.4
  24.6 0.0 copy-start.5
  24.6 3.7 %collective-permute-start.3 = (s32[136,512]{1,0:T(8,128)S(1)}, s32[136,512]{1,0:T(8,128)S(1)}, u32[]{:S(2)}, u32[]{:S(2)}) collective-permute-start(s32[136,512]{1,0:T(8,128)S(1)} %get-tuple-element.26), channel_id=1, source_target_pairs={{0,4},{2,6},{4,0},{6,2},{1,5},{3,7},{5,1},{7,3},{8,12},{10,14},{12... | collective-permute-start | bytes 835592 | tf_op jit(solution)/shard_map/ppermute | solution.py:321
  28.3 0.7 %collective-permute-start.4 = (s32[136,512]{1,0:T(8,128)S(1)}, s32[136,512]{1,0:T(8,128)S(1)}, u32[]{:S(2)}, u32[]{:S(2)}) collective-permute-start(s32[136,512]{1,0:T(8,128)S(1)} %get-tuple-element.27), channel_id=1, source_target_pairs={{0,2},{2,4},{4,6},{6,0},{1,3},{3,5},{5,7},{7,1},{8,10},{10,12},{12... | collective-permute-start | bytes 835592 | tf_op jit(solution)/shard_map/ppermute | solution.py:321
  29.1 1.9 %collective-permute-start.5 = (s32[136,512]{1,0:T(8,128)S(1)}, s32[136,512]{1,0:T(8,128)S(1)}, u32[]{:S(2)}, u32[]{:S(2)}) collective-permute-start(s32[136,512]{1,0:T(8,128)S(1)} %get-tuple-element.28), channel_id=1, source_target_pairs={{0,6},{2,0},{4,2},{6,4},{1,7},{3,1},{5,3},{7,5},{8,14},{10,8},{12,... | collective-permute-start | bytes 835592 | tf_op jit(solution)/shard_map/ppermute | solution.py:321
  31.0 9.5 %all-to-all-start = ((s32[64,1,128]{2,1,0:T(1,128)}), s32[64,1,128]{2,1,0:T(1,128)S(1)}, u32[]{:S(2)}, u32[]{:S(2)}) async-start(s32[64,1,128]{2,1,0:T(1,128)} %get-tuple-element.29), calls=%async_computation | async-start | bytes 65536 | tf_op jit(solution)/shard_map/all_to_all | solution.py:343
  40.5 0.0 collective-permute-done.1.came_ref
  40.5 8.3 %all-to-all-done.info_ref = s32[64,1,128]{2,1,0:T(1,128)S(1)} async-done(((s32[64,1,128]{2,1,0:T(1,128)}), s32[64,1,128]{2,1,0:T(1,128)S(1)}, u32[]{:S(2)}, u32[]{:S(2)}) %all-to-all-start) | async-done | bytes 32800 | tf_op jit(solution)/shard_map/all_to_all | solution.py:343
  48.8 0.0 collective-permute-done.3.a_ref
  48.8 0.0 collective-permute-done.4.b_ref
  48.8 0.0 collective-permute-done.5.c_ref
  48.8 0.0 copy-done.2
  48.8 2.0 %shard_map.72 = (f32[256,512]{1,0:T(8,128)}, f32[512,128]{1,0:T(8,128)S(1)}) custom-call(s32[4]{0:T(128)S(1)} %pad_add_fusion.here_ref, f32[256,512]{1,0:T(8,128)S(1)} %get-tuple-element.21.keep_ref, f32[256,512]{1,0:T(8,128)S(1)} %collective-permute-done.1.came_ref, f32[8,512]{1,0:T(8,128)S(1)} %get-tuple-element.25.energy_ref, ...), custom_call_target="tpu_custom_call" | custom-call | flops 16777216 | bytes 1048576 | tf_op jit(solution)/shard_map/pallas_call | solution.py:25
  50.8 16.7 %all_to_all.10 = f32[128,4,128]{2,1,0:T(4,128)S(1)} all-to-all(f32[128,4,128]{2,1,0:T(4,128)S(1)} %bitcast.8), channel_id=1, replica_groups=mesh['tm'=16,'z'=4,'core'=2] {'core','tm','z'}, dimensions={0} | all-to-all | bytes 524288 | tf_op jit(solution)/shard_map/all_to_all | solution.py:359
  67.5 0.0 copy-done.4
  67.5 0.0 copy-done.5
  67.5 2.8 %shard_map.73 = f32[16,128]{1,0:T(8,128)} custom-call(s32[4]{0:T(128)S(1)} %pad_add_fusion.here_ref, s32[16]{0:T(128)S(1)} %copy-done.5, s32[2,16]{1,0:T(2,128)S(1)} %bitcast.12, s32[64,1,128]{2,1,0:T(1,128)S(1)} %all-to-all-done.info_ref, f32[512,128]{1,0:T(8,128)S(1)} %bitcast.7), custom_call_target="tpu_custom_call" | custom-call | flops 16777216 | bytes 1048576 | tf_op jit(solution)/shard_map/pallas_call | solution.py:25
Async XLA Ops:
  0.6 5.2 %collective-permute-start = (bf16[8,512]{1,0:T(8,128)(2,1)}, bf16[8,512]{1,0:T(8,128)(2,1)S(1)}, u32[]{:S(2)}, u32[]{:S(2)}) collective-permute-start(bf16[8,512]{1,0:T(8,128)(2,1)} %wave_ref.1), channel_id=1, source_target_pairs={{8,0},{16,8},{24,16},{32,24},{40,32},{48,40},{56,48},{64,56},{72,6... | collective-permute-start | bytes 24584 | tf_op jit(solution)/shard_map/ppermute | solution.py:284
  2.0 0.7 copy-start
  2.7 0.7 copy-start.1
  3.4 0.7 copy-start.3
  16.5 7.4 %collective-permute-start.2 = (f32[776,512]{1,0:T(8,128)S(1)}, f32[776,512]{1,0:T(8,128)S(1)}, u32[]{:S(2)}, u32[]{:S(2)}) collective-permute-start(f32[776,512]{1,0:T(8,128)S(1)} %get-tuple-element.23), channel_id=1, source_target_pairs={{0,1},{1,0},{2,3},{3,2},{4,5},{5,4},{6,7},{7,6},{8,9},{9,8},{10,11... | collective-permute-start | bytes 4767752 | tf_op jit(solution)/shard_map/ppermute | solution.py:324
  23.5 17.0 %collective-permute-start.1 = (f32[256,512]{1,0:T(8,128)S(1)}, f32[256,512]{1,0:T(8,128)S(1)}, u32[]{:S(2)}, u32[]{:S(2)}) collective-permute-start(f32[256,512]{1,0:T(8,128)S(1)} %get-tuple-element.22), channel_id=1, source_target_pairs={{0,1},{1,0},{2,3},{3,2},{4,5},{5,4},{6,7},{7,6},{8,9},{9,8},{10,11... | collective-permute-start | bytes 1572872 | tf_op jit(solution)/shard_map/ppermute | solution.py:324
  23.8 25.0 %copy-start.2 = (s32[256,1]{0,1:T(1,128)S(1)}, s32[256,1]{0,1:T(1,128)}, u32[]{:S(2)}) copy-start(s32[256,1]{0,1:T(1,128)} %param.7) | copy-start | bytes 3076
  24.6 42.9 %copy-start.4 = (s32[16,2]{0,1:T(2,128)S(1)}, s32[16,2]{0,1:T(2,128)}, u32[]{:S(2)}) copy-start(s32[16,2]{0,1:T(2,128)} %param.8) | copy-start | bytes 388
  24.6 42.9 %copy-start.5 = (s32[16]{0:T(128)S(1)}, s32[16]{0:T(128)}, u32[]{:S(2)}) copy-start(s32[16]{0:T(128)} %lags_ref.1) | copy-start | bytes 196
  24.6 24.2 %collective-permute-start.3 = (s32[136,512]{1,0:T(8,128)S(1)}, s32[136,512]{1,0:T(8,128)S(1)}, u32[]{:S(2)}, u32[]{:S(2)}) collective-permute-start(s32[136,512]{1,0:T(8,128)S(1)} %get-tuple-element.26), channel_id=1, source_target_pairs={{0,4},{2,6},{4,0},{6,2},{1,5},{3,7},{5,1},{7,3},{8,12},{10,14},{12... | collective-permute-start | bytes 835592 | tf_op jit(solution)/shard_map/ppermute | solution.py:321
  28.3 20.5 %collective-permute-start.4 = (s32[136,512]{1,0:T(8,128)S(1)}, s32[136,512]{1,0:T(8,128)S(1)}, u32[]{:S(2)}, u32[]{:S(2)}) collective-permute-start(s32[136,512]{1,0:T(8,128)S(1)} %get-tuple-element.27), channel_id=1, source_target_pairs={{0,2},{2,4},{4,6},{6,0},{1,3},{3,5},{5,7},{7,1},{8,10},{10,12},{12... | collective-permute-start | bytes 835592 | tf_op jit(solution)/shard_map/ppermute | solution.py:321
  29.1 19.8 %collective-permute-start.5 = (s32[136,512]{1,0:T(8,128)S(1)}, s32[136,512]{1,0:T(8,128)S(1)}, u32[]{:S(2)}, u32[]{:S(2)}) collective-permute-start(s32[136,512]{1,0:T(8,128)S(1)} %get-tuple-element.28), channel_id=1, source_target_pairs={{0,6},{2,0},{4,2},{6,4},{1,7},{3,1},{5,3},{7,5},{8,14},{10,8},{12,... | collective-permute-start | bytes 835592 | tf_op jit(solution)/shard_map/ppermute | solution.py:321
  31.0 17.8 %all-to-all-start = ((s32[64,1,128]{2,1,0:T(1,128)}), s32[64,1,128]{2,1,0:T(1,128)S(1)}, u32[]{:S(2)}, u32[]{:S(2)}) async-start(s32[64,1,128]{2,1,0:T(1,128)} %get-tuple-element.29), calls=%async_computation | async-start | bytes 65536 | tf_op jit(solution)/shard_map/all_to_all | solution.py:343

commit v5 on v4

--- a/solution.py
+++ b/solution.py
@@ -69,38 +69,36 @@
     return window[:, :BLK]
 
 
-def correlate(distances, here_ref, wave_ref, next_ref, words_ref, templates_ref, keep_ref, send_ref, waves, held, sliding, arrival):
+def correlate(distances, here_ref, wave_ref, next_ref, words_ref, templates_ref, keep_ref, send_ref, sliding, own, waves, held, arrival):
     planes = len(distances)
     group = held.shape[2]
     plane, core, around = here_ref[0], here_ref[1], here_ref[3]
 
     def copy(i, half):
-        chip = lax.rem(plane + distances[i], around)
+        chip = lax.rem(plane + distances[i], around) if i < planes else plane
         first = (chip * 2 + (1 - core if half == 0 else core)) * group
-        return pltpu.make_async_copy(
-            templates_ref.at[pl.ds(first, group)], held.at[i, half], arrival.at[i, half]
-        )
+        target = held.at[i, half] if i < planes else own.at[half]
+        return pltpu.make_async_copy(templates_ref.at[pl.ds(first, group)], target, arrival.at[i, half])
 
     pieces = [
-        pltpu.make_async_copy(wave_ref, waves.at[0], arrival.at[planes, 0]),
-        pltpu.make_async_copy(next_ref, waves.at[1], arrival.at[planes, 1]),
+        pltpu.make_async_copy(wave_ref, waves.at[0], arrival.at[planes + 1, 0]),
+        pltpu.make_async_copy(next_ref, waves.at[1], arrival.at[planes + 1, 1]),
     ]
     for piece in pieces:
         piece.start()
-    for i in range(planes):
+    for i in range(planes + 1):
         for half in range(2):
             copy(i, half).start()
     for piece in pieces:
         piece.wait()
     segment = jnp.concatenate([waves[0], waves[1]], axis=1).astype(f32)
     build(segment, sliding)
-    if keep_ref.shape[0] > planes * group:
-        energy = sums_of_window(jnp.sum(segment * segment, axis=0, keepdims=True))
-        words = jnp.concatenate([words_ref[...]] * (BLK // LANES), axis=1)
-        row = lax.broadcasted_iota(jnp.int32, energy.shape, 0)
-        below = jnp.where(row == WORDS, words, energy)
-        keep_ref[planes * group :] = below
-        send_ref[planes * group :] = below
+    energy = sums_of_window(jnp.sum(segment * segment, axis=0, keepdims=True))
+    words = jnp.concatenate([words_ref[...]] * (BLK // LANES), axis=1)
+    row = lax.broadcasted_iota(jnp.int32, energy.shape, 0)
+    below = jnp.where(row == WORDS, words, energy)
+    keep_ref[planes * group :] = below
+    send_ref[planes * group :] = below
     for i in range(planes):
         for half, out_ref in enumerate((send_ref, keep_ref)):
             copy(i, half).wait()
@@ -108,6 +106,14 @@
             out_ref[i * group : (i + 1) * group] = jnp.dot(
                 filters, sliding[...], preferred_element_type=f32
             )
+    for half in range(2):
+        copy(planes, half).wait()
+
+
+def correlate_own(own_ref, sliding_ref, keep_ref, send_ref):
+    for half, out_ref in enumerate((send_ref, keep_ref)):
+        filters = own_ref[half].reshape(own_ref.shape[1], -1)
+        out_ref[...] = jnp.dot(filters, sliding_ref[...], preferred_element_type=f32)
 
 
 def diagonal(size):
@@ -295,27 +301,30 @@
     )
 
     stations = templates.shape[1]
-
-    def partial(distances, here, below):
-        count = len(distances)
-        flops = 4 * count * group * stations * TLEN * BLK
-        shape = pltpu.VMEM((count * group + below, BLK), f32)
-        return pl.pallas_call(
-            functools.partial(correlate, distances),
-            out_shape=(shape, shape),
-            in_specs=[SMEM] + [pl.BlockSpec(memory_space=pl.ANY)] * 2 + [VMEM, pl.BlockSpec(memory_space=pltpu.HBM)],
-            out_specs=(VMEM, VMEM),
-            scratch_shapes=[
-                pltpu.VMEM((2, stations, BLK), bf16),
-                pltpu.VMEM((count, 2, group, stations, TLEN), bf16),
-                pltpu.VMEM((stations * TLEN, BLK), bf16),
-                pltpu.SemaphoreType.DMA((count + 1, 2)),
-            ],
-            compiler_params=pltpu.CompilerParams(vmem_limit_bytes=48 << 20),
-            cost_estimate=pl.CostEstimate(
-                flops=flops, bytes_accessed=flops // BLK, transcendentals=0
-            ),
-        )(here, waves, following, words, templates)
+    away = (2, 1, 3)
+    any_space = pl.BlockSpec(memory_space=pl.ANY)
+    flops = 4 * group * stations * TLEN * BLK
+    shape = pltpu.VMEM((len(away) * group + 8, BLK), f32)
+    keeps, sends, sliding, own = pl.pallas_call(
+        functools.partial(correlate, away),
+        out_shape=(
+            shape,
+            shape,
+            pltpu.VMEM((stations * TLEN, BLK), bf16),
+            pltpu.VMEM((2, group, stations, TLEN), bf16),
+        ),
+        in_specs=[SMEM, any_space, any_space, VMEM, pl.BlockSpec(memory_space=pltpu.HBM)],
+        out_specs=(VMEM,) * 4,
+        scratch_shapes=[
+            pltpu.VMEM((2, stations, BLK), bf16),
+            pltpu.VMEM((len(away), 2, group, stations, TLEN), bf16),
+            pltpu.SemaphoreType.DMA((len(away) + 2, 2)),
+        ],
+        compiler_params=pltpu.CompilerParams(vmem_limit_bytes=42 << 20),
+        cost_estimate=pl.CostEstimate(
+            flops=len(away) * flops, bytes_accessed=len(away) * flops // BLK, transcendentals=0
+        ),
+    )(here, waves, following, words, templates)
 
     def over(distance, values):
         return lax.ppermute(values, "z", [(i, (i + distance) % planes) for i in range(planes)])
@@ -323,11 +332,9 @@
     def swap(values):
         return lax.ppermute(values, "core", [(0, 1), (1, 0)])
 
-    away = (2, 1, 3)
-    keeps, sends = partial(away, here, 8)
     cames = swap(sends)
-    later, _ = lax.optimization_barrier((here, keeps))
-    keep, send = partial((0,), later, 0)
+    shape = pltpu.VMEM((group, BLK), f32)
+    keep, send = whole(correlate_own, (shape, shape), flops, own, sliding)
     came = swap(send)
     cames, _ = lax.optimization_barrier((cames, keep))
     shape = jax.ShapeDtypeStruct((group // 2 + 8, BLK), jnp.int32)
@@ -344,7 +351,7 @@
 
     network_stack, windows = whole(
         finish,
-        (jax.ShapeDtypeStruct((group, BLK), f32), jax.ShapeDtypeStruct((2 * chips * BLK // LANES, LANES), f32)),
+        (pltpu.VMEM((group, BLK), f32), jax.ShapeDtypeStruct((2 * chips * BLK // LANES, LANES), f32)),
         1 << 24,
         here,
         keep,

time: 70.6 us -> 68.8 us (0.975)
  blocking collectives: 16.7 us -> 0 us
  waiting for transfers between devices: 10 us -> 20 us
  starting transfers between devices: 19.5 us -> 25.7 us
  Pallas kernels: 21.3 us -> 19.2 us
  local copies, waits for them, and re-layouts: 2.07 us -> 2.87 us
    all_to_all x1 -> x0, blocking collectives: 16.7 us -> none  [shards(): received = lax.all_to_all(windows, ('core', 'tm', 'z'), 0, 0, tiled=True)]
    all_to_all x0 -> x1, waiting for transfers between devices: none -> 9.83 us  [shards(): received = lax.all_to_all(windows, ('core', 'tm', 'z'), 0, 0, tiled=True)]
    all_to_all x0 -> x1, starting transfers between devices: none -> 6.18 us  [shards(): received = lax.all_to_all(windows, ('core', 'tm', 'z'), 0, 0, tiled=True)]
    pallas_call x2 -> x1, Pallas kernels: 15.6 us -> 10.7 us  [shards(): pl.pallas_call(functools.partial(correlate, away), out_shape=(shape, shap...]
    pallas_call x4 -> x5, Pallas kernels: 5.65 us -> 8.53 us  [whole(): pl.pallas_call(kernel, out_shape=outs, in_specs=[SMEM] * smem + [VMEM] *...]
    unnamed x12 -> x13, local copies, waits for them, and re-layouts: 2.07 us -> 2.87 us
  transfers between devices with their start and end apart: 7 -> 8, of which waited for: 2 -> 4; matrix products, arithmetic and copies ran while one was open for 0% -> 1% of each run, Pallas kernels for 8% -> 5%
where the time goes in v5:
time: 68.8 us; the launch traced here: 68.5 us
  starting transfers between devices  25.7 us (37%)
  waiting for transfers between devices  20 us (29%)
  Pallas kernels  19.2 us (28%)
  local copies, waits for them, and re-layouts  2.87 us (4%)
  between operations  0.72 us (1%)
    pallas_call x1, Pallas kernels, shards(): pl.pallas_call(functools.partial(correlate, away), out_shape=(shape, shap...  10.7 us
    all_to_all x1, waiting for transfers between devices, shards(): received = lax.all_to_all(windows, ('core', 'tm', 'z'), 0, 0, tiled=True)  9.83 us
    all_to_all x1, starting transfers between devices, shards(): info = lax.all_to_all(note, ('tm', 'z'), 0, 0, tiled=True)  9.51 us
    pallas_call x5, Pallas kernels, whole(): pl.pallas_call(kernel, out_shape=outs, in_specs=[SMEM] * smem + [VMEM] *...  8.53 us
    all_to_all x1, waiting for transfers between devices, shards(): info = lax.all_to_all(note, ('tm', 'z'), 0, 0, tiled=True)  8.31 us
    ppermute x3, starting transfers between devices, over(): lax.ppermute(values, 'z', [(i, (i + distance) % planes) for i in range(pl...  6.35 us
    all_to_all x1, starting transfers between devices, shards(): received = lax.all_to_all(windows, ('core', 'tm', 'z'), 0, 0, tiled=True)  6.18 us
    unnamed x13, local copies, waits for them, and re-layouts  2.87 us
  transfers between devices with their start and end apart: 8, of which 4 were waited for; matrix products, arithmetic and copies ran while one was open for 1% of the time, Pallas kernels for 5%

profile of v5, /device:TPU:1, one launch (start us, length us, event | category | flops | bytes accessed | tf_op | source)
XLA Modules:
  0.0 68.5 jit_solution(13158512916163297864)
XLA Ops:
  0.6 1.3 %collective-permute-start = (bf16[8,512]{1,0:T(8,128)(2,1)}, bf16[8,512]{1,0:T(8,128)(2,1)S(1)}, u32[]{:S(2)}, u32[]{:S(2)}) collective-permute-start(bf16[8,512]{1,0:T(8,128)(2,1)} %wave_ref.1), channel_id=1, source_target_pairs={{8,0},{16,8},{24,16},{32,24},{40,32},{48,40},{56,48},{64,56},{72,6... | collective-permute-start | bytes 24584 | tf_op jit(solution)/shard_map/ppermute | solution.py:290
  1.9 0.1 pad_add_fusion.here_ref
  2.0 0.0 copy-start
  2.0 0.7 %copy-done = bf16[8,512]{1,0:T(8,128)(2,1)S(1)} copy-done((bf16[8,512]{1,0:T(8,128)(2,1)S(1)}, bf16[8,512]{1,0:T(8,128)(2,1)}, u32[]{:S(2)}) %copy-start) | copy-done | bytes 8216
  2.7 0.0 copy-start.1
  2.7 0.7 copy-done.1
  3.4 0.0 copy-start.3
  3.4 0.7 copy-done.3
  4.1 0.1 shard_map.68
  4.1 1.7 %collective-permute-done.next_ref = bf16[8,512]{1,0:T(8,128)(2,1)S(1)} collective-permute-done((bf16[8,512]{1,0:T(8,128)(2,1)}, bf16[8,512]{1,0:T(8,128)(2,1)S(1)}, u32[]{:S(2)}, u32[]{:S(2)}) %collective-permute-start) | collective-permute-done | bytes 8224 | tf_op jit(solution)/shard_map/ppermute | solution.py:290
  5.8 10.7 %shard_map.69 = (f32[776,512]{1,0:T(8,128)S(1)}, f32[776,512]{1,0:T(8,128)S(1)}, bf16[4096,512]{1,0:T(8,128)(2,1)S(1)}, bf16[2,256,8,512]{3,2,1,0:T(8,128)(2,1)S(1)}) custom-call(s32[4]{0:T(128)S(1)} %pad_add_fusion.here_ref, bf16[8,512]{1,0:T(8,128)(2,1)S(1)} %get-tuple-element.18.wave_ref, bf16[8,512]{1,0:T(8,128)(2,1)S(1)} %collective-permute-done.next_ref, ...), custom_call_target="tpu_custom_call" | custom-call | flops 6442450944 | bytes 12582912 | tf_op jit(solution)/shard_map/pallas_call | solution.py:308
  16.5 2.1 %collective-permute-start.2 = (f32[776,512]{1,0:T(8,128)S(1)}, f32[776,512]{1,0:T(8,128)S(1)}, u32[]{:S(2)}, u32[]{:S(2)}) collective-permute-start(f32[776,512]{1,0:T(8,128)S(1)} %get-tuple-element.25), channel_id=1, source_target_pairs={{0,1},{1,0},{2,3},{3,2},{4,5},{5,4},{6,7},{7,6},{8,9},{9,8},{10,11... | collective-permute-start | bytes 4767752 | tf_op jit(solution)/shard_map/ppermute | solution.py:333
  18.6 0.0 copy-start.2
  18.6 2.6 %shard_map.70 = (f32[256,512]{1,0:T(8,128)S(1)}, f32[256,512]{1,0:T(8,128)S(1)}) custom-call(bf16[2,256,8,512]{3,2,1,0:T(8,128)(2,1)S(1)} %get-tuple-element.20.own_ref, bf16[4096,512]{1,0:T(8,128)(2,1)S(1)} %get-tuple-element.21.sliding_ref), custom_call_target="tpu_custom_call" | custom-call | flops 2147483648 | bytes 1048576 | tf_op jit(solution)/shard_map/pallas_call | solution.py:25
  21.2 0.0 copy-start.4
  21.2 0.0 copy-start.5
  21.2 0.3 collective-permute-start.1
  21.5 0.1 collective-permute-done.2.came_ref
  21.7 0.9 %shard_map.71 = (f32[8,512]{1,0:T(8,128)S(1)}, s32[64,1,128]{2,1,0:T(1,128)}, s32[136,512]{1,0:T(8,128)S(1)}, s32[136,512]{1,0:T(8,128)S(1)}, s32[136,512]{1,0:T(8,128)S(1)}) custom-call(f32[776,512]{1,0:T(8,128)S(1)} %get-tuple-element.24.keep_ref, f32[776,512]{1,0:T(8,128)S(1)} %collective-permute-done.2.came_ref), custom_call_target="tpu_custom_call" | custom-call | flops 4194304 | bytes 1048576 | tf_op jit(solution)/shard_map/pallas_call | solution.py:25
  22.5 3.7 %collective-permute-start.3 = (s32[136,512]{1,0:T(8,128)S(1)}, s32[136,512]{1,0:T(8,128)S(1)}, u32[]{:S(2)}, u32[]{:S(2)}) collective-permute-start(s32[136,512]{1,0:T(8,128)S(1)} %get-tuple-element.28), channel_id=1, source_target_pairs={{0,4},{2,6},{4,0},{6,2},{1,5},{3,7},{5,1},{7,3},{8,12},{10,14},{12... | collective-permute-start | bytes 835592 | tf_op jit(solution)/shard_map/ppermute | solution.py:330
  26.2 0.7 %collective-permute-start.4 = (s32[136,512]{1,0:T(8,128)S(1)}, s32[136,512]{1,0:T(8,128)S(1)}, u32[]{:S(2)}, u32[]{:S(2)}) collective-permute-start(s32[136,512]{1,0:T(8,128)S(1)} %get-tuple-element.29), channel_id=1, source_target_pairs={{0,2},{2,4},{4,6},{6,0},{1,3},{3,5},{5,7},{7,1},{8,10},{10,12},{12... | collective-permute-start | bytes 835592 | tf_op jit(solution)/shard_map/ppermute | solution.py:330
  26.9 1.9 %collective-permute-start.5 = (s32[136,512]{1,0:T(8,128)S(1)}, s32[136,512]{1,0:T(8,128)S(1)}, u32[]{:S(2)}, u32[]{:S(2)}) collective-permute-start(s32[136,512]{1,0:T(8,128)S(1)} %get-tuple-element.30), channel_id=1, source_target_pairs={{0,6},{2,0},{4,2},{6,4},{1,7},{3,1},{5,3},{7,5},{8,14},{10,8},{12,... | collective-permute-start | bytes 835592 | tf_op jit(solution)/shard_map/ppermute | solution.py:330
  28.9 9.5 %all-to-all-start = ((s32[64,1,128]{2,1,0:T(1,128)}), s32[64,1,128]{2,1,0:T(1,128)S(1)}, u32[]{:S(2)}, u32[]{:S(2)}) async-start(s32[64,1,128]{2,1,0:T(1,128)} %get-tuple-element.31), calls=%async_computation | async-start | bytes 65536 | tf_op jit(solution)/shard_map/all_to_all | solution.py:350
  38.4 0.0 collective-permute-done.1.came_ref
  38.4 8.3 %all-to-all-done.info_ref = s32[64,1,128]{2,1,0:T(1,128)S(1)} async-done(((s32[64,1,128]{2,1,0:T(1,128)}), s32[64,1,128]{2,1,0:T(1,128)S(1)}, u32[]{:S(2)}, u32[]{:S(2)}) %all-to-all-start) | async-done | bytes 32800 | tf_op jit(solution)/shard_map/all_to_all | solution.py:350
  46.7 0.0 collective-permute-done.3.a_ref
  46.7 0.0 collective-permute-done.4.b_ref
  46.7 0.0 collective-permute-done.5.c_ref
  46.7 0.0 copy-done.2
  46.7 2.2 %shard_map.72 = (f32[256,512]{1,0:T(8,128)S(1)}, f32[512,128]{1,0:T(8,128)}) custom-call(s32[4]{0:T(128)S(1)} %pad_add_fusion.here_ref, f32[256,512]{1,0:T(8,128)S(1)} %get-tuple-element.22.keep_ref, f32[256,512]{1,0:T(8,128)S(1)} %collective-permute-done.1.came_ref, f32[8,512]{1,0:T(8,128)S(1)} %get-tuple-element.27.energy_ref, ...), custom_call_target="tpu_custom_call" | custom-call | flops 16777216 | bytes 1048576 | tf_op jit(solution)/shard_map/pallas_call | solution.py:25
  48.9 6.2 %all-to-all-start.1 = ((f32[128,4,128]{2,1,0:T(4,128)}), f32[128,4,128]{2,1,0:T(4,128)S(1)}, u32[]{:S(2)}, u32[]{:S(2)}) async-start(f32[128,4,128]{2,1,0:T(4,128)} %bitcast.5), calls=%async_computation.1 | async-start | bytes 524288 | tf_op jit(solution)/shard_map/all_to_all | solution.py:366
  55.1 0.8 %copy.7 = f32[256,512]{1,0:T(8,128)} copy(f32[256,512]{1,0:T(8,128)S(1)} %get-tuple-element.34) | data formatting | bytes 1048576
  55.9 9.8 %all-to-all-done.1 = f32[128,4,128]{2,1,0:T(4,128)S(1)} async-done(((f32[128,4,128]{2,1,0:T(4,128)}), f32[128,4,128]{2,1,0:T(4,128)S(1)}, u32[]{:S(2)}, u32[]{:S(2)}) %all-to-all-start.1) | async-done | bytes 262176 | tf_op jit(solution)/shard_map/all_to_all | solution.py:366
  65.7 0.0 copy-done.4
  65.7 0.0 copy-done.5
  65.7 2.8 %shard_map.73 = f32[16,128]{1,0:T(8,128)} custom-call(s32[4]{0:T(128)S(1)} %pad_add_fusion.here_ref, s32[16]{0:T(128)S(1)} %copy-done.5, s32[2,16]{1,0:T(2,128)S(1)} %bitcast.11, s32[64,1,128]{2,1,0:T(1,128)S(1)} %all-to-all-done.info_ref, f32[512,128]{1,0:T(8,128)S(1)} %bitcast.7), custom_call_target="tpu_custom_call" | custom-call | flops 16777216 | bytes 1048576 | tf_op jit(solution)/shard_map/pallas_call | solution.py:25
Async XLA Ops:
  0.6 5.2 %collective-permute-start = (bf16[8,512]{1,0:T(8,128)(2,1)}, bf16[8,512]{1,0:T(8,128)(2,1)S(1)}, u32[]{:S(2)}, u32[]{:S(2)}) collective-permute-start(bf16[8,512]{1,0:T(8,128)(2,1)} %wave_ref.1), channel_id=1, source_target_pairs={{8,0},{16,8},{24,16},{32,24},{40,32},{48,40},{56,48},{64,56},{72,6... | collective-permute-start | bytes 24584 | tf_op jit(solution)/shard_map/ppermute | solution.py:290
  2.0 0.7 %copy-start = (bf16[8,512]{1,0:T(8,128)(2,1)S(1)}, bf16[8,512]{1,0:T(8,128)(2,1)}, u32[]{:S(2)}) copy-start(bf16[8,512]{1,0:T(8,128)(2,1)} %wave_ref.1) | copy-start | bytes 24580
  2.7 0.7 copy-start.1
  3.4 0.7 copy-start.3
  16.5 5.1 %collective-permute-start.2 = (f32[776,512]{1,0:T(8,128)S(1)}, f32[776,512]{1,0:T(8,128)S(1)}, u32[]{:S(2)}, u32[]{:S(2)}) collective-permute-start(f32[776,512]{1,0:T(8,128)S(1)} %get-tuple-element.25), channel_id=1, source_target_pairs={{0,1},{1,0},{2,3},{3,2},{4,5},{5,4},{6,7},{7,6},{8,9},{9,8},{10,11... | collective-permute-start | bytes 4767752 | tf_op jit(solution)/shard_map/ppermute | solution.py:333
  18.6 28.1 %copy-start.2 = (s32[256,1]{0,1:T(1,128)S(1)}, s32[256,1]{0,1:T(1,128)}, u32[]{:S(2)}) copy-start(s32[256,1]{0,1:T(1,128)} %param.7) | copy-start | bytes 3076
  21.2 44.5 %copy-start.4 = (s32[16,2]{0,1:T(2,128)S(1)}, s32[16,2]{0,1:T(2,128)}, u32[]{:S(2)}) copy-start(s32[16,2]{0,1:T(2,128)} %param.8) | copy-start | bytes 388
  21.2 44.5 %copy-start.5 = (s32[16]{0:T(128)S(1)}, s32[16]{0:T(128)}, u32[]{:S(2)}) copy-start(s32[16]{0:T(128)} %lags_ref.1) | copy-start | bytes 196
  21.2 17.1 %collective-permute-start.1 = (f32[256,512]{1,0:T(8,128)S(1)}, f32[256,512]{1,0:T(8,128)S(1)}, u32[]{:S(2)}, u32[]{:S(2)}) collective-permute-start(f32[256,512]{1,0:T(8,128)S(1)} %get-tuple-element.23), channel_id=1, source_target_pairs={{0,1},{1,0},{2,3},{3,2},{4,5},{5,4},{6,7},{7,6},{8,9},{9,8},{10,11... | collective-permute-start | bytes 1572872 | tf_op jit(solution)/shard_map/ppermute | solution.py:333
  22.5 24.2 %collective-permute-start.3 = (s32[136,512]{1,0:T(8,128)S(1)}, s32[136,512]{1,0:T(8,128)S(1)}, u32[]{:S(2)}, u32[]{:S(2)}) collective-permute-start(s32[136,512]{1,0:T(8,128)S(1)} %get-tuple-element.28), channel_id=1, source_target_pairs={{0,4},{2,6},{4,0},{6,2},{1,5},{3,7},{5,1},{7,3},{8,12},{10,14},{12... | collective-permute-start | bytes 835592 | tf_op jit(solution)/shard_map/ppermute | solution.py:330
  26.2 20.5 %collective-permute-start.4 = (s32[136,512]{1,0:T(8,128)S(1)}, s32[136,512]{1,0:T(8,128)S(1)}, u32[]{:S(2)}, u32[]{:S(2)}) collective-permute-start(s32[136,512]{1,0:T(8,128)S(1)} %get-tuple-element.29), channel_id=1, source_target_pairs={{0,2},{2,4},{4,6},{6,0},{1,3},{3,5},{5,7},{7,1},{8,10},{10,12},{12... | collective-permute-start | bytes 835592 | tf_op jit(solution)/shard_map/ppermute | solution.py:330
  26.9 19.8 %collective-permute-start.5 = (s32[136,512]{1,0:T(8,128)S(1)}, s32[136,512]{1,0:T(8,128)S(1)}, u32[]{:S(2)}, u32[]{:S(2)}) collective-permute-start(s32[136,512]{1,0:T(8,128)S(1)} %get-tuple-element.30), channel_id=1, source_target_pairs={{0,6},{2,0},{4,2},{6,4},{1,7},{3,1},{5,3},{7,5},{8,14},{10,8},{12,... | collective-permute-start | bytes 835592 | tf_op jit(solution)/shard_map/ppermute | solution.py:330
  28.9 17.8 %all-to-all-start = ((s32[64,1,128]{2,1,0:T(1,128)}), s32[64,1,128]{2,1,0:T(1,128)S(1)}, u32[]{:S(2)}, u32[]{:S(2)}) async-start(s32[64,1,128]{2,1,0:T(1,128)} %get-tuple-element.31), calls=%async_computation | async-start | bytes 65536 | tf_op jit(solution)/shard_map/all_to_all | solution.py:350
  48.9 16.8 %all-to-all-start.1 = ((f32[128,4,128]{2,1,0:T(4,128)}), f32[128,4,128]{2,1,0:T(4,128)S(1)}, u32[]{:S(2)}, u32[]{:S(2)}) async-start(f32[128,4,128]{2,1,0:T(4,128)} %bitcast.5), calls=%async_computation.1 | async-start | bytes 524288 | tf_op jit(solution)/shard_map/all_to_all | solution.py:366

commit v6 on v5

--- a/solution.py
+++ b/solution.py
@@ -131,8 +131,7 @@
     words = [ref[last + WORDS : last + WORDS + 1, :LANES].astype(jnp.int32) for ref in (keep_ref, came_ref)]
     lane = lax.broadcasted_iota(jnp.int32, (1, LANES), 1)
     words = jnp.where(lane < SLOT, words[0], pltpu.roll(words[1], SLOT, 1))
-    words = jnp.concatenate([words] * (note_ref.shape[2] // LANES), axis=1)
-    note_ref[...] = jnp.broadcast_to(words[None], note_ref.shape)
+    note_ref[...] = jnp.broadcast_to(words, note_ref.shape)
     logarithm = jnp.log2(jnp.maximum(energy, 1e-30))
     sample = jnp.round(4.0 * logarithm)
     level = jnp.exp2(sample[:1] * -0.125)
@@ -180,7 +179,7 @@
     return high + (middle + low)
 
 
-def finish(here_ref, keep_ref, came_ref, energy_ref, a_ref, b_ref, c_ref, flags_ref, info_ref, stack_ref, windows_ref):
+def finish(keep_ref, came_ref, energy_ref, a_ref, b_ref, c_ref, flags_ref, stack_ref, parts_ref, before_ref, found_ref):
     group = stack_ref.shape[0]
     square = diagonal(group)
     stack = keep_ref[...] + came_ref[...]
@@ -191,38 +190,47 @@
         energy = energy + more
     stack = stack * (1.0 / jnp.sqrt(energy + epsilon))
     stack_ref[...] = stack
-    info = info_ref[:, 0, :LANES]
+    for i, part in enumerate(three(stack)):
+        parts_ref[i] = part
+    flags = jnp.broadcast_to(flags_ref[...], (8, group)).astype(f32)
+    earlier = lax.broadcasted_iota(jnp.int32, (group, group), 0) < lax.broadcasted_iota(
+        jnp.int32, (group, group), 1
+    )
+    before = jnp.dot(flags.astype(bf16), earlier.astype(f32).astype(bf16), preferred_element_type=f32)
+    before_ref[...] = jnp.where(flags > 0.5, before, -2.0)
+    found = jnp.sum(flags_ref[...], axis=1, keepdims=True)
+    found_ref[...] = jnp.broadcast_to(found, found_ref.shape)
+
+
+def select(here_ref, parts_ref, before_ref, found_ref, info_ref, windows_ref):
+    info = info_ref[...]
     chips = info.shape[0]
     core, here = here_ref[1], here_ref[2]
     lanes = lax.broadcasted_iota(jnp.int32, info.shape, 1)
     second = lanes >= SLOT
     device = 2 * lax.broadcasted_iota(jnp.int32, info.shape, 0) + jnp.where(second, 1 - core, core)
     word = jnp.where(second, lanes - SLOT, lanes)
-    start = jnp.sum(jnp.where((word == SLOT - 1) & (device < here), info, 0))
-    found = jnp.sum(flags_ref[...])
+    start = jnp.where((word == SLOT - 1) & (device < here), info, 0)
+    start = jnp.sum(jnp.sum(start, axis=0, keepdims=True), axis=1, keepdims=True)
+    found = found_ref[:1, :1]
     mine = (info >= start) & (info < start + found) & (word < 32)
     rank = jnp.where(mine, info - start + 1, 0)
     ranks = [jnp.sum(jnp.where(side, rank, 0), axis=1, keepdims=True) - 1 for side in (lanes < SLOT, second)]
     ranks = [jnp.where(core == 0, ranks[k], ranks[1 - k]) for k in range(2)]
     rank = jnp.concatenate(ranks, axis=0)
-    flags = jnp.broadcast_to(flags_ref[...], (8, group)).astype(f32)
-    earlier = lax.broadcasted_iota(jnp.int32, (group, group), 0) < lax.broadcasted_iota(
-        jnp.int32, (group, group), 1
-    )
-    before = jnp.dot(flags.astype(bf16), earlier.astype(f32).astype(bf16), preferred_element_type=f32)
-    before = jnp.where(flags > 0.5, before, -2.0)
-    selector = jnp.broadcast_to(before[:1], (2 * chips, group)) == rank.astype(f32)
-    windows = pick(selector.astype(f32).astype(bf16), three(stack))
+    before = jnp.broadcast_to(before_ref[:1], (2 * chips, before_ref.shape[1]))
+    selector = before == rank.astype(f32)
+    windows = pick(selector.astype(f32).astype(bf16), [parts_ref[i] for i in range(3)])
     across = BLK // LANES
     for k in range(across):
         rows = pl.ds(k, windows.shape[0], stride=across)
         windows_ref[rows, :] = windows[:, k * LANES : (k + 1) * LANES]
 
 
-def cross(here_ref, lags_ref, events_ref, info_ref, received_ref, out_ref, turned, products):
-    info = info_ref[:, 0, :LANES]
+def choose(here_ref, events_ref, info_ref, selector_ref):
+    info = info_ref[...]
     chips = info.shape[0]
-    pairs = out_ref.shape[0]
+    pairs = events_ref.shape[1]
     core = here_ref[1]
     counts = [jnp.where(core == k, info[:, SLOT - 1 : SLOT], info[:, LANES - 1 :]) for k in range(2)]
     rows = lax.broadcasted_iota(jnp.int32, (chips, 2 * chips), 0)
@@ -242,10 +250,15 @@
         ],
         axis=0,
     )
-    selector = (starts <= both) & (both < ends)
+    selector_ref[...] = ((starts <= both) & (both < ends)).astype(f32)
+
+
+def cross(lags_ref, selector_ref, received_ref, out_ref, turned, products):
+    pairs = out_ref.shape[0]
     across = BLK // LANES
-    received = [received_ref[pl.ds(k, 2 * chips, stride=across), :] for k in range(across)]
-    picked = pick(selector.astype(f32).astype(bf16), three(jnp.concatenate(received, axis=1)))
+    sources = selector_ref.shape[1]
+    received = [received_ref[pl.ds(k, sources, stride=across), :] for k in range(across)]
+    picked = pick(selector_ref[...].astype(bf16), three(jnp.concatenate(received, axis=1)))
     first, second = picked[:pairs], picked[pairs:]
     length = 2 * BLK
     nothing = jnp.zeros((pairs, BLK), f32)
@@ -337,28 +350,42 @@
     keep, send = whole(correlate_own, (shape, shape), flops, own, sliding)
     came = swap(send)
     cames, _ = lax.optimization_barrier((cames, keep))
-    shape = jax.ShapeDtypeStruct((group // 2 + 8, BLK), jnp.int32)
-    note = jax.ShapeDtypeStruct((chips, 1, LANES), jnp.int32)
+    shape = pltpu.VMEM((group // 2 + 8, BLK), jnp.int32)
+    note = pltpu.VMEM((chips, LANES), jnp.int32)
     energy, note, *codes = whole(
         merge,
-        (jax.ShapeDtypeStruct((8, BLK), f32), note) + (shape,) * len(away),
+        (pltpu.VMEM((8, BLK), f32), note) + (shape,) * len(away),
         1 << 22,
         keeps,
         cames,
     )
     arrived = [over(distance, values) for distance, values in zip(away, codes)]
-    info = lax.all_to_all(note, ("tm", "z"), 0, 0, tiled=True)
-
-    network_stack, windows = whole(
+    info = lax.all_to_all(note.reshape(chips, 1, LANES), ("tm", "z"), 0, 0, tiled=True)
+    info = info.reshape(chips, LANES)
+
+    network_stack, parts, before, found = whole(
         finish,
-        (pltpu.VMEM((group, BLK), f32), jax.ShapeDtypeStruct((2 * chips * BLK // LANES, LANES), f32)),
+        (
+            pltpu.VMEM((group, BLK), f32),
+            pltpu.VMEM((3, group, BLK), bf16),
+            pltpu.VMEM((8, group), f32),
+            pltpu.VMEM((8, LANES), jnp.int32),
+        ),
         1 << 24,
-        here,
         keep,
         came,
         energy,
         *arrived,
         flags,
+    )
+    windows = whole(
+        select,
+        pltpu.VMEM((2 * chips * BLK // LANES, LANES), f32),
+        1 << 24,
+        here,
+        parts,
+        before,
+        found,
         info,
         smem=1,
     )
@@ -366,16 +393,17 @@
     received = lax.all_to_all(windows, ("core", "tm", "z"), 0, 0, tiled=True)
     received = received.reshape(-1, LANES)
     pairs = pair_events.shape[0]
+    selector = whole(
+        choose, pltpu.VMEM((2 * pairs, 2 * chips), f32), 1 << 20, here, events, info, smem=1
+    )
     pair_cc = whole(
         cross,
         jax.ShapeDtypeStruct((pairs, NLAG), f32),
         1 << 24,
-        here,
         pair_lags,
-        events,
-        info,
+        selector,
         received,
-        smem=2,
+        smem=1,
         scratch=[
             pltpu.VMEM((NLAG // 8, pairs, NLAG + BLK), f32),
             pltpu.VMEM((pairs * NLAG, LANES), f32),

time: 68.8 us -> 68.1 us (0.990)
  waiting for transfers between devices: 20 us -> 18.6 us
    all_to_all x1, waiting for transfers between devices: 8.31 us -> 6.81 us  [shards(): lax.all_to_all(note.reshape(chips, 1, LANES), ('tm', 'z'), 0, 0, tiled=True)]
    ppermute x3, waiting for transfers between devices: 0.01 us -> 0.94 us  [over(): lax.ppermute(values, 'z', [(i, (i + distance) % planes) for i in range(pl...]
    all_to_all x1, waiting for transfers between devices: 9.83 us -> 9.1 us  [shards(): received = lax.all_to_all(windows, ('core', 'tm', 'z'), 0, 0, tiled=True)]
    pallas_call x5 -> x7, Pallas kernels: 8.53 us -> 9.11 us  [whole(): pl.pallas_call(kernel, out_shape=outs, in_specs=[SMEM] * smem + [VMEM] *...]
  transfers between devices with their start and end apart: 8 -> 8, of which waited for: 4 -> 6; matrix products, arithmetic and copies ran while one was open for 1% -> 1% of each run, Pallas kernels for 5% -> 7%
where the time goes in v6:
time: 68.1 us; the launch traced here: 67.8 us
  starting transfers between devices  25.7 us (38%)
  Pallas kernels  19.8 us (29%)
  waiting for transfers between devices  18.6 us (27%)
  local copies, waits for them, and re-layouts  2.87 us (4%)
  between operations  0.74 us (1%)
    pallas_call x1, Pallas kernels, shards(): pl.pallas_call(functools.partial(correlate, away), out_shape=(shape, shap...  10.7 us
    all_to_all x1, starting transfers between devices, shards(): lax.all_to_all(note.reshape(chips, 1, LANES), ('tm', 'z'), 0, 0, tiled=True)  9.51 us
    pallas_call x7, Pallas kernels, whole(): pl.pallas_call(kernel, out_shape=outs, in_specs=[SMEM] * smem + [VMEM] *...  9.11 us
    all_to_all x1, waiting for transfers between devices, shards(): received = lax.all_to_all(windows, ('core', 'tm', 'z'), 0, 0, tiled=True)  9.1 us
    all_to_all x1, waiting for transfers between devices, shards(): lax.all_to_all(note.reshape(chips, 1, LANES), ('tm', 'z'), 0, 0, tiled=True)  6.81 us
    ppermute x3, starting transfers between devices, over(): lax.ppermute(values, 'z', [(i, (i + distance) % planes) for i in range(pl...  6.35 us
    all_to_all x1, starting transfers between devices, shards(): received = lax.all_to_all(windows, ('core', 'tm', 'z'), 0, 0, tiled=True)  6.18 us
    unnamed x13, local copies, waits for them, and re-layouts  2.87 us
  transfers between devices with their start and end apart: 8, of which 6 were waited for; matrix products, arithmetic and copies ran while one was open for 1% of the time, Pallas kernels for 7%

profile of v6, /device:TPU:1, one launch (start us, length us, event | category | flops | bytes accessed | tf_op | source)
XLA Modules:
  0.0 67.8 jit_solution(15895206874570735682)
XLA Ops:
  0.6 1.3 %collective-permute-start = (bf16[8,512]{1,0:T(8,128)(2,1)}, bf16[8,512]{1,0:T(8,128)(2,1)S(1)}, u32[]{:S(2)}, u32[]{:S(2)}) collective-permute-start(bf16[8,512]{1,0:T(8,128)(2,1)} %wave_ref.1), channel_id=1, source_target_pairs={{8,0},{16,8},{24,16},{32,24},{40,32},{48,40},{56,48},{64,56},{72,6... | collective-permute-start | bytes 24584 | tf_op jit(solution)/shard_map/ppermute | solution.py:303
  1.9 0.1 pad_add_fusion.here_ref
  2.0 0.0 copy-start
  2.0 0.7 %copy-done = bf16[8,512]{1,0:T(8,128)(2,1)S(1)} copy-done((bf16[8,512]{1,0:T(8,128)(2,1)S(1)}, bf16[8,512]{1,0:T(8,128)(2,1)}, u32[]{:S(2)}) %copy-start) | copy-done | bytes 8216
  2.7 0.0 copy-start.1
  2.7 0.7 copy-done.1
  3.4 0.0 copy-start.3
  3.4 0.7 copy-done.3
  4.1 0.1 shard_map.68
  4.1 1.7 %collective-permute-done.next_ref = bf16[8,512]{1,0:T(8,128)(2,1)S(1)} collective-permute-done((bf16[8,512]{1,0:T(8,128)(2,1)}, bf16[8,512]{1,0:T(8,128)(2,1)S(1)}, u32[]{:S(2)}, u32[]{:S(2)}) %collective-permute-start) | collective-permute-done | bytes 8224 | tf_op jit(solution)/shard_map/ppermute | solution.py:303
  5.8 10.7 %shard_map.69 = (f32[776,512]{1,0:T(8,128)S(1)}, f32[776,512]{1,0:T(8,128)S(1)}, bf16[4096,512]{1,0:T(8,128)(2,1)S(1)}, bf16[2,256,8,512]{3,2,1,0:T(8,128)(2,1)S(1)}) custom-call(s32[4]{0:T(128)S(1)} %pad_add_fusion.here_ref, bf16[8,512]{1,0:T(8,128)(2,1)S(1)} %get-tuple-element.20.wave_ref, bf16[8,512]{1,0:T(8,128)(2,1)S(1)} %collective-permute-done.next_ref, ...), custom_call_target="tpu_custom_call" | custom-call | flops 6442450944 | bytes 12582912 | tf_op jit(solution)/shard_map/pallas_call | solution.py:321
  16.5 2.1 %collective-permute-start.2 = (f32[776,512]{1,0:T(8,128)S(1)}, f32[776,512]{1,0:T(8,128)S(1)}, u32[]{:S(2)}, u32[]{:S(2)}) collective-permute-start(f32[776,512]{1,0:T(8,128)S(1)} %get-tuple-element.27), channel_id=1, source_target_pairs={{0,1},{1,0},{2,3},{3,2},{4,5},{5,4},{6,7},{7,6},{8,9},{9,8},{10,11... | collective-permute-start | bytes 4767752 | tf_op jit(solution)/shard_map/ppermute | solution.py:346
  18.6 0.0 copy-start.2
  18.6 2.6 %shard_map.70 = (f32[256,512]{1,0:T(8,128)S(1)}, f32[256,512]{1,0:T(8,128)S(1)}) custom-call(bf16[2,256,8,512]{3,2,1,0:T(8,128)(2,1)S(1)} %get-tuple-element.22.own_ref, bf16[4096,512]{1,0:T(8,128)(2,1)S(1)} %get-tuple-element.23.sliding_ref), custom_call_target="tpu_custom_call" | custom-call | flops 2147483648 | bytes 1048576 | tf_op jit(solution)/shard_map/pallas_call | solution.py:25
  21.2 0.0 copy-start.4
  21.2 0.0 copy-start.5
  21.2 0.3 collective-permute-start.1
  21.5 0.1 collective-permute-done.2.came_ref
  21.7 0.8 %shard_map.71 = (f32[8,512]{1,0:T(8,128)S(1)}, s32[64,128]{1,0:T(8,128)}, s32[136,512]{1,0:T(8,128)S(1)}, s32[136,512]{1,0:T(8,128)S(1)}, s32[136,512]{1,0:T(8,128)S(1)}) custom-call(f32[776,512]{1,0:T(8,128)S(1)} %get-tuple-element.26.keep_ref, f32[776,512]{1,0:T(8,128)S(1)} %collective-permute-done.2.came_ref), custom_call_target="tpu_custom_call" | custom-call | flops 4194304 | bytes 1048576 | tf_op jit(solution)/shard_map/pallas_call | solution.py:25
  22.5 3.7 %collective-permute-start.3 = (s32[136,512]{1,0:T(8,128)S(1)}, s32[136,512]{1,0:T(8,128)S(1)}, u32[]{:S(2)}, u32[]{:S(2)}) collective-permute-start(s32[136,512]{1,0:T(8,128)S(1)} %get-tuple-element.30), channel_id=1, source_target_pairs={{0,4},{2,6},{4,0},{6,2},{1,5},{3,7},{5,1},{7,3},{8,12},{10,14},{12... | collective-permute-start | bytes 835592 | tf_op jit(solution)/shard_map/ppermute | solution.py:343
  26.2 0.7 %collective-permute-start.4 = (s32[136,512]{1,0:T(8,128)S(1)}, s32[136,512]{1,0:T(8,128)S(1)}, u32[]{:S(2)}, u32[]{:S(2)}) collective-permute-start(s32[136,512]{1,0:T(8,128)S(1)} %get-tuple-element.31), channel_id=1, source_target_pairs={{0,2},{2,4},{4,6},{6,0},{1,3},{3,5},{5,7},{7,1},{8,10},{10,12},{12... | collective-permute-start | bytes 835592 | tf_op jit(solution)/shard_map/ppermute | solution.py:343
  26.9 1.9 %collective-permute-start.5 = (s32[136,512]{1,0:T(8,128)S(1)}, s32[136,512]{1,0:T(8,128)S(1)}, u32[]{:S(2)}, u32[]{:S(2)}) collective-permute-start(s32[136,512]{1,0:T(8,128)S(1)} %get-tuple-element.32), channel_id=1, source_target_pairs={{0,6},{2,0},{4,2},{6,4},{1,7},{3,1},{5,3},{7,5},{8,14},{10,8},{12,... | collective-permute-start | bytes 835592 | tf_op jit(solution)/shard_map/ppermute | solution.py:343
  28.9 9.5 %all-to-all-start = ((s32[64,1,128]{2,1,0:T(1,128)}), s32[64,1,128]{2,1,0:T(1,128)S(1)}, u32[]{:S(2)}, u32[]{:S(2)}) async-start(s32[64,1,128]{2,1,0:T(1,128)} %bitcast.6), calls=%async_computation | async-start | bytes 65536 | tf_op jit(solution)/shard_map/all_to_all | solution.py:363
  38.4 0.0 collective-permute-done.1.came_ref
  38.4 0.0 collective-permute-done.3.a_ref
  38.4 0.9 %collective-permute-done.4.b_ref = s32[136,512]{1,0:T(8,128)S(1)} collective-permute-done((s32[136,512]{1,0:T(8,128)S(1)}, s32[136,512]{1,0:T(8,128)S(1)}, u32[]{:S(2)}, u32[]{:S(2)}) %collective-permute-start.4) | collective-permute-done | bytes 278560 | tf_op jit(solution)/shard_map/ppermute | solution.py:343
  39.3 0.1 collective-permute-done.5.c_ref
  39.3 0.0 copy-done.2
  39.3 0.6 shard_map.72
  39.9 6.8 %all-to-all-done = s32[64,1,128]{2,1,0:T(1,128)S(1)} async-done(((s32[64,1,128]{2,1,0:T(1,128)}), s32[64,1,128]{2,1,0:T(1,128)S(1)}, u32[]{:S(2)}, u32[]{:S(2)}) %all-to-all-start) | async-done | bytes 32800 | tf_op jit(solution)/shard_map/all_to_all | solution.py:363
  46.7 1.8 %shard_map.74 = f32[512,128]{1,0:T(8,128)} custom-call(s32[4]{0:T(128)S(1)} %pad_add_fusion.here_ref, bf16[3,256,512]{2,1,0:T(8,128)(2,1)S(1)} %get-tuple-element.35.parts_ref, f32[8,256]{1,0:T(8,128)S(1)} %get-tuple-element.36.before_ref, s32[8,128]{1,0:T(8,128)S(1)} %get-tuple-element.37.found_ref, s32[64,128]{1,0:T(8,128)S(1)} %bitcast.12), custom_call_target="tpu_custom_call" | custom-call | flops 16777216 | bytes 1048576 | tf_op jit(solution)/shard_map/pallas_call | solution.py:25
  48.5 6.2 %all-to-all-start.1 = ((f32[128,4,128]{2,1,0:T(4,128)}), f32[128,4,128]{2,1,0:T(4,128)S(1)}, u32[]{:S(2)}, u32[]{:S(2)}) async-start(f32[128,4,128]{2,1,0:T(4,128)} %bitcast.8), calls=%async_computation.1 | async-start | bytes 524288 | tf_op jit(solution)/shard_map/all_to_all | solution.py:393
  54.7 0.0 copy-done.4
  54.7 0.7 %shard_map.73.selector_ref = f32[32,128]{1,0:T(8,128)S(1)} custom-call(s32[4]{0:T(128)S(1)} %pad_add_fusion.here_ref, s32[2,16]{1,0:T(2,128)S(1)} %bitcast.17, s32[64,128]{1,0:T(8,128)S(1)} %bitcast.13), custom_call_target="tpu_custom_call" | custom-call | flops 1048576 | bytes 1048576 | tf_op jit(solution)/shard_map/pallas_call | solution.py:25
  55.4 0.8 %copy.8 = f32[256,512]{1,0:T(8,128)} copy(f32[256,512]{1,0:T(8,128)S(1)} %get-tuple-element.38) | data formatting | bytes 1048576
  56.2 9.1 %all-to-all-done.1 = f32[128,4,128]{2,1,0:T(4,128)S(1)} async-done(((f32[128,4,128]{2,1,0:T(4,128)}), f32[128,4,128]{2,1,0:T(4,128)S(1)}, u32[]{:S(2)}, u32[]{:S(2)}) %all-to-all-start.1) | async-done | bytes 262176 | tf_op jit(solution)/shard_map/all_to_all | solution.py:393
  65.3 0.0 copy-done.5
  65.3 2.5 %shard_map.75 = f32[16,128]{1,0:T(8,128)} custom-call(s32[16]{0:T(128)S(1)} %copy-done.5, f32[32,128]{1,0:T(8,128)S(1)} %shard_map.73.selector_ref, f32[512,128]{1,0:T(8,128)S(1)} %bitcast.11), custom_call_target="tpu_custom_call" | custom-call | flops 16777216 | bytes 1048576 | tf_op jit(solution)/shard_map/pallas_call | solution.py:25
Async XLA Ops:
  0.6 5.2 %collective-permute-start = (bf16[8,512]{1,0:T(8,128)(2,1)}, bf16[8,512]{1,0:T(8,128)(2,1)S(1)}, u32[]{:S(2)}, u32[]{:S(2)}) collective-permute-start(bf16[8,512]{1,0:T(8,128)(2,1)} %wave_ref.1), channel_id=1, source_target_pairs={{8,0},{16,8},{24,16},{32,24},{40,32},{48,40},{56,48},{64,56},{72,6... | collective-permute-start | bytes 24584 | tf_op jit(solution)/shard_map/ppermute | solution.py:303
  2.0 0.7 %copy-start = (bf16[8,512]{1,0:T(8,128)(2,1)S(1)}, bf16[8,512]{1,0:T(8,128)(2,1)}, u32[]{:S(2)}) copy-start(bf16[8,512]{1,0:T(8,128)(2,1)} %wave_ref.1) | copy-start | bytes 24580
  2.7 0.7 %copy-start.1 = (s32[256,1]{0,1:T(1,128)S(1)}, s32[256,1]{0,1:T(1,128)}, u32[]{:S(2)}) copy-start(s32[256,1]{0,1:T(1,128)} %param.7) | copy-start | bytes 3076
  3.4 0.7 %copy-start.3 = (s32[16,2]{0,1:T(2,128)S(1)}, s32[16,2]{0,1:T(2,128)}, u32[]{:S(2)}) copy-start(s32[16,2]{0,1:T(2,128)} %param.8) | copy-start | bytes 388
  16.5 5.1 %collective-permute-start.2 = (f32[776,512]{1,0:T(8,128)S(1)}, f32[776,512]{1,0:T(8,128)S(1)}, u32[]{:S(2)}, u32[]{:S(2)}) collective-permute-start(f32[776,512]{1,0:T(8,128)S(1)} %get-tuple-element.27), channel_id=1, source_target_pairs={{0,1},{1,0},{2,3},{3,2},{4,5},{5,4},{6,7},{7,6},{8,9},{9,8},{10,11... | collective-permute-start | bytes 4767752 | tf_op jit(solution)/shard_map/ppermute | solution.py:346
  18.6 20.7 %copy-start.2 = (s32[256,1]{0,1:T(1,128)S(1)}, s32[256,1]{0,1:T(1,128)}, u32[]{:S(2)}) copy-start(s32[256,1]{0,1:T(1,128)} %param.7) | copy-start | bytes 3076
  21.2 33.5 %copy-start.4 = (s32[16,2]{0,1:T(2,128)S(1)}, s32[16,2]{0,1:T(2,128)}, u32[]{:S(2)}) copy-start(s32[16,2]{0,1:T(2,128)} %param.8) | copy-start | bytes 388
  21.2 44.1 %copy-start.5 = (s32[16]{0:T(128)S(1)}, s32[16]{0:T(128)}, u32[]{:S(2)}) copy-start(s32[16]{0:T(128)} %lags_ref.1) | copy-start | bytes 196
  21.2 17.1 %collective-permute-start.1 = (f32[256,512]{1,0:T(8,128)S(1)}, f32[256,512]{1,0:T(8,128)S(1)}, u32[]{:S(2)}, u32[]{:S(2)}) collective-permute-start(f32[256,512]{1,0:T(8,128)S(1)} %get-tuple-element.25), channel_id=1, source_target_pairs={{0,1},{1,0},{2,3},{3,2},{4,5},{5,4},{6,7},{7,6},{8,9},{9,8},{10,11... | collective-permute-start | bytes 1572872 | tf_op jit(solution)/shard_map/ppermute | solution.py:346
  22.5 15.9 %collective-permute-start.3 = (s32[136,512]{1,0:T(8,128)S(1)}, s32[136,512]{1,0:T(8,128)S(1)}, u32[]{:S(2)}, u32[]{:S(2)}) collective-permute-start(s32[136,512]{1,0:T(8,128)S(1)} %get-tuple-element.30), channel_id=1, source_target_pairs={{0,4},{2,6},{4,0},{6,2},{1,5},{3,7},{5,1},{7,3},{8,12},{10,14},{12... | collective-permute-start | bytes 835592 | tf_op jit(solution)/shard_map/ppermute | solution.py:343
  26.2 13.1 %collective-permute-start.4 = (s32[136,512]{1,0:T(8,128)S(1)}, s32[136,512]{1,0:T(8,128)S(1)}, u32[]{:S(2)}, u32[]{:S(2)}) collective-permute-start(s32[136,512]{1,0:T(8,128)S(1)} %get-tuple-element.31), channel_id=1, source_target_pairs={{0,2},{2,4},{4,6},{6,0},{1,3},{3,5},{5,7},{7,1},{8,10},{10,12},{12... | collective-permute-start | bytes 835592 | tf_op jit(solution)/shard_map/ppermute | solution.py:343
  26.9 12.4 %collective-permute-start.5 = (s32[136,512]{1,0:T(8,128)S(1)}, s32[136,512]{1,0:T(8,128)S(1)}, u32[]{:S(2)}, u32[]{:S(2)}) collective-permute-start(s32[136,512]{1,0:T(8,128)S(1)} %get-tuple-element.32), channel_id=1, source_target_pairs={{0,6},{2,0},{4,2},{6,4},{1,7},{3,1},{5,3},{7,5},{8,14},{10,8},{12,... | collective-permute-start | bytes 835592 | tf_op jit(solution)/shard_map/ppermute | solution.py:343
  28.9 17.8 %all-to-all-start = ((s32[64,1,128]{2,1,0:T(1,128)}), s32[64,1,128]{2,1,0:T(1,128)S(1)}, u32[]{:S(2)}, u32[]{:S(2)}) async-start(s32[64,1,128]{2,1,0:T(1,128)} %bitcast.6), calls=%async_computation | async-start | bytes 65536 | tf_op jit(solution)/shard_map/all_to_all | solution.py:363
  48.5 16.8 %all-to-all-start.1 = ((f32[128,4,128]{2,1,0:T(4,128)}), f32[128,4,128]{2,1,0:T(4,128)S(1)}, u32[]{:S(2)}, u32[]{:S(2)}) async-start(f32[128,4,128]{2,1,0:T(4,128)} %bitcast.8), calls=%async_computation.1 | async-start | bytes 524288 | tf_op jit(solution)/shard_map/all_to_all | solution.py:393

commit v7 on v6

--- a/solution.py
+++ b/solution.py
@@ -175,8 +175,7 @@
 
 
 def pick(selector, parts):
-    high, middle, low = [jnp.dot(selector, part, preferred_element_type=f32) for part in parts]
-    return high + (middle + low)
+    return jnp.dot(jnp.concatenate([selector] * 3, axis=1), parts, preferred_element_type=f32)
 
 
 def finish(keep_ref, came_ref, energy_ref, a_ref, b_ref, c_ref, flags_ref, stack_ref, parts_ref, before_ref, found_ref):
@@ -190,8 +189,7 @@
         energy = energy + more
     stack = stack * (1.0 / jnp.sqrt(energy + epsilon))
     stack_ref[...] = stack
-    for i, part in enumerate(three(stack)):
-        parts_ref[i] = part
+    parts_ref[...] = jnp.concatenate(three(stack), axis=0)
     flags = jnp.broadcast_to(flags_ref[...], (8, group)).astype(f32)
     earlier = lax.broadcasted_iota(jnp.int32, (group, group), 0) < lax.broadcasted_iota(
         jnp.int32, (group, group), 1
@@ -220,7 +218,7 @@
     rank = jnp.concatenate(ranks, axis=0)
     before = jnp.broadcast_to(before_ref[:1], (2 * chips, before_ref.shape[1]))
     selector = before == rank.astype(f32)
-    windows = pick(selector.astype(f32).astype(bf16), [parts_ref[i] for i in range(3)])
+    windows = pick(selector.astype(f32).astype(bf16), parts_ref[...])
     across = BLK // LANES
     for k in range(across):
         rows = pl.ds(k, windows.shape[0], stride=across)
@@ -258,7 +256,7 @@
     across = BLK // LANES
     sources = selector_ref.shape[1]
     received = [received_ref[pl.ds(k, sources, stride=across), :] for k in range(across)]
-    picked = pick(selector_ref[...].astype(bf16), three(jnp.concatenate(received, axis=1)))
+    picked = pick(selector_ref[...].astype(bf16), jnp.concatenate(three(jnp.concatenate(received, axis=1)), axis=0))
     first, second = picked[:pairs], picked[pairs:]
     length = 2 * BLK
     nothing = jnp.zeros((pairs, BLK), f32)
@@ -314,7 +312,7 @@
     )
 
     stations = templates.shape[1]
-    away = (2, 1, 3)
+    away = (1, 3, 2)
     any_space = pl.BlockSpec(memory_space=pl.ANY)
     flops = 4 * group * stations * TLEN * BLK
     shape = pltpu.VMEM((len(away) * group + 8, BLK), f32)
@@ -367,7 +365,7 @@
         finish,
         (
             pltpu.VMEM((group, BLK), f32),
-            pltpu.VMEM((3, group, BLK), bf16),
+            pltpu.VMEM((3 * group, BLK), bf16),
             pltpu.VMEM((8, group), f32),
             pltpu.VMEM((8, LANES), jnp.int32),
         ),

time: 68.1 us -> 68 us (level)
    all_to_all x1, starting transfers between devices: 9.51 us -> 10.9 us  [shards(): lax.all_to_all(note.reshape(chips, 1, LANES), ('tm', 'z'), 0, 0, tiled=True)]
    ppermute x3, starting transfers between devices: 6.35 us -> 5.14 us  [over(): lax.ppermute(values, 'z', [(i, (i + distance) % planes) for i in range(pl...]
  transfers between devices with their start and end apart: 8 -> 8, of which waited for: 6 -> 5; matrix products, arithmetic and copies ran while one was open for 1% -> 1% of each run, Pallas kernels for 7% -> 7%
where the time goes in v7:
time: 68 us; the launch traced here: 67.7 us
  starting transfers between devices  25.6 us (38%)
  Pallas kernels  19.8 us (29%)
  waiting for transfers between devices  18.6 us (27%)
  local copies, waits for them, and re-layouts  2.87 us (4%)
  between operations  0.75 us (1%)
    all_to_all x1, starting transfers between devices, shards(): lax.all_to_all(note.reshape(chips, 1, LANES), ('tm', 'z'), 0, 0, tiled=True)  10.9 us
    pallas_call x1, Pallas kernels, shards(): pl.pallas_call(functools.partial(correlate, away), out_shape=(shape, shap...  10.7 us
    all_to_all x1, waiting for transfers between devices, shards(): received = lax.all_to_all(windows, ('core', 'tm', 'z'), 0, 0, tiled=True)  9.1 us
    pallas_call x7, Pallas kernels, whole(): pl.pallas_call(kernel, out_shape=outs, in_specs=[SMEM] * smem + [VMEM] *...  9.08 us
    all_to_all x1, waiting for transfers between devices, shards(): lax.all_to_all(note.reshape(chips, 1, LANES), ('tm', 'z'), 0, 0, tiled=True)  6.41 us
    all_to_all x1, starting transfers between devices, shards(): received = lax.all_to_all(windows, ('core', 'tm', 'z'), 0, 0, tiled=True)  5.9 us
    ppermute x3, starting transfers between devices, over(): lax.ppermute(values, 'z', [(i, (i + distance) % planes) for i in range(pl...  5.14 us
    unnamed x13, local copies, waits for them, and re-layouts  2.87 us
  transfers between devices with their start and end apart: 8, of which 5 were waited for; matrix products, arithmetic and copies ran while one was open for 1% of the time, Pallas kernels for 7%

profile of v7, /device:TPU:1, one launch (start us, length us, event | category | flops | bytes accessed | tf_op | source)
XLA Modules:
  0.0 67.7 jit_solution(8338516904818823554)
XLA Ops:
  0.6 1.3 %collective-permute-start = (bf16[8,512]{1,0:T(8,128)(2,1)}, bf16[8,512]{1,0:T(8,128)(2,1)S(1)}, u32[]{:S(2)}, u32[]{:S(2)}) collective-permute-start(bf16[8,512]{1,0:T(8,128)(2,1)} %wave_ref.1), channel_id=1, source_target_pairs={{8,0},{16,8},{24,16},{32,24},{40,32},{48,40},{56,48},{64,56},{72,6... | collective-permute-start | bytes 24584 | tf_op jit(solution)/shard_map/ppermute | solution.py:301
  1.9 0.1 pad_add_fusion.here_ref
  2.0 0.0 copy-start
  2.0 0.7 %copy-done = bf16[8,512]{1,0:T(8,128)(2,1)S(1)} copy-done((bf16[8,512]{1,0:T(8,128)(2,1)S(1)}, bf16[8,512]{1,0:T(8,128)(2,1)}, u32[]{:S(2)}) %copy-start) | copy-done | bytes 8216
  2.7 0.0 copy-start.1
  2.7 0.7 %copy-done.1 = s32[256,1]{0,1:T(1,128)S(1)} copy-done((s32[256,1]{0,1:T(1,128)S(1)}, s32[256,1]{0,1:T(1,128)}, u32[]{:S(2)}) %copy-start.1) | copy-done | bytes 1048
  3.4 0.0 copy-start.3
  3.4 0.7 %copy-done.3 = s32[16,2]{0,1:T(2,128)S(1)} copy-done((s32[16,2]{0,1:T(2,128)S(1)}, s32[16,2]{0,1:T(2,128)}, u32[]{:S(2)}) %copy-start.3) | copy-done | bytes 152
  4.1 0.1 shard_map.68
  4.1 1.7 %collective-permute-done.next_ref = bf16[8,512]{1,0:T(8,128)(2,1)S(1)} collective-permute-done((bf16[8,512]{1,0:T(8,128)(2,1)}, bf16[8,512]{1,0:T(8,128)(2,1)S(1)}, u32[]{:S(2)}, u32[]{:S(2)}) %collective-permute-start) | collective-permute-done | bytes 8224 | tf_op jit(solution)/shard_map/ppermute | solution.py:301
  5.8 10.7 %shard_map.69 = (f32[776,512]{1,0:T(8,128)S(1)}, f32[776,512]{1,0:T(8,128)S(1)}, bf16[4096,512]{1,0:T(8,128)(2,1)S(1)}, bf16[2,256,8,512]{3,2,1,0:T(8,128)(2,1)S(1)}) custom-call(s32[4]{0:T(128)S(1)} %pad_add_fusion.here_ref, bf16[8,512]{1,0:T(8,128)(2,1)S(1)} %get-tuple-element.20.wave_ref, bf16[8,512]{1,0:T(8,128)(2,1)S(1)} %collective-permute-done.next_ref, ...), custom_call_target="tpu_custom_call" | custom-call | flops 6442450944 | bytes 12582912 | tf_op jit(solution)/shard_map/pallas_call | solution.py:319
  16.5 2.1 %collective-permute-start.2 = (f32[776,512]{1,0:T(8,128)S(1)}, f32[776,512]{1,0:T(8,128)S(1)}, u32[]{:S(2)}, u32[]{:S(2)}) collective-permute-start(f32[776,512]{1,0:T(8,128)S(1)} %get-tuple-element.27), channel_id=1, source_target_pairs={{0,1},{1,0},{2,3},{3,2},{4,5},{5,4},{6,7},{7,6},{8,9},{9,8},{10,11... | collective-permute-start | bytes 4767752 | tf_op jit(solution)/shard_map/ppermute | solution.py:344
  18.6 0.0 copy-start.2
  18.6 2.6 %shard_map.70 = (f32[256,512]{1,0:T(8,128)S(1)}, f32[256,512]{1,0:T(8,128)S(1)}) custom-call(bf16[2,256,8,512]{3,2,1,0:T(8,128)(2,1)S(1)} %get-tuple-element.22.own_ref, bf16[4096,512]{1,0:T(8,128)(2,1)S(1)} %get-tuple-element.23.sliding_ref), custom_call_target="tpu_custom_call" | custom-call | flops 2147483648 | bytes 1048576 | tf_op jit(solution)/shard_map/pallas_call | solution.py:25
  21.2 0.0 copy-start.4
  21.2 0.0 copy-start.5
  21.2 0.3 collective-permute-start.1
  21.5 0.1 collective-permute-done.2.came_ref
  21.7 0.8 %shard_map.71 = (f32[8,512]{1,0:T(8,128)S(1)}, s32[64,128]{1,0:T(8,128)}, s32[136,512]{1,0:T(8,128)S(1)}, s32[136,512]{1,0:T(8,128)S(1)}, s32[136,512]{1,0:T(8,128)S(1)}) custom-call(f32[776,512]{1,0:T(8,128)S(1)} %get-tuple-element.26.keep_ref, f32[776,512]{1,0:T(8,128)S(1)} %collective-permute-done.2.came_ref), custom_call_target="tpu_custom_call" | custom-call | flops 4194304 | bytes 1048576 | tf_op jit(solution)/shard_map/pallas_call | solution.py:25
  22.5 1.7 %collective-permute-start.3 = (s32[136,512]{1,0:T(8,128)S(1)}, s32[136,512]{1,0:T(8,128)S(1)}, u32[]{:S(2)}, u32[]{:S(2)}) collective-permute-start(s32[136,512]{1,0:T(8,128)S(1)} %get-tuple-element.30), channel_id=1, source_target_pairs={{0,2},{2,4},{4,6},{6,0},{1,3},{3,5},{5,7},{7,1},{8,10},{10,12},{12... | collective-permute-start | bytes 835592 | tf_op jit(solution)/shard_map/ppermute | solution.py:341
  24.2 2.1 %collective-permute-start.4 = (s32[136,512]{1,0:T(8,128)S(1)}, s32[136,512]{1,0:T(8,128)S(1)}, u32[]{:S(2)}, u32[]{:S(2)}) collective-permute-start(s32[136,512]{1,0:T(8,128)S(1)} %get-tuple-element.31), channel_id=1, source_target_pairs={{0,6},{2,0},{4,2},{6,4},{1,7},{3,1},{5,3},{7,5},{8,14},{10,8},{12,... | collective-permute-start | bytes 835592 | tf_op jit(solution)/shard_map/ppermute | solution.py:341
  26.3 1.3 %collective-permute-start.5 = (s32[136,512]{1,0:T(8,128)S(1)}, s32[136,512]{1,0:T(8,128)S(1)}, u32[]{:S(2)}, u32[]{:S(2)}) collective-permute-start(s32[136,512]{1,0:T(8,128)S(1)} %get-tuple-element.32), channel_id=1, source_target_pairs={{0,4},{2,6},{4,0},{6,2},{1,5},{3,7},{5,1},{7,3},{8,12},{10,14},{12... | collective-permute-start | bytes 835592 | tf_op jit(solution)/shard_map/ppermute | solution.py:341
  27.6 10.9 %all-to-all-start = ((s32[64,1,128]{2,1,0:T(1,128)}), s32[64,1,128]{2,1,0:T(1,128)S(1)}, u32[]{:S(2)}, u32[]{:S(2)}) async-start(s32[64,1,128]{2,1,0:T(1,128)} %bitcast.6), calls=%async_computation | async-start | bytes 65536 | tf_op jit(solution)/shard_map/all_to_all | solution.py:361
  38.5 0.0 collective-permute-done.1.came_ref
  38.6 0.0 collective-permute-done.3.a_ref
  38.6 0.0 collective-permute-done.4.b_ref
  38.6 1.3 %collective-permute-done.5.c_ref = s32[136,512]{1,0:T(8,128)S(1)} collective-permute-done((s32[136,512]{1,0:T(8,128)S(1)}, s32[136,512]{1,0:T(8,128)S(1)}, u32[]{:S(2)}, u32[]{:S(2)}) %collective-permute-start.5) | collective-permute-done | bytes 278560 | tf_op jit(solution)/shard_map/ppermute | solution.py:341
  39.9 0.0 copy-done.2
  39.9 0.6 shard_map.72
  40.5 6.4 %all-to-all-done = s32[64,1,128]{2,1,0:T(1,128)S(1)} async-done(((s32[64,1,128]{2,1,0:T(1,128)}), s32[64,1,128]{2,1,0:T(1,128)S(1)}, u32[]{:S(2)}, u32[]{:S(2)}) %all-to-all-start) | async-done | bytes 32800 | tf_op jit(solution)/shard_map/all_to_all | solution.py:361
  46.9 1.8 %shard_map.74 = f32[512,128]{1,0:T(8,128)} custom-call(s32[4]{0:T(128)S(1)} %pad_add_fusion.here_ref, bf16[768,512]{1,0:T(8,128)(2,1)S(1)} %get-tuple-element.35.parts_ref, f32[8,256]{1,0:T(8,128)S(1)} %get-tuple-element.36.before_ref, s32[8,128]{1,0:T(8,128)S(1)} %get-tuple-element.37.found_ref, s32[64,128]{1,0:T(8,128)S(1)} %bitcast.12), custom_call_target="tpu_custom_call" | custom-call | flops 16777216 | bytes 1048576 | tf_op jit(solution)/shard_map/pallas_call | solution.py:25
  48.7 5.9 %all-to-all-start.1 = ((f32[128,4,128]{2,1,0:T(4,128)}), f32[128,4,128]{2,1,0:T(4,128)S(1)}, u32[]{:S(2)}, u32[]{:S(2)}) async-start(f32[128,4,128]{2,1,0:T(4,128)} %bitcast.8), calls=%async_computation.1 | async-start | bytes 524288 | tf_op jit(solution)/shard_map/all_to_all | solution.py:391
  54.6 0.0 copy-done.4
  54.6 0.7 %shard_map.73.selector_ref = f32[32,128]{1,0:T(8,128)S(1)} custom-call(s32[4]{0:T(128)S(1)} %pad_add_fusion.here_ref, s32[2,16]{1,0:T(2,128)S(1)} %bitcast.17, s32[64,128]{1,0:T(8,128)S(1)} %bitcast.13), custom_call_target="tpu_custom_call" | custom-call | flops 1048576 | bytes 1048576 | tf_op jit(solution)/shard_map/pallas_call | solution.py:25
  55.3 0.8 %copy.8 = f32[256,512]{1,0:T(8,128)} copy(f32[256,512]{1,0:T(8,128)S(1)} %get-tuple-element.38) | data formatting | bytes 1048576
  56.1 9.1 %all-to-all-done.1 = f32[128,4,128]{2,1,0:T(4,128)S(1)} async-done(((f32[128,4,128]{2,1,0:T(4,128)}), f32[128,4,128]{2,1,0:T(4,128)S(1)}, u32[]{:S(2)}, u32[]{:S(2)}) %all-to-all-start.1) | async-done | bytes 262176 | tf_op jit(solution)/shard_map/all_to_all | solution.py:391
  65.2 0.0 copy-done.5
  65.2 2.5 %shard_map.75 = f32[16,128]{1,0:T(8,128)} custom-call(s32[16]{0:T(128)S(1)} %copy-done.5, f32[32,128]{1,0:T(8,128)S(1)} %shard_map.73.selector_ref, f32[512,128]{1,0:T(8,128)S(1)} %bitcast.11), custom_call_target="tpu_custom_call" | custom-call | flops 16777216 | bytes 1048576 | tf_op jit(solution)/shard_map/pallas_call | solution.py:25
Async XLA Ops:
  0.6 5.2 %collective-permute-start = (bf16[8,512]{1,0:T(8,128)(2,1)}, bf16[8,512]{1,0:T(8,128)(2,1)S(1)}, u32[]{:S(2)}, u32[]{:S(2)}) collective-permute-start(bf16[8,512]{1,0:T(8,128)(2,1)} %wave_ref.1), channel_id=1, source_target_pairs={{8,0},{16,8},{24,16},{32,24},{40,32},{48,40},{56,48},{64,56},{72,6... | collective-permute-start | bytes 24584 | tf_op jit(solution)/shard_map/ppermute | solution.py:301
  2.0 0.7 %copy-start = (bf16[8,512]{1,0:T(8,128)(2,1)S(1)}, bf16[8,512]{1,0:T(8,128)(2,1)}, u32[]{:S(2)}) copy-start(bf16[8,512]{1,0:T(8,128)(2,1)} %wave_ref.1) | copy-start | bytes 24580
  2.7 0.7 %copy-start.1 = (s32[256,1]{0,1:T(1,128)S(1)}, s32[256,1]{0,1:T(1,128)}, u32[]{:S(2)}) copy-start(s32[256,1]{0,1:T(1,128)} %param.7) | copy-start | bytes 3076
  3.4 0.7 %copy-start.3 = (s32[16,2]{0,1:T(2,128)S(1)}, s32[16,2]{0,1:T(2,128)}, u32[]{:S(2)}) copy-start(s32[16,2]{0,1:T(2,128)} %param.8) | copy-start | bytes 388
  16.5 5.1 %collective-permute-start.2 = (f32[776,512]{1,0:T(8,128)S(1)}, f32[776,512]{1,0:T(8,128)S(1)}, u32[]{:S(2)}, u32[]{:S(2)}) collective-permute-start(f32[776,512]{1,0:T(8,128)S(1)} %get-tuple-element.27), channel_id=1, source_target_pairs={{0,1},{1,0},{2,3},{3,2},{4,5},{5,4},{6,7},{7,6},{8,9},{9,8},{10,11... | collective-permute-start | bytes 4767752 | tf_op jit(solution)/shard_map/ppermute | solution.py:344
  18.6 21.3 %copy-start.2 = (s32[256,1]{0,1:T(1,128)S(1)}, s32[256,1]{0,1:T(1,128)}, u32[]{:S(2)}) copy-start(s32[256,1]{0,1:T(1,128)} %param.7) | copy-start | bytes 3076
  21.2 33.4 %copy-start.4 = (s32[16,2]{0,1:T(2,128)S(1)}, s32[16,2]{0,1:T(2,128)}, u32[]{:S(2)}) copy-start(s32[16,2]{0,1:T(2,128)} %param.8) | copy-start | bytes 388
  21.2 44.0 %copy-start.5 = (s32[16]{0:T(128)S(1)}, s32[16]{0:T(128)}, u32[]{:S(2)}) copy-start(s32[16]{0:T(128)} %lags_ref.1) | copy-start | bytes 196
  21.2 17.3 %collective-permute-start.1 = (f32[256,512]{1,0:T(8,128)S(1)}, f32[256,512]{1,0:T(8,128)S(1)}, u32[]{:S(2)}, u32[]{:S(2)}) collective-permute-start(f32[256,512]{1,0:T(8,128)S(1)} %get-tuple-element.25), channel_id=1, source_target_pairs={{0,1},{1,0},{2,3},{3,2},{4,5},{5,4},{6,7},{7,6},{8,9},{9,8},{10,11... | collective-permute-start | bytes 1572872 | tf_op jit(solution)/shard_map/ppermute | solution.py:344
  22.5 16.1 %collective-permute-start.3 = (s32[136,512]{1,0:T(8,128)S(1)}, s32[136,512]{1,0:T(8,128)S(1)}, u32[]{:S(2)}, u32[]{:S(2)}) collective-permute-start(s32[136,512]{1,0:T(8,128)S(1)} %get-tuple-element.30), channel_id=1, source_target_pairs={{0,2},{2,4},{4,6},{6,0},{1,3},{3,5},{5,7},{7,1},{8,10},{10,12},{12... | collective-permute-start | bytes 835592 | tf_op jit(solution)/shard_map/ppermute | solution.py:341
  24.2 14.3 %collective-permute-start.4 = (s32[136,512]{1,0:T(8,128)S(1)}, s32[136,512]{1,0:T(8,128)S(1)}, u32[]{:S(2)}, u32[]{:S(2)}) collective-permute-start(s32[136,512]{1,0:T(8,128)S(1)} %get-tuple-element.31), channel_id=1, source_target_pairs={{0,6},{2,0},{4,2},{6,4},{1,7},{3,1},{5,3},{7,5},{8,14},{10,8},{12,... | collective-permute-start | bytes 835592 | tf_op jit(solution)/shard_map/ppermute | solution.py:341
  26.3 13.6 %collective-permute-start.5 = (s32[136,512]{1,0:T(8,128)S(1)}, s32[136,512]{1,0:T(8,128)S(1)}, u32[]{:S(2)}, u32[]{:S(2)}) collective-permute-start(s32[136,512]{1,0:T(8,128)S(1)} %get-tuple-element.32), channel_id=1, source_target_pairs={{0,4},{2,6},{4,0},{6,2},{1,5},{3,7},{5,1},{7,3},{8,12},{10,14},{12... | collective-permute-start | bytes 835592 | tf_op jit(solution)/shard_map/ppermute | solution.py:341
  27.6 19.2 %all-to-all-start = ((s32[64,1,128]{2,1,0:T(1,128)}), s32[64,1,128]{2,1,0:T(1,128)S(1)}, u32[]{:S(2)}, u32[]{:S(2)}) async-start(s32[64,1,128]{2,1,0:T(1,128)} %bitcast.6), calls=%async_computation | async-start | bytes 65536 | tf_op jit(solution)/shard_map/all_to_all | solution.py:361
  48.7 16.5 %all-to-all-start.1 = ((f32[128,4,128]{2,1,0:T(4,128)}), f32[128,4,128]{2,1,0:T(4,128)S(1)}, u32[]{:S(2)}, u32[]{:S(2)}) async-start(f32[128,4,128]{2,1,0:T(4,128)} %bitcast.8), calls=%async_computation.1 | async-start | bytes 524288 | tf_op jit(solution)/shard_map/all_to_all | solution.py:391

commit v8 on v7

--- a/solution.py
+++ b/solution.py
@@ -166,16 +166,13 @@
     return codes.astype(f32) * (jnp.exp2(exponent * 0.125) * (1.0 / STEPS)) * level, energy
 
 
-def three(values):
+def halves(values):
     high = values.astype(bf16)
-    rest = values - high.astype(f32)
-    middle = rest.astype(bf16)
-    low = (rest - middle.astype(f32)).astype(bf16)
-    return high, middle, low
+    return high, (values - high.astype(f32)).astype(bf16)
 
 
 def pick(selector, parts):
-    return jnp.dot(jnp.concatenate([selector] * 3, axis=1), parts, preferred_element_type=f32)
+    return jnp.dot(jnp.concatenate([selector] * 2, axis=1), parts, preferred_element_type=f32)
 
 
 def finish(keep_ref, came_ref, energy_ref, a_ref, b_ref, c_ref, flags_ref, stack_ref, parts_ref, before_ref, found_ref):
@@ -189,7 +186,7 @@
         energy = energy + more
     stack = stack * (1.0 / jnp.sqrt(energy + epsilon))
     stack_ref[...] = stack
-    parts_ref[...] = jnp.concatenate(three(stack), axis=0)
+    parts_ref[...] = jnp.concatenate(halves(stack), axis=0)
     flags = jnp.broadcast_to(flags_ref[...], (8, group)).astype(f32)
     earlier = lax.broadcasted_iota(jnp.int32, (group, group), 0) < lax.broadcasted_iota(
         jnp.int32, (group, group), 1
@@ -256,7 +253,7 @@
     across = BLK // LANES
     sources = selector_ref.shape[1]
     received = [received_ref[pl.ds(k, sources, stride=across), :] for k in range(across)]
-    picked = pick(selector_ref[...].astype(bf16), jnp.concatenate(three(jnp.concatenate(received, axis=1)), axis=0))
+    picked = pick(selector_ref[...].astype(bf16), jnp.concatenate(halves(jnp.concatenate(received, axis=1)), axis=0))
     first, second = picked[:pairs], picked[pairs:]
     length = 2 * BLK
     nothing = jnp.zeros((pairs, BLK), f32)
@@ -279,10 +276,9 @@
                 part = part + product[:, k : k + LANES]
             products[pl.ds(p * NLAG + 8 * u, 8), :] = part
     ones = jnp.ones((8, LANES), bf16)
-    high, middle, _ = three(products[...])
     high, middle = [
         lax.dot_general(ones, part, (((1,), (1,)), ((), ())), preferred_element_type=f32)
-        for part in (high, middle)
+        for part in halves(products[...])
     ]
     raw = high + middle
     raw = jnp.concatenate([raw[:1, p * NLAG : (p + 1) * NLAG] for p in range(pairs)], axis=0)
@@ -312,7 +308,7 @@
     )
 
     stations = templates.shape[1]
-    away = (1, 3, 2)
+    away = (2, 1, 3)
     any_space = pl.BlockSpec(memory_space=pl.ANY)
     flops = 4 * group * stations * TLEN * BLK
     shape = pltpu.VMEM((len(away) * group + 8, BLK), f32)
@@ -365,7 +361,7 @@
         finish,
         (
             pltpu.VMEM((group, BLK), f32),
-            pltpu.VMEM((3 * group, BLK), bf16),
+            pltpu.VMEM((2 * group, BLK), bf16),
             pltpu.VMEM((8, group), f32),
             pltpu.VMEM((8, LANES), jnp.int32),
         ),

time: 68 us -> 68.5 us (level)
    all_to_all x1, starting transfers between devices: 10.9 us -> 9.51 us  [shards(): lax.all_to_all(note.reshape(chips, 1, LANES), ('tm', 'z'), 0, 0, tiled=True)]
    ppermute x3, starting transfers between devices: 5.14 us -> 6.35 us  [over(): lax.ppermute(values, 'z', [(i, (i + distance) % planes) for i in range(pl...]
  transfers between devices with their start and end apart: 8 -> 8, of which waited for: 5 -> 6; matrix products, arithmetic and copies ran while one was open for 1% -> 1% of each run, Pallas kernels for 7% -> 8%
where the time goes in v8:
time: 68.5 us; the launch traced here: 68.2 us
  starting transfers between devices  25.7 us (38%)
  Pallas kernels  20.1 us (29%)
  waiting for transfers between devices  18.7 us (27%)
  local copies, waits for them, and re-layouts  2.87 us (4%)
  between operations  0.74 us (1%)
    pallas_call x1, Pallas kernels, shards(): pl.pallas_call(functools.partial(correlate, away), out_shape=(shape, shap...  10.7 us
    all_to_all x1, starting transfers between devices, shards(): lax.all_to_all(note.reshape(chips, 1, LANES), ('tm', 'z'), 0, 0, tiled=True)  9.51 us
    pallas_call x7, Pallas kernels, whole(): pl.pallas_call(kernel, out_shape=outs, in_specs=[SMEM] * smem + [VMEM] *...  9.38 us
    all_to_all x1, waiting for transfers between devices, shards(): received = lax.all_to_all(windows, ('core', 'tm', 'z'), 0, 0, tiled=True)  9.1 us
    all_to_all x1, waiting for transfers between devices, shards(): lax.all_to_all(note.reshape(chips, 1, LANES), ('tm', 'z'), 0, 0, tiled=True)  6.7 us
    ppermute x3, starting transfers between devices, over(): lax.ppermute(values, 'z', [(i, (i + distance) % planes) for i in range(pl...  6.35 us
    all_to_all x1, starting transfers between devices, shards(): received = lax.all_to_all(windows, ('core', 'tm', 'z'), 0, 0, tiled=True)  6.21 us
    unnamed x13, local copies, waits for them, and re-layouts  2.87 us
  transfers between devices with their start and end apart: 8, of which 6 were waited for; matrix products, arithmetic and copies ran while one was open for 1% of the time, Pallas kernels for 8%

profile of v8, /device:TPU:1, one launch (start us, length us, event | category | flops | bytes accessed | tf_op | source)
XLA Modules:
  0.0 68.2 jit_solution(14699875218645210377)
XLA Ops:
  0.6 1.3 %collective-permute-start = (bf16[8,512]{1,0:T(8,128)(2,1)}, bf16[8,512]{1,0:T(8,128)(2,1)S(1)}, u32[]{:S(2)}, u32[]{:S(2)}) collective-permute-start(bf16[8,512]{1,0:T(8,128)(2,1)} %wave_ref.1), channel_id=1, source_target_pairs={{8,0},{16,8},{24,16},{32,24},{40,32},{48,40},{56,48},{64,56},{72,6... | collective-permute-start | bytes 24584 | tf_op jit(solution)/shard_map/ppermute | solution.py:297
  1.9 0.1 pad_add_fusion.here_ref
  2.0 0.0 copy-start
  2.0 0.7 %copy-done = bf16[8,512]{1,0:T(8,128)(2,1)S(1)} copy-done((bf16[8,512]{1,0:T(8,128)(2,1)S(1)}, bf16[8,512]{1,0:T(8,128)(2,1)}, u32[]{:S(2)}) %copy-start) | copy-done | bytes 8216
  2.7 0.0 copy-start.1
  2.7 0.7 copy-done.1
  3.4 0.0 copy-start.3
  3.4 0.7 copy-done.3
  4.1 0.1 shard_map.68
  4.1 1.7 %collective-permute-done.next_ref = bf16[8,512]{1,0:T(8,128)(2,1)S(1)} collective-permute-done((bf16[8,512]{1,0:T(8,128)(2,1)}, bf16[8,512]{1,0:T(8,128)(2,1)S(1)}, u32[]{:S(2)}, u32[]{:S(2)}) %collective-permute-start) | collective-permute-done | bytes 8224 | tf_op jit(solution)/shard_map/ppermute | solution.py:297
  5.8 10.7 %shard_map.69 = (f32[776,512]{1,0:T(8,128)S(1)}, f32[776,512]{1,0:T(8,128)S(1)}, bf16[4096,512]{1,0:T(8,128)(2,1)S(1)}, bf16[2,256,8,512]{3,2,1,0:T(8,128)(2,1)S(1)}) custom-call(s32[4]{0:T(128)S(1)} %pad_add_fusion.here_ref, bf16[8,512]{1,0:T(8,128)(2,1)S(1)} %get-tuple-element.20.wave_ref, bf16[8,512]{1,0:T(8,128)(2,1)S(1)} %collective-permute-done.next_ref, ...), custom_call_target="tpu_custom_call" | custom-call | flops 6442450944 | bytes 12582912 | tf_op jit(solution)/shard_map/pallas_call | solution.py:315
  16.5 2.1 %collective-permute-start.2 = (f32[776,512]{1,0:T(8,128)S(1)}, f32[776,512]{1,0:T(8,128)S(1)}, u32[]{:S(2)}, u32[]{:S(2)}) collective-permute-start(f32[776,512]{1,0:T(8,128)S(1)} %get-tuple-element.27), channel_id=1, source_target_pairs={{0,1},{1,0},{2,3},{3,2},{4,5},{5,4},{6,7},{7,6},{8,9},{9,8},{10,11... | collective-permute-start | bytes 4767752 | tf_op jit(solution)/shard_map/ppermute | solution.py:340
  18.6 0.0 copy-start.2
  18.6 2.6 %shard_map.70 = (f32[256,512]{1,0:T(8,128)S(1)}, f32[256,512]{1,0:T(8,128)S(1)}) custom-call(bf16[2,256,8,512]{3,2,1,0:T(8,128)(2,1)S(1)} %get-tuple-element.22.own_ref, bf16[4096,512]{1,0:T(8,128)(2,1)S(1)} %get-tuple-element.23.sliding_ref), custom_call_target="tpu_custom_call" | custom-call | flops 2147483648 | bytes 1048576 | tf_op jit(solution)/shard_map/pallas_call | solution.py:25
  21.2 0.0 copy-start.4
  21.2 0.0 copy-start.5
  21.2 0.3 collective-permute-start.1
  21.5 0.1 collective-permute-done.2.came_ref
  21.7 1.3 %shard_map.71 = (f32[8,512]{1,0:T(8,128)S(1)}, s32[64,128]{1,0:T(8,128)}, s32[136,512]{1,0:T(8,128)}, s32[136,512]{1,0:T(8,128)S(1)}, s32[136,512]{1,0:T(8,128)S(1)}) custom-call(f32[776,512]{1,0:T(8,128)S(1)} %get-tuple-element.26.keep_ref, f32[776,512]{1,0:T(8,128)S(1)} %collective-permute-done.2.came_ref), custom_call_target="tpu_custom_call" | custom-call | flops 4194304 | bytes 1048576 | tf_op jit(solution)/shard_map/pallas_call | solution.py:25
  22.9 3.7 %collective-permute-start.3 = (s32[136,512]{1,0:T(8,128)}, s32[136,512]{1,0:T(8,128)S(1)}, u32[]{:S(2)}, u32[]{:S(2)}) collective-permute-start(s32[136,512]{1,0:T(8,128)} %get-tuple-element.30), channel_id=1, source_target_pairs={{0,4},{2,6},{4,0},{6,2},{1,5},{3,7},{5,1},{7,3},{8,12},{10,14},{12... | collective-permute-start | bytes 835592 | tf_op jit(solution)/shard_map/ppermute | solution.py:337
  26.6 0.7 %collective-permute-start.4 = (s32[136,512]{1,0:T(8,128)S(1)}, s32[136,512]{1,0:T(8,128)S(1)}, u32[]{:S(2)}, u32[]{:S(2)}) collective-permute-start(s32[136,512]{1,0:T(8,128)S(1)} %get-tuple-element.31), channel_id=1, source_target_pairs={{0,2},{2,4},{4,6},{6,0},{1,3},{3,5},{5,7},{7,1},{8,10},{10,12},{12... | collective-permute-start | bytes 835592 | tf_op jit(solution)/shard_map/ppermute | solution.py:337
  27.3 1.9 %collective-permute-start.5 = (s32[136,512]{1,0:T(8,128)S(1)}, s32[136,512]{1,0:T(8,128)S(1)}, u32[]{:S(2)}, u32[]{:S(2)}) collective-permute-start(s32[136,512]{1,0:T(8,128)S(1)} %get-tuple-element.32), channel_id=1, source_target_pairs={{0,6},{2,0},{4,2},{6,4},{1,7},{3,1},{5,3},{7,5},{8,14},{10,8},{12,... | collective-permute-start | bytes 835592 | tf_op jit(solution)/shard_map/ppermute | solution.py:337
  29.3 9.5 %all-to-all-start = ((s32[64,1,128]{2,1,0:T(1,128)}), s32[64,1,128]{2,1,0:T(1,128)S(1)}, u32[]{:S(2)}, u32[]{:S(2)}) async-start(s32[64,1,128]{2,1,0:T(1,128)} %bitcast.6), calls=%async_computation | async-start | bytes 65536 | tf_op jit(solution)/shard_map/all_to_all | solution.py:357
  38.8 0.0 collective-permute-done.1.came_ref
  38.8 0.0 collective-permute-done.3.a_ref
  38.8 1.1 %collective-permute-done.4.b_ref = s32[136,512]{1,0:T(8,128)S(1)} collective-permute-done((s32[136,512]{1,0:T(8,128)S(1)}, s32[136,512]{1,0:T(8,128)S(1)}, u32[]{:S(2)}, u32[]{:S(2)}) %collective-permute-start.4) | collective-permute-done | bytes 278560 | tf_op jit(solution)/shard_map/ppermute | solution.py:337
  39.9 0.1 collective-permute-done.5.c_ref
  40.0 0.0 copy-done.2
  40.0 0.5 shard_map.72
  40.5 6.7 %all-to-all-done = s32[64,1,128]{2,1,0:T(1,128)S(1)} async-done(((s32[64,1,128]{2,1,0:T(1,128)}), s32[64,1,128]{2,1,0:T(1,128)S(1)}, u32[]{:S(2)}, u32[]{:S(2)}) %all-to-all-start) | async-done | bytes 32800 | tf_op jit(solution)/shard_map/all_to_all | solution.py:357
  47.2 1.8 %shard_map.74 = f32[512,128]{1,0:T(8,128)} custom-call(s32[4]{0:T(128)S(1)} %pad_add_fusion.here_ref, bf16[512,512]{1,0:T(8,128)(2,1)S(1)} %get-tuple-element.35.parts_ref, f32[8,256]{1,0:T(8,128)S(1)} %get-tuple-element.36.before_ref, s32[8,128]{1,0:T(8,128)S(1)} %get-tuple-element.37.found_ref, s32[64,128]{1,0:T(8,128)S(1)} %bitcast.12), custom_call_target="tpu_custom_call" | custom-call | flops 16777216 | bytes 1048576 | tf_op jit(solution)/shard_map/pallas_call | solution.py:25
  48.9 6.2 %all-to-all-start.1 = ((f32[128,4,128]{2,1,0:T(4,128)}), f32[128,4,128]{2,1,0:T(4,128)S(1)}, u32[]{:S(2)}, u32[]{:S(2)}) async-start(f32[128,4,128]{2,1,0:T(4,128)} %bitcast.8), calls=%async_computation.1 | async-start | bytes 524288 | tf_op jit(solution)/shard_map/all_to_all | solution.py:387
  55.2 0.0 copy-done.4
  55.2 0.7 %shard_map.73.selector_ref = f32[32,128]{1,0:T(8,128)S(1)} custom-call(s32[4]{0:T(128)S(1)} %pad_add_fusion.here_ref, s32[2,16]{1,0:T(2,128)S(1)} %bitcast.17, s32[64,128]{1,0:T(8,128)S(1)} %bitcast.13), custom_call_target="tpu_custom_call" | custom-call | flops 1048576 | bytes 1048576 | tf_op jit(solution)/shard_map/pallas_call | solution.py:25
  55.9 0.8 %copy.8 = f32[256,512]{1,0:T(8,128)} copy(f32[256,512]{1,0:T(8,128)S(1)} %get-tuple-element.38) | data formatting | bytes 1048576
  56.7 9.1 %all-to-all-done.1 = f32[128,4,128]{2,1,0:T(4,128)S(1)} async-done(((f32[128,4,128]{2,1,0:T(4,128)}), f32[128,4,128]{2,1,0:T(4,128)S(1)}, u32[]{:S(2)}, u32[]{:S(2)}) %all-to-all-start.1) | async-done | bytes 262176 | tf_op jit(solution)/shard_map/all_to_all | solution.py:387
  65.8 0.0 copy-done.5
  65.8 2.4 %shard_map.75 = f32[16,128]{1,0:T(8,128)} custom-call(s32[16]{0:T(128)S(1)} %copy-done.5, f32[32,128]{1,0:T(8,128)S(1)} %shard_map.73.selector_ref, f32[512,128]{1,0:T(8,128)S(1)} %bitcast.11), custom_call_target="tpu_custom_call" | custom-call | flops 16777216 | bytes 1048576 | tf_op jit(solution)/shard_map/pallas_call | solution.py:25
Async XLA Ops:
  0.6 5.2 %collective-permute-start = (bf16[8,512]{1,0:T(8,128)(2,1)}, bf16[8,512]{1,0:T(8,128)(2,1)S(1)}, u32[]{:S(2)}, u32[]{:S(2)}) collective-permute-start(bf16[8,512]{1,0:T(8,128)(2,1)} %wave_ref.1), channel_id=1, source_target_pairs={{8,0},{16,8},{24,16},{32,24},{40,32},{48,40},{56,48},{64,56},{72,6... | collective-permute-start | bytes 24584 | tf_op jit(solution)/shard_map/ppermute | solution.py:297
  2.0 0.7 %copy-start = (bf16[8,512]{1,0:T(8,128)(2,1)S(1)}, bf16[8,512]{1,0:T(8,128)(2,1)}, u32[]{:S(2)}) copy-start(bf16[8,512]{1,0:T(8,128)(2,1)} %wave_ref.1) | copy-start | bytes 24580
  2.7 0.7 copy-start.1
  3.4 0.7 copy-start.3
  16.5 5.1 %collective-permute-start.2 = (f32[776,512]{1,0:T(8,128)S(1)}, f32[776,512]{1,0:T(8,128)S(1)}, u32[]{:S(2)}, u32[]{:S(2)}) collective-permute-start(f32[776,512]{1,0:T(8,128)S(1)} %get-tuple-element.27), channel_id=1, source_target_pairs={{0,1},{1,0},{2,3},{3,2},{4,5},{5,4},{6,7},{7,6},{8,9},{9,8},{10,11... | collective-permute-start | bytes 4767752 | tf_op jit(solution)/shard_map/ppermute | solution.py:340
  18.6 21.4 %copy-start.2 = (s32[256,1]{0,1:T(1,128)S(1)}, s32[256,1]{0,1:T(1,128)}, u32[]{:S(2)}) copy-start(s32[256,1]{0,1:T(1,128)} %param.7) | copy-start | bytes 3076
  21.2 33.9 %copy-start.4 = (s32[16,2]{0,1:T(2,128)S(1)}, s32[16,2]{0,1:T(2,128)}, u32[]{:S(2)}) copy-start(s32[16,2]{0,1:T(2,128)} %param.8) | copy-start | bytes 388
  21.2 44.6 %copy-start.5 = (s32[16]{0:T(128)S(1)}, s32[16]{0:T(128)}, u32[]{:S(2)}) copy-start(s32[16]{0:T(128)} %lags_ref.1) | copy-start | bytes 196
  21.2 17.5 %collective-permute-start.1 = (f32[256,512]{1,0:T(8,128)S(1)}, f32[256,512]{1,0:T(8,128)S(1)}, u32[]{:S(2)}, u32[]{:S(2)}) collective-permute-start(f32[256,512]{1,0:T(8,128)S(1)} %get-tuple-element.25), channel_id=1, source_target_pairs={{0,1},{1,0},{2,3},{3,2},{4,5},{5,4},{6,7},{7,6},{8,9},{9,8},{10,11... | collective-permute-start | bytes 1572872 | tf_op jit(solution)/shard_map/ppermute | solution.py:340
  22.9 15.9 %collective-permute-start.3 = (s32[136,512]{1,0:T(8,128)}, s32[136,512]{1,0:T(8,128)S(1)}, u32[]{:S(2)}, u32[]{:S(2)}) collective-permute-start(s32[136,512]{1,0:T(8,128)} %get-tuple-element.30), channel_id=1, source_target_pairs={{0,4},{2,6},{4,0},{6,2},{1,5},{3,7},{5,1},{7,3},{8,12},{10,14},{12... | collective-permute-start | bytes 835592 | tf_op jit(solution)/shard_map/ppermute | solution.py:337
  26.6 13.3 %collective-permute-start.4 = (s32[136,512]{1,0:T(8,128)S(1)}, s32[136,512]{1,0:T(8,128)S(1)}, u32[]{:S(2)}, u32[]{:S(2)}) collective-permute-start(s32[136,512]{1,0:T(8,128)S(1)} %get-tuple-element.31), channel_id=1, source_target_pairs={{0,2},{2,4},{4,6},{6,0},{1,3},{3,5},{5,7},{7,1},{8,10},{10,12},{12... | collective-permute-start | bytes 835592 | tf_op jit(solution)/shard_map/ppermute | solution.py:337
  27.3 12.6 %collective-permute-start.5 = (s32[136,512]{1,0:T(8,128)S(1)}, s32[136,512]{1,0:T(8,128)S(1)}, u32[]{:S(2)}, u32[]{:S(2)}) collective-permute-start(s32[136,512]{1,0:T(8,128)S(1)} %get-tuple-element.32), channel_id=1, source_target_pairs={{0,6},{2,0},{4,2},{6,4},{1,7},{3,1},{5,3},{7,5},{8,14},{10,8},{12,... | collective-permute-start | bytes 835592 | tf_op jit(solution)/shard_map/ppermute | solution.py:337
  29.3 17.9 %all-to-all-start = ((s32[64,1,128]{2,1,0:T(1,128)}), s32[64,1,128]{2,1,0:T(1,128)S(1)}, u32[]{:S(2)}, u32[]{:S(2)}) async-start(s32[64,1,128]{2,1,0:T(1,128)} %bitcast.6), calls=%async_computation | async-start | bytes 65536 | tf_op jit(solution)/shard_map/all_to_all | solution.py:357
  48.9 16.8 %all-to-all-start.1 = ((f32[128,4,128]{2,1,0:T(4,128)}), f32[128,4,128]{2,1,0:T(4,128)S(1)}, u32[]{:S(2)}, u32[]{:S(2)}) async-start(f32[128,4,128]{2,1,0:T(4,128)} %bitcast.8), calls=%async_computation.1 | async-start | bytes 524288 | tf_op jit(solution)/shard_map/all_to_all | solution.py:387
